TPU v7x, 128 devices: a whole 4x4x4 slice. The times are simulated.
128 devices in a mesh: layer: 8 (over z, core), grid: 16 (over x, y).
Axes of the slice: x: 4, y: 4, z: 4, core: 2. Of those that a mesh axis runs over, the one named last changes fastest.
Arguments:
- leaf_rhs: float32 [1024, 256, 256], P(('layer', 'grid')), may hold values from -6 to 6
- leaf_linv: float32 [1024, 256, 256], P(('layer', 'grid')), as said below
- leaf_uinv: float32 [1024, 256, 256], P(('layer', 'grid')), as said below
- low_couple: float32 [1024, 2, 256, 256], P(('layer', 'grid')), may hold values from -0.09375 to 0.09375
- up_couple: float32 [1024, 2, 256, 256], P(('layer', 'grid')), may hold values from -0.25 to 0.25
- targets: int32 [1024, 2], P(('layer', 'grid')), may hold values from 0 to 31, all different within a row
- top_rhs: float32 [32, 256, 256], P('grid'), may hold values from -6 to 6
- top_linv: float32 [32, 256, 256], P('grid'), as said below
- top_uinv: float32 [32, 256, 256], P('grid'), as said below
- top_lower: float32 [32, 256, 256], P('grid'), may hold values from -0.375 to 0.375
- top_upper: float32 [32, 256, 256], P('grid'), may hold values from -0.375 to 0.375
Outputs:
- leaf_sol: float32 [1024, 256, 256], P(('layer', 'grid'))
- top_sol: float32 [32, 256, 256], P('grid')
Inputs may be any that keep to these rules, and one draw needn't show every extreme that they name: The 2 targets of one subtree supernode are distinct, and every ancestor is named by some coupling block. `leaf_linv`: unit lower triangular tiles. `leaf_uinv`: upper triangular tiles with positive diagonal. `top_linv`: unit lower triangular tiles. `top_uinv`: upper triangular tiles with positive diagonal.
All inputs are finite; a program needn't handle non-finite values.
Results may differ from a plain program's by a relative error of at most 0.00028.
Values sent between devices are 32-bit elements; how exact they have to be, the bound alone decides.
No kernel may reach another device: no remote copies, remote signals or barrier semaphores. Data moves between devices by JAX's collectives and lax.ppermute only.
A program may use at most 128 MiB of HBM per device.

v0:
```python
import jax
import jax.numpy as jnp
from jax import lax
from jax.sharding import PartitionSpec as P

highest = lax.Precision.HIGHEST


def passed_along(value, axis, steps):
    count = lax.axis_size(axis)
    initial, last = (max(0, -steps), min(count, count - steps))
    return lax.ppermute(value, axis, [(source, source + steps) for source in range(initial, last)])


def compose(matrices, vectors, order):
    whole_matrix = matrices[order[0]]
    whole_vector = vectors[order[0]]
    for index in order[1:]:
        whole_matrix = jnp.dot(matrices[index], whole_matrix, precision=highest)
        whole_vector = jnp.dot(matrices[index], whole_vector, precision=highest) + vectors[index]
    return (whole_matrix, whole_vector)


def sweep(matrices, vectors, order, incoming):
    results = [None] * len(order)
    previous = incoming
    for index in order:
        previous = jnp.dot(matrices[index], previous, precision=highest) + vectors[index]
        results[index] = previous
    return jnp.stack(results)


def relay_down(matrix, vector):

    def one_turn(counter, carried):
        result = jnp.dot(matrix, carried, precision=highest) + vector
        return passed_along(result, "grid", 1)

    return lax.fori_loop(0, lax.axis_size("grid") - 1, one_turn, jnp.zeros_like(vector))


def relay_up(matrix, vector):

    def one_turn(counter, carried):
        result = jnp.dot(matrix, carried, precision=highest) + vector
        return passed_along(result, "grid", -1)

    return lax.fori_loop(0, lax.axis_size("grid") - 1, one_turn, jnp.zeros_like(vector))


def local(
    leaf_rhs,
    leaf_linv,
    leaf_uinv,
    low_couple,
    up_couple,
    targets,
    top_rhs,
    top_linv,
    top_uinv,
    top_lower,
    top_upper,
):
    top_dev = top_rhs.shape[0]
    blocks = top_dev * lax.axis_size("grid")
    leaf_fwd = jnp.einsum("lij,ljr->lir", leaf_linv, leaf_rhs, precision=highest)
    coupled = jnp.einsum("lcij,ljr->lcir", low_couple, leaf_fwd, precision=highest)
    owners = (targets[:, :, None] == jnp.arange(blocks, dtype=jnp.int32)[None, None, :]).astype(
        jnp.float32
    )
    partial_value = jnp.einsum("lct,lcir->tir", owners, coupled, precision=highest)
    summed = lax.psum(partial_value, ("layer", "grid"))
    owned = lax.dynamic_slice_in_dim(summed, lax.axis_index("grid") * top_dev, top_dev, 0)
    reduced = top_rhs - owned
    forward_mats = -jnp.einsum("tij,tjk->tik", top_linv, top_lower, precision=highest)
    forward_vecs = jnp.einsum("tij,tjr->tir", top_linv, reduced, precision=highest)
    ascending = list(range(top_dev))
    whole_matrix, whole_vector = compose(forward_mats, forward_vecs, ascending)
    incoming = relay_down(whole_matrix, whole_vector)
    top_fwd = sweep(forward_mats, forward_vecs, ascending, incoming)
    backward_mats = -jnp.einsum("tij,tjk->tik", top_uinv, top_upper, precision=highest)
    backward_vecs = jnp.einsum("tij,tjr->tir", top_uinv, top_fwd, precision=highest)
    descending = ascending[::-1]
    back_matrix, back_vector = compose(backward_mats, backward_vecs, descending)
    arriving = relay_up(back_matrix, back_vector)
    top_sol = sweep(backward_mats, backward_vecs, descending, arriving)
    whole_sol = lax.all_gather(top_sol, "grid", axis=0, tiled=True)
    picked = whole_sol[targets]
    correction = jnp.einsum("lcij,lcjr->lir", up_couple, picked, precision=highest)
    leaf_sol = jnp.einsum("lij,ljr->lir", leaf_uinv, leaf_fwd - correction, precision=highest)
    return (leaf_sol, top_sol)


def solution(mesh):
    return jax.shard_map(
        local,
        mesh=mesh,
        in_specs=(
            P(("layer", "grid"), None, None),
            P(("layer", "grid"), None, None),
            P(("layer", "grid"), None, None),
            P(("layer", "grid"), None, None, None),
            P(("layer", "grid"), None, None, None),
            P(("layer", "grid"), None),
            P("grid", None, None),
            P("grid", None, None),
            P("grid", None, None),
            P("grid", None, None),
            P("grid", None, None),
        ),
        out_specs=(P(("layer", "grid"), None, None), P("grid", None, None)),
        check_vma=False,
    )
```

profile of v0, /device:TPU:1, one launch (start us, length us, event | category | flops | bytes accessed | tf_op | source)
XLA Modules:
  0.0 657.8 jit_solution(10784003293316719440)
XLA Ops:
  13.9 8.3 %convolution_bitcast_fusion.1 = f32[8,2,256,256]{2,3,1,0:T(8,128)} fusion(f32[8,2,256,256]{3,2,1,0:T(8,128)S(1)} %copy-done.4, f32[8,256,256]{2,1,0:T(8,128)S(1)} %fusion.17), kind=kOutput, calls=%fused_computation.4 | convolution fusion | flops 3221225472 | bytes 10485760 | tf_op jit(solution)/shard_map/lcij,ljr->lcir/dot_general | solution.py:67
  33.3 8.1 %copy.58 = f32[32,256,256]{2,1,0:T(8,128)} copy(f32[32,256,256]{2,0,1:T(8,128)S(1)} %convolution_bitcast_fusion) | data formatting | bytes 16777216 | tf_op jit(solution)/shard_map/lct,lcir->tir/dot_general | solution.py:71
  45.8 160.8 %all-reduce.2.cloned.1.call-done = f32[32,256,256]{2,1,0:T(8,128)} async-done(((f32[32,256,256]{2,1,0:T(8,128)}), f32[32,256,256]{2,1,0:T(8,128)}) %all-reduce.2.cloned.1.call-update) | async-done | bytes 8388624 | tf_op jit(solution)/shard_map/psum | solution.py:72
  209.4 140.8 %while.20 = (s32[]{:T(128)}, f32[256,256]{1,0:T(8,128)S(1)}, f32[256,256]{1,0:T(8,128)S(1)}, f32[256,256]{1,0:T(8,128)S(1)}, s32[]{:T(128)}) while((s32[]{:T(128)}, f32[256,256]{1,0:T(8,128)S(1)}, f32[256,256]{1,0:T(8,128)S(1)}, f32[256,256]{1,0:T(8,128)S(1)}, s32[]{:T(128)}) %tuple.47), condition=%wide.region_2.0_spmd, body=%wide.region_1.0_spmd.sunk | while | flops 201392128 | bytes 2097253 | solution.py:39
  287.7 6.7 %collective-permute-start = (f32[256,256]{1,0:T(8,128)S(1)}, f32[256,256]{1,0:T(8,128)S(1)}, u32[]{:S(2)}, u32[]{:S(2)}) collective-permute-start(f32[256,256]{1,0:T(8,128)S(1)} %convolution_add_fusion.10), channel_id=1, source_target_pairs={{0,1},{1,2},{2,3},{3,4},{4,5},{5,6},{6,7},{7,8},{8,9},{9,10},{10,1... | collective-permute-start | bytes 786440 | tf_op jit(solution)/shard_map/while/body/eval_jaxpr/ppermute | solution.py:12
  300.8 6.4 collective-permute-start
  353.5 159.2 %while.21 = (s32[]{:T(128)}, f32[256,256]{1,0:T(8,128)S(1)}, f32[256,256]{1,0:T(8,128)S(1)}, f32[256,256]{1,0:T(8,128)S(1)}, s32[]{:T(128)}) while((s32[]{:T(128)}, f32[256,256]{1,0:T(8,128)S(1)}, f32[256,256]{1,0:T(8,128)S(1)}, f32[256,256]{1,0:T(8,128)S(1)}, s32[]{:T(128)}) %tuple.50), condition=%wide.region_4.0_spmd, body=%wide.region_3.0_spmd.sunk | while | flops 201392128 | bytes 2097253 | solution.py:48
  355.2 8.8 %collective-permute-done.1 = f32[256,256]{1,0:T(8,128)S(1)} collective-permute-done((f32[256,256]{1,0:T(8,128)S(1)}, f32[256,256]{1,0:T(8,128)S(1)}, u32[]{:S(2)}, u32[]{:S(2)}) %collective-permute-start.1) | collective-permute-done | bytes 262176 | tf_op jit(solution)/shard_map/while/body/eval_jaxpr/ppermute | solution.py:12
  365.7 8.7 %collective-permute-done.1 = f32[256,256]{1,0:T(8,128)S(1)} collective-permute-done((f32[256,256]{1,0:T(8,128)S(1)}, f32[256,256]{1,0:T(8,128)S(1)}, u32[]{:S(2)}, u32[]{:S(2)}) %collective-permute-start.1) | collective-permute-done | bytes 262176 | tf_op jit(solution)/shard_map/while/body/eval_jaxpr/ppermute | solution.py:12
  376.1 8.4 %collective-permute-done.1 = f32[256,256]{1,0:T(8,128)S(1)} collective-permute-done((f32[256,256]{1,0:T(8,128)S(1)}, f32[256,256]{1,0:T(8,128)S(1)}, u32[]{:S(2)}, u32[]{:S(2)}) %collective-permute-start.1) | collective-permute-done | bytes 262176 | tf_op jit(solution)/shard_map/while/body/eval_jaxpr/ppermute | solution.py:12
  386.1 8.5 %collective-permute-done.1 = f32[256,256]{1,0:T(8,128)S(1)} collective-permute-done((f32[256,256]{1,0:T(8,128)S(1)}, f32[256,256]{1,0:T(8,128)S(1)}, u32[]{:S(2)}, u32[]{:S(2)}) %collective-permute-start.1) | collective-permute-done | bytes 262176 | tf_op jit(solution)/shard_map/while/body/eval_jaxpr/ppermute | solution.py:12
  396.3 10.8 %collective-permute-done.1 = f32[256,256]{1,0:T(8,128)S(1)} collective-permute-done((f32[256,256]{1,0:T(8,128)S(1)}, f32[256,256]{1,0:T(8,128)S(1)}, u32[]{:S(2)}, u32[]{:S(2)}) %collective-permute-start.1) | collective-permute-done | bytes 262176 | tf_op jit(solution)/shard_map/while/body/eval_jaxpr/ppermute | solution.py:12
  408.9 13.0 %collective-permute-done.1 = f32[256,256]{1,0:T(8,128)S(1)} collective-permute-done((f32[256,256]{1,0:T(8,128)S(1)}, f32[256,256]{1,0:T(8,128)S(1)}, u32[]{:S(2)}, u32[]{:S(2)}) %collective-permute-start.1) | collective-permute-done | bytes 262176 | tf_op jit(solution)/shard_map/while/body/eval_jaxpr/ppermute | solution.py:12
  423.6 9.5 %collective-permute-done.1 = f32[256,256]{1,0:T(8,128)S(1)} collective-permute-done((f32[256,256]{1,0:T(8,128)S(1)}, f32[256,256]{1,0:T(8,128)S(1)}, u32[]{:S(2)}, u32[]{:S(2)}) %collective-permute-start.1) | collective-permute-done | bytes 262176 | tf_op jit(solution)/shard_map/while/body/eval_jaxpr/ppermute | solution.py:12
  434.8 8.0 %collective-permute-done.1 = f32[256,256]{1,0:T(8,128)S(1)} collective-permute-done((f32[256,256]{1,0:T(8,128)S(1)}, f32[256,256]{1,0:T(8,128)S(1)}, u32[]{:S(2)}, u32[]{:S(2)}) %collective-permute-start.1) | collective-permute-done | bytes 262176 | tf_op jit(solution)/shard_map/while/body/eval_jaxpr/ppermute | solution.py:12
  444.5 7.0 %collective-permute-done.1 = f32[256,256]{1,0:T(8,128)S(1)} collective-permute-done((f32[256,256]{1,0:T(8,128)S(1)}, f32[256,256]{1,0:T(8,128)S(1)}, u32[]{:S(2)}, u32[]{:S(2)}) %collective-permute-start.1) | collective-permute-done | bytes 262176 | tf_op jit(solution)/shard_map/while/body/eval_jaxpr/ppermute | solution.py:12
  453.2 7.2 %collective-permute-done.1 = f32[256,256]{1,0:T(8,128)S(1)} collective-permute-done((f32[256,256]{1,0:T(8,128)S(1)}, f32[256,256]{1,0:T(8,128)S(1)}, u32[]{:S(2)}, u32[]{:S(2)}) %collective-permute-start.1) | collective-permute-done | bytes 262176 | tf_op jit(solution)/shard_map/while/body/eval_jaxpr/ppermute | solution.py:12
  462.0 7.9 %collective-permute-done.1 = f32[256,256]{1,0:T(8,128)S(1)} collective-permute-done((f32[256,256]{1,0:T(8,128)S(1)}, f32[256,256]{1,0:T(8,128)S(1)}, u32[]{:S(2)}, u32[]{:S(2)}) %collective-permute-start.1) | collective-permute-done | bytes 262176 | tf_op jit(solution)/shard_map/while/body/eval_jaxpr/ppermute | solution.py:12
  471.6 7.9 %collective-permute-done.1 = f32[256,256]{1,0:T(8,128)S(1)} collective-permute-done((f32[256,256]{1,0:T(8,128)S(1)}, f32[256,256]{1,0:T(8,128)S(1)}, u32[]{:S(2)}, u32[]{:S(2)}) %collective-permute-start.1) | collective-permute-done | bytes 262176 | tf_op jit(solution)/shard_map/while/body/eval_jaxpr/ppermute | solution.py:12
  481.3 8.0 %collective-permute-done.1 = f32[256,256]{1,0:T(8,128)S(1)} collective-permute-done((f32[256,256]{1,0:T(8,128)S(1)}, f32[256,256]{1,0:T(8,128)S(1)}, u32[]{:S(2)}, u32[]{:S(2)}) %collective-permute-start.1) | collective-permute-done | bytes 262176 | tf_op jit(solution)/shard_map/while/body/eval_jaxpr/ppermute | solution.py:12
  490.9 9.4 %collective-permute-done.1 = f32[256,256]{1,0:T(8,128)S(1)} collective-permute-done((f32[256,256]{1,0:T(8,128)S(1)}, f32[256,256]{1,0:T(8,128)S(1)}, u32[]{:S(2)}, u32[]{:S(2)}) %collective-permute-start.1) | collective-permute-done | bytes 262176 | tf_op jit(solution)/shard_map/while/body/eval_jaxpr/ppermute | solution.py:12
  502.0 10.7 %collective-permute-done.1 = f32[256,256]{1,0:T(8,128)S(1)} collective-permute-done((f32[256,256]{1,0:T(8,128)S(1)}, f32[256,256]{1,0:T(8,128)S(1)}, u32[]{:S(2)}, u32[]{:S(2)}) %collective-permute-start.1) | collective-permute-done | bytes 262176 | tf_op jit(solution)/shard_map/while/body/eval_jaxpr/ppermute | solution.py:12
  515.0 111.6 %all-gather.2.cloned.1.call-done = f32[32,256,256]{2,1,0:T(8,128)} async-done(((f32[2,256,256]{2,1,0:T(8,128)}), f32[32,256,256]{2,1,0:T(8,128)}) %all-gather.2.cloned.1.call-update) | async-done | bytes 8388624 | tf_op jit(solution)/shard_map/all_gather | solution.py:87
  632.8 10.4 %fusion.18 = f32[8,256,256,1]{1,2,3,0:T(8,128)S(1)} fusion(f32[8,2,256,256]{3,2,1,0:T(8,128)} %bitcast.102, f32[8,2,256,256]{3,2,1,0:T(8,128)} %param.19), kind=kOutput, calls=%fused_computation.45 | convolution fusion | flops 3221225472 | bytes 10485760 | tf_op jit(solution)/shard_map/lcij,lcjr->lir/dot_general | solution.py:89
  (125 shorter events, 196.9 us)
Async XLA Ops:
  7.2 199.4 %all-reduce.2.cloned.1.call-start = ((), (), s32[]{:S(2)}) async-start(), calls=%async_computation | async-start | bytes 16777216 | tf_op jit(solution)/shard_map/psum | solution.py:72
  41.5 585.1 %all-gather.2.cloned.1.call-start = ((), (), s32[]{:S(2)}) async-start(), calls=%async_computation.1 | async-start | bytes 8912896 | tf_op jit(solution)/shard_map/all_gather | solution.py:87
  223.6 8.5 %collective-permute-start = (f32[256,256]{1,0:T(8,128)S(1)}, f32[256,256]{1,0:T(8,128)S(1)}, u32[]{:S(2)}, u32[]{:S(2)}) collective-permute-start(f32[256,256]{1,0:T(8,128)S(1)} %convolution_add_fusion.10), channel_id=1, source_target_pairs={{0,1},{1,2},{2,3},{3,4},{4,5},{5,6},{6,7},{7,8},{8,9},{9,10},{10,1... | collective-permute-start | bytes 786440 | tf_op jit(solution)/shard_map/while/body/eval_jaxpr/ppermute | solution.py:12
  256.6 9.0 %collective-permute-start = (f32[256,256]{1,0:T(8,128)S(1)}, f32[256,256]{1,0:T(8,128)S(1)}, u32[]{:S(2)}, u32[]{:S(2)}) collective-permute-start(f32[256,256]{1,0:T(8,128)S(1)} %convolution_add_fusion.10), channel_id=1, source_target_pairs={{0,1},{1,2},{2,3},{3,4},{4,5},{5,6},{6,7},{7,8},{8,9},{9,10},{10,1... | collective-permute-start | bytes 786440 | tf_op jit(solution)/shard_map/while/body/eval_jaxpr/ppermute | solution.py:12
  266.0 9.8 %collective-permute-start = (f32[256,256]{1,0:T(8,128)S(1)}, f32[256,256]{1,0:T(8,128)S(1)}, u32[]{:S(2)}, u32[]{:S(2)}) collective-permute-start(f32[256,256]{1,0:T(8,128)S(1)} %convolution_add_fusion.10), channel_id=1, source_target_pairs={{0,1},{1,2},{2,3},{3,4},{4,5},{5,6},{6,7},{7,8},{8,9},{9,10},{10,1... | collective-permute-start | bytes 786440 | tf_op jit(solution)/shard_map/while/body/eval_jaxpr/ppermute | solution.py:12
  276.2 11.1 %collective-permute-start = (f32[256,256]{1,0:T(8,128)S(1)}, f32[256,256]{1,0:T(8,128)S(1)}, u32[]{:S(2)}, u32[]{:S(2)}) collective-permute-start(f32[256,256]{1,0:T(8,128)S(1)} %convolution_add_fusion.10), channel_id=1, source_target_pairs={{0,1},{1,2},{2,3},{3,4},{4,5},{5,6},{6,7},{7,8},{8,9},{9,10},{10,1... | collective-permute-start | bytes 786440 | tf_op jit(solution)/shard_map/while/body/eval_jaxpr/ppermute | solution.py:12
  287.7 12.7 %collective-permute-start = (f32[256,256]{1,0:T(8,128)S(1)}, f32[256,256]{1,0:T(8,128)S(1)}, u32[]{:S(2)}, u32[]{:S(2)}) collective-permute-start(f32[256,256]{1,0:T(8,128)S(1)} %convolution_add_fusion.10), channel_id=1, source_target_pairs={{0,1},{1,2},{2,3},{3,4},{4,5},{5,6},{6,7},{7,8},{8,9},{9,10},{10,1... | collective-permute-start | bytes 786440 | tf_op jit(solution)/shard_map/while/body/eval_jaxpr/ppermute | solution.py:12
  300.8 11.4 %collective-permute-start = (f32[256,256]{1,0:T(8,128)S(1)}, f32[256,256]{1,0:T(8,128)S(1)}, u32[]{:S(2)}, u32[]{:S(2)}) collective-permute-start(f32[256,256]{1,0:T(8,128)S(1)} %convolution_add_fusion.10), channel_id=1, source_target_pairs={{0,1},{1,2},{2,3},{3,4},{4,5},{5,6},{6,7},{7,8},{8,9},{9,10},{10,1... | collective-permute-start | bytes 786440 | tf_op jit(solution)/shard_map/while/body/eval_jaxpr/ppermute | solution.py:12
  312.5 9.5 %collective-permute-start = (f32[256,256]{1,0:T(8,128)S(1)}, f32[256,256]{1,0:T(8,128)S(1)}, u32[]{:S(2)}, u32[]{:S(2)}) collective-permute-start(f32[256,256]{1,0:T(8,128)S(1)} %convolution_add_fusion.10), channel_id=1, source_target_pairs={{0,1},{1,2},{2,3},{3,4},{4,5},{5,6},{6,7},{7,8},{8,9},{9,10},{10,1... | collective-permute-start | bytes 786440 | tf_op jit(solution)/shard_map/while/body/eval_jaxpr/ppermute | solution.py:12
  330.8 9.5 %collective-permute-start = (f32[256,256]{1,0:T(8,128)S(1)}, f32[256,256]{1,0:T(8,128)S(1)}, u32[]{:S(2)}, u32[]{:S(2)}) collective-permute-start(f32[256,256]{1,0:T(8,128)S(1)} %convolution_add_fusion.10), channel_id=1, source_target_pairs={{0,1},{1,2},{2,3},{3,4},{4,5},{5,6},{6,7},{7,8},{8,9},{9,10},{10,1... | collective-permute-start | bytes 786440 | tf_op jit(solution)/shard_map/while/body/eval_jaxpr/ppermute | solution.py:12
  340.7 9.5 %collective-permute-start = (f32[256,256]{1,0:T(8,128)S(1)}, f32[256,256]{1,0:T(8,128)S(1)}, u32[]{:S(2)}, u32[]{:S(2)}) collective-permute-start(f32[256,256]{1,0:T(8,128)S(1)} %convolution_add_fusion.10), channel_id=1, source_target_pairs={{0,1},{1,2},{2,3},{3,4},{4,5},{5,6},{6,7},{7,8},{8,9},{9,10},{10,1... | collective-permute-start | bytes 786440 | tf_op jit(solution)/shard_map/while/body/eval_jaxpr/ppermute | solution.py:12
  353.9 10.1 %collective-permute-start.1 = (f32[256,256]{1,0:T(8,128)S(1)}, f32[256,256]{1,0:T(8,128)S(1)}, u32[]{:S(2)}, u32[]{:S(2)}) collective-permute-start(f32[256,256]{1,0:T(8,128)S(1)} %convolution_add_fusion.11), channel_id=1, source_target_pairs={{1,0},{2,1},{3,2},{4,3},{5,4},{6,5},{7,6},{8,7},{9,8},{10,9},{11,1... | collective-permute-start | bytes 786440 | tf_op jit(solution)/shard_map/while/body/eval_jaxpr/ppermute | solution.py:12
  364.4 10.0 %collective-permute-start.1 = (f32[256,256]{1,0:T(8,128)S(1)}, f32[256,256]{1,0:T(8,128)S(1)}, u32[]{:S(2)}, u32[]{:S(2)}) collective-permute-start(f32[256,256]{1,0:T(8,128)S(1)} %convolution_add_fusion.11), channel_id=1, source_target_pairs={{1,0},{2,1},{3,2},{4,3},{5,4},{6,5},{7,6},{8,7},{9,8},{10,9},{11,1... | collective-permute-start | bytes 786440 | tf_op jit(solution)/shard_map/while/body/eval_jaxpr/ppermute | solution.py:12
  374.8 9.7 %collective-permute-start.1 = (f32[256,256]{1,0:T(8,128)S(1)}, f32[256,256]{1,0:T(8,128)S(1)}, u32[]{:S(2)}, u32[]{:S(2)}) collective-permute-start(f32[256,256]{1,0:T(8,128)S(1)} %convolution_add_fusion.11), channel_id=1, source_target_pairs={{1,0},{2,1},{3,2},{4,3},{5,4},{6,5},{7,6},{8,7},{9,8},{10,9},{11,1... | collective-permute-start | bytes 786440 | tf_op jit(solution)/shard_map/while/body/eval_jaxpr/ppermute | solution.py:12
  384.8 9.8 %collective-permute-start.1 = (f32[256,256]{1,0:T(8,128)S(1)}, f32[256,256]{1,0:T(8,128)S(1)}, u32[]{:S(2)}, u32[]{:S(2)}) collective-permute-start(f32[256,256]{1,0:T(8,128)S(1)} %convolution_add_fusion.11), channel_id=1, source_target_pairs={{1,0},{2,1},{3,2},{4,3},{5,4},{6,5},{7,6},{8,7},{9,8},{10,9},{11,1... | collective-permute-start | bytes 786440 | tf_op jit(solution)/shard_map/while/body/eval_jaxpr/ppermute | solution.py:12
  395.0 12.1 %collective-permute-start.1 = (f32[256,256]{1,0:T(8,128)S(1)}, f32[256,256]{1,0:T(8,128)S(1)}, u32[]{:S(2)}, u32[]{:S(2)}) collective-permute-start(f32[256,256]{1,0:T(8,128)S(1)} %convolution_add_fusion.11), channel_id=1, source_target_pairs={{1,0},{2,1},{3,2},{4,3},{5,4},{6,5},{7,6},{8,7},{9,8},{10,9},{11,1... | collective-permute-start | bytes 786440 | tf_op jit(solution)/shard_map/while/body/eval_jaxpr/ppermute | solution.py:12
  407.5 14.3 %collective-permute-start.1 = (f32[256,256]{1,0:T(8,128)S(1)}, f32[256,256]{1,0:T(8,128)S(1)}, u32[]{:S(2)}, u32[]{:S(2)}) collective-permute-start(f32[256,256]{1,0:T(8,128)S(1)} %convolution_add_fusion.11), channel_id=1, source_target_pairs={{1,0},{2,1},{3,2},{4,3},{5,4},{6,5},{7,6},{8,7},{9,8},{10,9},{11,1... | collective-permute-start | bytes 786440 | tf_op jit(solution)/shard_map/while/body/eval_jaxpr/ppermute | solution.py:12
  422.3 10.8 %collective-permute-start.1 = (f32[256,256]{1,0:T(8,128)S(1)}, f32[256,256]{1,0:T(8,128)S(1)}, u32[]{:S(2)}, u32[]{:S(2)}) collective-permute-start(f32[256,256]{1,0:T(8,128)S(1)} %convolution_add_fusion.11), channel_id=1, source_target_pairs={{1,0},{2,1},{3,2},{4,3},{5,4},{6,5},{7,6},{8,7},{9,8},{10,9},{11,1... | collective-permute-start | bytes 786440 | tf_op jit(solution)/shard_map/while/body/eval_jaxpr/ppermute | solution.py:12
  433.5 9.3 %collective-permute-start.1 = (f32[256,256]{1,0:T(8,128)S(1)}, f32[256,256]{1,0:T(8,128)S(1)}, u32[]{:S(2)}, u32[]{:S(2)}) collective-permute-start(f32[256,256]{1,0:T(8,128)S(1)} %convolution_add_fusion.11), channel_id=1, source_target_pairs={{1,0},{2,1},{3,2},{4,3},{5,4},{6,5},{7,6},{8,7},{9,8},{10,9},{11,1... | collective-permute-start | bytes 786440 | tf_op jit(solution)/shard_map/while/body/eval_jaxpr/ppermute | solution.py:12
  460.7 9.2 %collective-permute-start.1 = (f32[256,256]{1,0:T(8,128)S(1)}, f32[256,256]{1,0:T(8,128)S(1)}, u32[]{:S(2)}, u32[]{:S(2)}) collective-permute-start(f32[256,256]{1,0:T(8,128)S(1)} %convolution_add_fusion.11), channel_id=1, source_target_pairs={{1,0},{2,1},{3,2},{4,3},{5,4},{6,5},{7,6},{8,7},{9,8},{10,9},{11,1... | collective-permute-start | bytes 786440 | tf_op jit(solution)/shard_map/while/body/eval_jaxpr/ppermute | solution.py:12
  470.3 9.2 %collective-permute-start.1 = (f32[256,256]{1,0:T(8,128)S(1)}, f32[256,256]{1,0:T(8,128)S(1)}, u32[]{:S(2)}, u32[]{:S(2)}) collective-permute-start(f32[256,256]{1,0:T(8,128)S(1)} %convolution_add_fusion.11), channel_id=1, source_target_pairs={{1,0},{2,1},{3,2},{4,3},{5,4},{6,5},{7,6},{8,7},{9,8},{10,9},{11,1... | collective-permute-start | bytes 786440 | tf_op jit(solution)/shard_map/while/body/eval_jaxpr/ppermute | solution.py:12
  480.0 9.3 %collective-permute-start.1 = (f32[256,256]{1,0:T(8,128)S(1)}, f32[256,256]{1,0:T(8,128)S(1)}, u32[]{:S(2)}, u32[]{:S(2)}) collective-permute-start(f32[256,256]{1,0:T(8,128)S(1)} %convolution_add_fusion.11), channel_id=1, source_target_pairs={{1,0},{2,1},{3,2},{4,3},{5,4},{6,5},{7,6},{8,7},{9,8},{10,9},{11,1... | collective-permute-start | bytes 786440 | tf_op jit(solution)/shard_map/while/body/eval_jaxpr/ppermute | solution.py:12
  489.6 10.7 %collective-permute-start.1 = (f32[256,256]{1,0:T(8,128)S(1)}, f32[256,256]{1,0:T(8,128)S(1)}, u32[]{:S(2)}, u32[]{:S(2)}) collective-permute-start(f32[256,256]{1,0:T(8,128)S(1)} %convolution_add_fusion.11), channel_id=1, source_target_pairs={{1,0},{2,1},{3,2},{4,3},{5,4},{6,5},{7,6},{8,7},{9,8},{10,9},{11,1... | collective-permute-start | bytes 786440 | tf_op jit(solution)/shard_map/while/body/eval_jaxpr/ppermute | solution.py:12
  500.7 12.0 %collective-permute-start.1 = (f32[256,256]{1,0:T(8,128)S(1)}, f32[256,256]{1,0:T(8,128)S(1)}, u32[]{:S(2)}, u32[]{:S(2)}) collective-permute-start(f32[256,256]{1,0:T(8,128)S(1)} %convolution_add_fusion.11), channel_id=1, source_target_pairs={{1,0},{2,1},{3,2},{4,3},{5,4},{6,5},{7,6},{8,7},{9,8},{10,9},{11,1... | collective-permute-start | bytes 786440 | tf_op jit(solution)/shard_map/while/body/eval_jaxpr/ppermute | solution.py:12
  (18 other events, 107.6 us)
Sparse Core Ops, SparseCore 0:
  41.6 164.9 all-reduce.1
  514.9 111.6 all-gather.1
where the time goes:
time: 659 us; the launch traced here: 658 us
  waiting for transfers between devices  463 us (70%)
  starting transfers between devices  97.9 us (15%)
  matrix products  54.1 us (8%)
  local copies, waits for them, and re-layouts  28 us (4%)
  between operations  14.3 us (2%)
    ppermute x30, waiting for transfers between devices, passed_along(): lax.ppermute(value, axis, [(source, source + steps) for source in range(i...  190 us
    psum x1, waiting for transfers between devices, local(): summed = lax.psum(partial_value, ('layer', 'grid'))  161 us
    all_gather x1, waiting for transfers between devices, local(): whole_sol = lax.all_gather(top_sol, 'grid', axis=0, tiled=True)  112 us
    ppermute x30, starting transfers between devices, passed_along(): lax.ppermute(value, axis, [(source, source + steps) for source in range(i...  97.6 us
  transfers between devices with their start and end apart: 32, of which 32 were waited for; matrix products, arithmetic and copies ran while one was open for 0% of the time, Pallas kernels for 0%

commit v1 on v0

v1 whole, which is shorter than its diff:
```python
import functools

import jax
import jax.numpy as jnp
from jax import lax
from jax.experimental import pallas as pl
from jax.experimental.pallas import tpu as pltpu
from jax.sharding import PartitionSpec as P

LAYERS = 8
GRID = 16
TILE = 256
COLS = TILE // LAYERS
TOPS = 32
VMEM_LIMIT = 56 * 1024 * 1024

NN = (((1,), (0,)), ((), ()))
NT = (((1,), (1,)), ((), ()))

whole = pl.BlockSpec(memory_space=pltpu.VMEM)
in_hbm = pl.BlockSpec(memory_space=pl.ANY)


def split(value):
    high = value.astype(jnp.bfloat16)
    low = (value - high.astype(jnp.float32)).astype(jnp.bfloat16)
    return high, low


def product(left, right, dims):
    def one(a, b):
        return lax.dot_general(a, b, dims, preferred_element_type=jnp.float32)

    return one(left[0], right[0]) + (one(left[0], right[1]) + one(left[1], right[0]))


def params(**more):
    return pltpu.CompilerParams(vmem_limit_bytes=VMEM_LIMIT, **more)


def prepare_kernel(linv, lower, uinv, upper, rhs, fmat, bmat, fall, ball, rhs_t):
    def maps(inverse, coupling, out):
        made = []
        for i in range(2):
            made.append(-product(split(inverse[i]), split(coupling[i]), NN))
            out[i] = made[i]
        return [split(m) for m in made]

    first, second = maps(linv, lower, fmat)
    fall[...] = product(second, first, NN)
    first, second = maps(uinv, upper, bmat)
    ball[...] = product(first, second, NN)
    for i in range(2):
        rhs_t[i] = rhs[i].T


def leaf_forward_kernel(targets, place, linv, rhs, low, fwd, *rest):
    outs, (acc, sems) = rest[:8], rest[8:]
    k = pl.program_id(0)
    core, z = place[0], place[1]

    @pl.when(k == 0)
    def _():
        def clear(i, carry):
            acc[i] = jnp.zeros(acc.shape[1:], jnp.float32)
            return carry

        lax.fori_loop(0, acc.shape[0], clear, 0)

    value = product(split(linv[0]), split(rhs[0]), NN)
    fwd[0] = value
    turned = split(value.T)
    for c in range(2):
        t = targets[2 * k + c]
        coupled = product(turned, split(low[0, c]), NT)
        for layer in range(LAYERS):
            side = lax.rem(layer % 2 + core, 2)
            away = lax.rem(layer // 2 - z + 4, 4)
            acc[(side * 4 + away) * TOPS + t] += coupled[layer * COLS : (layer + 1) * COLS]

    @pl.when(k == pl.num_programs(0) - 1)
    def _():
        copies = [
            pltpu.make_async_copy(acc.at[pl.ds(i * TOPS, TOPS)], outs[i], sems.at[i])
            for i in range(8)
        ]
        for copy in copies:
            copy.start()
        for copy in copies:
            copy.wait()


def leaf_forward(targets, place, linv, rhs, low):
    leaves = linv.shape[0]
    tile = pl.BlockSpec((1, TILE, TILE), lambda k, *_: (k, 0, 0))
    pair = pl.BlockSpec((1, 2, TILE, TILE), lambda k, *_: (k, 0, 0, 0))
    part = jax.ShapeDtypeStruct((TOPS, COLS, TILE), jnp.float32)
    return pl.pallas_call(
        leaf_forward_kernel,
        out_shape=[jax.ShapeDtypeStruct(linv.shape, jnp.float32)] + [part] * 8,
        grid_spec=pltpu.PrefetchScalarGridSpec(
            num_scalar_prefetch=2,
            grid=(leaves,),
            in_specs=[tile, tile, pair],
            out_specs=[tile] + [in_hbm] * 8,
            scratch_shapes=[
                pltpu.VMEM((8 * TOPS, COLS, TILE), jnp.float32),
                pltpu.SemaphoreType.DMA((8,)),
            ],
        ),
        compiler_params=params(),
        name="leaf_forward",
    )(targets, place, linv, rhs, low)


def enter_kernel(parts, rhs_t, linv, fmat, vec, spread):
    made = []
    for i in range(2):
        total = parts[0, i]
        for g in range(1, GRID):
            total = total + parts[g, i]
        made.append(product(split(rhs_t[i] - total), split(linv[i]), NT))
        vec[i] = made[i]
    last = made[1] + product(split(made[0]), split(fmat[1]), NT)
    for g in range(GRID):
        spread[g] = last


def turn_kernel(place, values, chain, vec, fmat, uinv, bmat, out, spread, states):
    states[0] = jnp.zeros(states.shape[1:], jnp.float32)
    states[1] = values[0]
    carried = values[0]
    for h in range(1, GRID - 1):
        carried = values[h] + product(split(carried), split(chain[h]), NT)
        states[h + 1] = carried
    incoming = states[place[2]]
    first = vec[0] + product(split(incoming), split(fmat[0]), NT)
    second = vec[1] + product(split(first), split(fmat[1]), NT)
    upper_second = product(split(second), split(uinv[1]), NT)
    upper_first = product(split(first), split(uinv[0]), NT)
    out[0] = upper_first
    out[1] = upper_second
    last = upper_first + product(split(upper_second), split(bmat[0]), NT)
    for g in range(GRID):
        spread[g] = last


def leave_kernel(place, values, chain, vec, bmat, out, states):
    states[GRID - 1] = jnp.zeros(states.shape[1:], jnp.float32)
    states[GRID - 2] = values[GRID - 1]
    carried = values[GRID - 1]
    for h in range(GRID - 2, 0, -1):
        carried = values[h] + product(split(carried), split(chain[h]), NT)
        states[h - 1] = carried
    incoming = states[place[2]]
    second = vec[1] + product(split(incoming), split(bmat[1]), NT)
    out[1] = second
    out[0] = vec[0] + product(split(second), split(bmat[0]), NT)


def leaf_back_kernel(targets, place, uinv, up, fwd, solved, out, own):
    k = pl.program_id(0)
    rest = fwd[0]
    for c in range(2):
        t = targets[2 * k + c]
        picked = solved[:, t].reshape(TILE, TILE)
        rest = rest - product(split(up[0, c]), split(picked), NT)
    out[0] = product(split(uinv[0]), split(rest), NN)

    @pl.when(k < 2)
    def _():
        own[k] = solved[:, 2 * place[2] + k].reshape(TILE, TILE).T


def leaf_back(targets, place, uinv, up, fwd, solved):
    leaves = uinv.shape[0]
    tile = pl.BlockSpec((1, TILE, TILE), lambda k, *_: (k, 0, 0))
    pair = pl.BlockSpec((1, 2, TILE, TILE), lambda k, *_: (k, 0, 0, 0))
    return pl.pallas_call(
        leaf_back_kernel,
        out_shape=[
            jax.ShapeDtypeStruct(uinv.shape, jnp.float32),
            jax.ShapeDtypeStruct((2, TILE, TILE), jnp.float32),
        ],
        grid_spec=pltpu.PrefetchScalarGridSpec(
            num_scalar_prefetch=2,
            grid=(leaves,),
            in_specs=[tile, pair, tile, whole],
            out_specs=[tile, pl.BlockSpec((2, TILE, TILE), lambda k, *_: (0, 0, 0))],
        ),
        compiler_params=params(),
        name="leaf_back",
    )(targets, place, uinv, up, fwd, solved)


def local(
    leaf_rhs,
    leaf_linv,
    leaf_uinv,
    low_couple,
    up_couple,
    targets,
    top_rhs,
    top_linv,
    top_uinv,
    top_lower,
    top_upper,
):
    layer, grid = lax.axis_index("layer"), lax.axis_index("grid")
    core, z = lax.rem(layer, 2), lax.div(layer, 2)
    place = jnp.stack([core, z, grid, layer]).astype(jnp.int32)
    flat = targets.reshape(-1)
    struct = jax.ShapeDtypeStruct
    square = struct((TILE, TILE), jnp.float32)
    two = struct((2, TILE, TILE), jnp.float32)
    slim = struct((2, COLS, TILE), jnp.float32)
    spread = struct((GRID, COLS, TILE), jnp.float32)
    smem = pl.BlockSpec(memory_space=pltpu.SMEM)

    fmat, bmat, fall, ball, rhs_t = pl.pallas_call(
        prepare_kernel,
        out_shape=[two, two, square, square, two],
        in_specs=[whole] * 5,
        out_specs=[whole] * 5,
        compiler_params=params(),
        name="prepare",
    )(top_linv, top_lower, top_uinv, top_upper, top_rhs)
    fchain = lax.all_gather(fall, "grid", axis=0, tiled=False)
    bchain = lax.all_gather(ball, "grid", axis=0, tiled=False)

    fwd, *parts = leaf_forward(flat, place, leaf_linv, leaf_rhs, low_couple)
    other = [(i, i + 1 - 2 * (i % 2)) for i in range(LAYERS)]
    sums = [parts[d] + lax.ppermute(parts[4 + d], "layer", other) for d in range(4)]

    def along_z(value, d):
        return lax.ppermute(value, "layer", [(i, (i + 2 * d) % LAYERS) for i in range(LAYERS)])

    total = sums[0] + along_z(sums[1], 1) + along_z(sums[2], 2) + along_z(sums[3], 3)
    arrived = lax.all_to_all(
        total.reshape(GRID * 2, COLS, TILE), "grid", split_axis=0, concat_axis=0, tiled=True
    ).reshape(GRID, 2, COLS, TILE)

    mine = pl.BlockSpec((2, COLS, TILE), lambda i, where: (0, where[3], 0))

    def plain(shape):
        return pl.BlockSpec(shape, lambda i, where: (0,) * len(shape))

    def enter(where, *refs):
        enter_kernel(*refs)

    vec, sent = pl.pallas_call(
        enter,
        out_shape=[slim, spread],
        grid_spec=pltpu.PrefetchScalarGridSpec(
            num_scalar_prefetch=1,
            grid=(1,),
            in_specs=[
                plain((GRID, 2, COLS, TILE)),
                mine,
                plain((2, TILE, TILE)),
                plain((2, TILE, TILE)),
            ],
            out_specs=[plain((2, COLS, TILE)), plain((GRID, COLS, TILE))],
        ),
        compiler_params=params(),
        name="enter",
    )(place, arrived, rhs_t, top_linv, fmat)

    values = lax.all_to_all(sent, "grid", split_axis=0, concat_axis=0, tiled=True)
    states = pltpu.VMEM((GRID, COLS, TILE), jnp.float32)
    upper_vec, sent_back = pl.pallas_call(
        turn_kernel,
        out_shape=[slim, spread],
        in_specs=[smem] + [whole] * 6,
        out_specs=[whole] * 2,
        scratch_shapes=[states],
        compiler_params=params(),
        name="turn",
    )(place, values, fchain, vec, fmat, top_uinv, bmat)

    values_back = lax.all_to_all(sent_back, "grid", split_axis=0, concat_axis=0, tiled=True)
    sol_t = pl.pallas_call(
        leave_kernel,
        out_shape=slim,
        in_specs=[smem] + [whole] * 4,
        out_specs=whole,
        scratch_shapes=[states],
        compiler_params=params(),
        name="leave",
    )(place, values_back, bchain, upper_vec, bmat)

    solved = lax.all_gather(sol_t, ("layer", "grid"), axis=0, tiled=True)
    solved = solved.reshape(LAYERS, TOPS, COLS, TILE)
    return tuple(leaf_back(flat, place, leaf_uinv, up_couple, fwd, solved))


def solution(mesh):
    leaf = P(("layer", "grid"), None, None)
    leaf_pair = P(("layer", "grid"), None, None, None)
    top = P("grid", None, None)
    return jax.shard_map(
        local,
        mesh=mesh,
        in_specs=(leaf, leaf, leaf, leaf_pair, leaf_pair, P(("layer", "grid"), None))
        + (top,) * 5,
        out_specs=(leaf, top),
        check_vma=False,
    )
```

time: 659 us -> 256 us (0.39)
  waiting for transfers between devices: 463 us -> 131 us
  starting transfers between devices: 97.9 us -> 11.8 us
  matrix products: 54.1 us -> 0 us
  Pallas kernels: 0 us -> 52 us
  blocking collectives: 0 us -> 40 us
  local copies, waits for them, and re-layouts: 28 us -> 2.18 us
    psum x1 -> x0, waiting for transfers between devices: 161 us -> none  [local(): summed = lax.psum(partial_value, ('layer', 'grid'))]
    ppermute x30 -> x7, waiting for transfers between devices: 190 us -> 45.8 us  [the longest x3 43.9 us: along_z(): lax.ppermute(value, 'layer', [(i, (i + 2 * d) % LAYERS) for i in range(LA...]
    ppermute x30 -> x7, starting transfers between devices: 97.6 us -> 8.09 us  [the longest x3 5.99 us: along_z(): lax.ppermute(value, 'layer', [(i, (i + 2 * d) % LAYERS) for i in range(LA...]
    dot_general x47 -> x0, matrix products: 54.1 us -> none  [the longest x30 11.4 us: one_turn(): result = jnp.dot(matrix, carried, precision=highest) + vector]
    pallas_call x0 -> x6, Pallas kernels: none -> 52 us  [the longest x1 15.4 us: leaf_forward(): pl.pallas_call(leaf_forward_kernel, out_shape=[jax.ShapeDtypeStruct(linv....]
    all_to_all x0 -> x2, blocking collectives: none -> 40 us  [the longest x1 24 us: local(): lax.all_to_all(total.reshape(GRID * 2, COLS, TILE), 'grid', split_axis=0,...]
    all_gather x1 -> x3, waiting for transfers between devices: 112 us -> 75.6 us  [the longest x1 75.6 us: local(): solved = lax.all_gather(sol_t, ('layer', 'grid'), axis=0, tiled=True)]
    dot_general x2 -> x0, local copies, waits for them, and re-layouts: 13.7 us -> none  [the longest x1 8.1 us: local(): jnp.einsum('lct,lcir->tir', owners, coupled, precision=highest)]
  transfers between devices with their start and end apart: 32 -> 11, of which waited for: 32 -> 6; matrix products, arithmetic and copies ran while one was open for 0% -> 2% of each run, Pallas kernels for 0% -> 11%
where the time goes in v1:
time: 256 us; the launch traced here: 255 us
  waiting for transfers between devices  131 us (51%)
  Pallas kernels  52 us (20%)
  blocking collectives  40 us (16%)
  between operations  13.8 us (5%)
  starting transfers between devices  11.8 us (5%)
  other arithmetic  4.32 us (2%)
    all_gather x1, waiting for transfers between devices, local(): solved = lax.all_gather(sol_t, ('layer', 'grid'), axis=0, tiled=True)  75.6 us
    ppermute x3, waiting for transfers between devices, along_z(): lax.ppermute(value, 'layer', [(i, (i + 2 * d) % LAYERS) for i in range(LA...  43.9 us
    all_to_all x1, blocking collectives, local(): lax.all_to_all(total.reshape(GRID * 2, COLS, TILE), 'grid', split_axis=0,...  24 us
    all_to_all x1, blocking collectives, local(): lax.all_to_all(sent, 'grid', split_axis=0, concat_axis=0, tiled=True)  16 us
    pallas_call x1, Pallas kernels, leaf_forward(): pl.pallas_call(leaf_forward_kernel, out_shape=[jax.ShapeDtypeStruct(linv....  15.4 us
    pallas_call x1, Pallas kernels, leaf_back(): pl.pallas_call(leaf_back_kernel, out_shape=[jax.ShapeDtypeStruct(uinv.sha...  13.7 us
    all_to_all x1, waiting for transfers between devices, local(): lax.all_to_all(sent_back, 'grid', split_axis=0, concat_axis=0, tiled=True)  8.83 us
    pallas_call x1, Pallas kernels, local(): pl.pallas_call(turn_kernel, out_shape=[slim, spread], in_specs=[smem] + [...  8.23 us
  transfers between devices with their start and end apart: 11, of which 6 were waited for; matrix products, arithmetic and copies ran while one was open for 2% of the time, Pallas kernels for 11%

profile of v1, /device:TPU:1, one launch (start us, length us, event | category | flops | bytes accessed | tf_op | source)
XLA Modules:
  0.0 255.1 jit_solution(12247448089966475208)
XLA Ops:
  7.2 3.8 %prepare.1 = (f32[2,256,256]{2,1,0:T(8,128)}, f32[2,256,256]{2,1,0:T(8,128)}, f32[256,256]{1,0:T(8,128)}, f32[256,256]{1,0:T(8,128)}, f32[2,256,256]{2,1,0:T(8,128)}) custom-call(f32[2,256,256]{2,1,0:T(8,128)} %refs_2_.1, f32[2,256,256]{2,1,0:T(8,128)} %lower.1, f32[2,256,256]{2,1,0:T(8,128)} %uinv.4, f32[2,256,256]{2,1,0:T(8,128)} %upper.1, f32[2,256,256]{2,1,0:T(8,128)} %rhs.3), custom_call_target="tpu_custom_call" | custom-call | tf_op jit(solution)/shard_map/prepare/pallas_call | solution.py:220
  11.1 0.7 all-gather.10.cloned.1.call-update
  11.8 0.8 copy.15
  13.8 15.4 %leaf_forward.1 = (f32[8,256,256]{2,1,0:T(8,128)}, f32[32,32,256]{2,1,0:T(8,128)}, f32[32,32,256]{2,1,0:T(8,128)}, f32[32,32,256]{2,1,0:T(8,128)}, f32[32,32,256...) custom-call(s32[16]{0:T(128)} %reshape.13.targets, ...), custom_call_target="tpu_custom_call" | custom-call | tf_op jit(solution)/shard_map/leaf_forward/pallas_call | solution.py:98
  29.2 1.5 collective-permute-start.1
  31.3 1.9 collective-permute-done.1
  33.2 1.5 add.22
  34.7 1.7 collective-permute-start.2
  36.4 1.4 add.24
  37.8 3.4 %collective-permute-start.4 = (f32[32,32,256]{2,1,0:T(8,128)S(1)}, f32[32,32,256]{2,1,0:T(8,128)S(1)}, u32[]{:S(2)}, u32[]{:S(2)}) collective-permute-start(f32[32,32,256]{2,1,0:T(8,128)S(1)} %add.24), channel_id=1, source_target_pairs={{0,64},{16,80},{32,96},{48,112},{64,0},{80,16},{96,32},{112,48},{1... | collective-permute-start | bytes 3145736 | tf_op jit(solution)/shard_map/ppermute | solution.py:236
  41.5 0.8 collective-permute-start.6
  42.3 19.7 %collective-permute-done.2 = f32[32,32,256]{2,1,0:T(8,128)S(1)} collective-permute-done((f32[32,32,256]{2,1,0:T(8,128)S(1)}, f32[32,32,256]{2,1,0:T(8,128)S(1)}, u32[]{:S(2)}, u32[]{:S(2)}) %collective-permute-start.2) | collective-permute-done | bytes 1048608 | tf_op jit(solution)/shard_map/ppermute | solution.py:236
  61.9 23.2 %collective-permute-done.4 = f32[32,32,256]{2,1,0:T(8,128)S(1)} collective-permute-done((f32[32,32,256]{2,1,0:T(8,128)S(1)}, f32[32,32,256]{2,1,0:T(8,128)S(1)}, u32[]{:S(2)}, u32[]{:S(2)}) %collective-permute-start.4) | collective-permute-done | bytes 1048608 | tf_op jit(solution)/shard_map/ppermute | solution.py:236
  85.2 1.0 collective-permute-done.6
  86.8 24.0 %all_to_all.15 = f32[32,32,256]{2,1,0:T(8,128)} all-to-all(f32[32,32,256]{2,1,0:T(8,128)S(1)} %add_add_fusion), channel_id=1, replica_groups=mesh['layer'=8,'grid'=16] {'grid'}, dimensions={0} | all-to-all | bytes 2097152 | tf_op jit(solution)/shard_map/all_to_all | solution.py:239
  110.8 3.6 %enter.1 = (f32[2,32,256]{2,1,0:T(8,128)}, f32[16,32,256]{2,1,0:T(8,128)}) custom-call(s32[4]{0:T(128)} %pad_add_fusion.place.where, f32[16,2,32,256]{3,2,1,0:T(8,128)} %bitcast.11, f32[2,256,256]{2,1,0:T(8,128)} %get-tuple-element.29.refs_1_, f32[2,256,256]{2,1,0:T(8,128)} %refs_2_.1, f32[2,256,256]{2,1,0:T(8,128)} %get-tuple-element.30.refs_3_.fmat), custom_call_target="tpu_custom_call" | custom-call | tf_op jit(solution)/shard_map/enter/pallas_call | solution.py:251
  114.4 16.0 %all_to_all.16.values = f32[16,32,256]{2,1,0:T(8,128)} all-to-all(f32[16,32,256]{2,1,0:T(8,128)} %get-tuple-element.31), channel_id=1, replica_groups=mesh['layer'=8,'grid'=16] {'grid'}, dimensions={0} | all-to-all | bytes 1048576 | tf_op jit(solution)/shard_map/all_to_all | solution.py:269
  130.4 8.2 %turn.1 = (f32[2,32,256]{2,1,0:T(8,128)}, f32[16,32,256]{2,1,0:T(8,128)}) custom-call(s32[4]{0:T(128)} %pad_add_fusion.place.where, f32[16,32,256]{2,1,0:T(8,128)} %all_to_all.16.values, f32[16,256,256]{2,1,0:T(8,128)} %bitcast.9, f32[2,32,256]{2,1,0:T(8,128)} %get-tuple-element.33.vec, f32[2,256,256]{2,1,0:T(8,128)} %get-tuple-element.30.refs_3_.fmat, ...), custom_call_target="tpu_custom_call" | custom-call | tf_op jit(solution)/shard_map/turn/pallas_call | solution.py:271
  138.6 3.6 %all-to-all-start.2 = ((f32[16,32,256]{2,1,0:T(8,128)}), f32[16,32,256]{2,1,0:T(8,128)S(1)}, u32[]{:S(2)}, u32[]{:S(2)}) async-start(f32[16,32,256]{2,1,0:T(8,128)} %get-tuple-element.35), calls=%async_computation.2 | async-start | bytes 1048576 | tf_op jit(solution)/shard_map/all_to_all | solution.py:281
  142.3 8.8 %all-to-all-done.2.values = f32[16,32,256]{2,1,0:T(8,128)S(1)} async-done(((f32[16,32,256]{2,1,0:T(8,128)}), f32[16,32,256]{2,1,0:T(8,128)S(1)}, u32[]{:S(2)}, u32[]{:S(2)}) %all-to-all-start.2) | async-done | bytes 524320 | tf_op jit(solution)/shard_map/all_to_all | solution.py:281
  151.1 0.8 copy-done
  151.9 7.3 %leave.1 = f32[2,32,256]{2,1,0:T(8,128)} custom-call(s32[4]{0:T(128)} %pad_add_fusion.place.where, f32[16,32,256]{2,1,0:T(8,128)} %copy-done, f32[16,256,256]{2,1,0:T(8,128)} %bitcast.10, f32[2,32,256]{2,1,0:T(8,128)} %get-tuple-element.37.vec, f32[2,256,256]{2,1,0:T(8,128)} %get-tuple-element.34.bmat), custom_call_target="tpu_custom_call" | custom-call | tf_op jit(solution)/shard_map/leave/pallas_call | solution.py:282
  159.2 75.6 %all-gather.6.cloned.1.call-done = f32[256,32,256]{2,1,0:T(8,128)} async-done(((f32[2,32,256]{2,1,0:T(8,128)}), f32[256,32,256]{2,1,0:T(8,128)}) %all-gather.6.cloned.1.call-update) | async-done | bytes 8388624 | tf_op jit(solution)/shard_map/all_gather | solution.py:292
  234.8 13.7 %leaf_back.1 = (f32[8,256,256]{2,1,0:T(8,128)}, f32[2,256,256]{2,1,0:T(8,128)}) custom-call(s32[16]{0:T(128)} %reshape.13.targets, s32[4]{0:T(128)} %pad_add_fusion.place.where, f32[8,256,256]{2,1,0:T(8,128)} %uinv.5, f32[8,2,256,256]{3,2,1,0:T(8,128)} %up.1, f32[8,256,256]{2,1,0:T(8,128)} %get-tuple-element.20.fwd, f32[8,32,32,256]{3,2,1,0:T(8,128)} %bitcast.8), custom_call_target="tpu_custom_call" | custom-call | tf_op jit(solution)/shard_map/leaf_back/pallas_call | solution.py:179
  (22 shorter events, 2.9 us)
Async XLA Ops:
  7.2 123.2 %all-gather.8.cloned.1.call-start = ((), (), s32[]{:S(2)}) async-start(), calls=%async_computation.4 | async-start | bytes 4456448 | tf_op jit(solution)/shard_map/all_gather | solution.py:228
  11.0 131.2 %all-gather.10.cloned.1.call-start = ((), (), s32[]{:S(2)}) async-start(), calls=%async_computation.5 | async-start | bytes 4456448 | tf_op jit(solution)/shard_map/all_gather | solution.py:229
  29.2 12.1 %copy-start.1 = (f32[32,32,256]{2,1,0:T(8,128)S(1)}, f32[32,32,256]{2,1,0:T(8,128)}, u32[]{:S(2)}) copy-start(f32[32,32,256]{2,1,0:T(8,128)} %get-tuple-element.27) | copy-start | bytes 3145732
  29.2 4.0 %collective-permute-start.1 = (f32[32,32,256]{2,1,0:T(8,128)}, f32[32,32,256]{2,1,0:T(8,128)S(1)}, u32[]{:S(2)}, u32[]{:S(2)}) collective-permute-start(f32[32,32,256]{2,1,0:T(8,128)} %get-tuple-element.24), channel_id=1, source_target_pairs={{0,16},{16,0},{32,48},{48,32},{64,80},{80,64},{96,112},{112,96},{1... | collective-permute-start | bytes 3145736 | tf_op jit(solution)/shard_map/ppermute | solution.py:233
  30.7 5.7 %collective-permute-start.3 = (f32[32,32,256]{2,1,0:T(8,128)}, f32[32,32,256]{2,1,0:T(8,128)S(1)}, u32[]{:S(2)}, u32[]{:S(2)}) collective-permute-start(f32[32,32,256]{2,1,0:T(8,128)} %get-tuple-element.26), channel_id=1, source_target_pairs={{0,16},{16,0},{32,48},{48,32},{64,80},{80,64},{96,112},{112,96},{1... | collective-permute-start | bytes 3145736 | tf_op jit(solution)/shard_map/ppermute | solution.py:233
  30.8 10.5 %collective-permute-start.5 = (f32[32,32,256]{2,1,0:T(8,128)}, f32[32,32,256]{2,1,0:T(8,128)S(1)}, u32[]{:S(2)}, u32[]{:S(2)}) collective-permute-start(f32[32,32,256]{2,1,0:T(8,128)} %get-tuple-element.28), channel_id=1, source_target_pairs={{0,16},{16,0},{32,48},{48,32},{64,80},{80,64},{96,112},{112,96},{1... | collective-permute-start | bytes 3145736 | tf_op jit(solution)/shard_map/ppermute | solution.py:233
  31.2 11.0 %collective-permute-start = (f32[32,32,256]{2,1,0:T(8,128)}, f32[32,32,256]{2,1,0:T(8,128)S(1)}, u32[]{:S(2)}, u32[]{:S(2)}) collective-permute-start(f32[32,32,256]{2,1,0:T(8,128)} %get-tuple-element.22), channel_id=1, source_target_pairs={{0,16},{16,0},{32,48},{48,32},{64,80},{80,64},{96,112},{112,96},{1... | collective-permute-start | bytes 3145736 | tf_op jit(solution)/shard_map/ppermute | solution.py:233
  33.2 53.0 %copy-start.2 = (f32[32,32,256]{2,1,0:T(8,128)S(1)}, f32[32,32,256]{2,1,0:T(8,128)}, u32[]{:S(2)}) copy-start(f32[32,32,256]{2,1,0:T(8,128)} %get-tuple-element.21) | copy-start | bytes 3145732
  34.7 27.2 %collective-permute-start.2 = (f32[32,32,256]{2,1,0:T(8,128)S(1)}, f32[32,32,256]{2,1,0:T(8,128)S(1)}, u32[]{:S(2)}, u32[]{:S(2)}) collective-permute-start(f32[32,32,256]{2,1,0:T(8,128)S(1)} %add.22), channel_id=1, source_target_pairs={{0,32},{16,48},{32,64},{48,80},{64,96},{80,112},{96,0},{112,16},{1... | collective-permute-start | bytes 3145736 | tf_op jit(solution)/shard_map/ppermute | solution.py:236
  37.8 47.3 %collective-permute-start.4 = (f32[32,32,256]{2,1,0:T(8,128)S(1)}, f32[32,32,256]{2,1,0:T(8,128)S(1)}, u32[]{:S(2)}, u32[]{:S(2)}) collective-permute-start(f32[32,32,256]{2,1,0:T(8,128)S(1)} %add.24), channel_id=1, source_target_pairs={{0,64},{16,80},{32,96},{48,112},{64,0},{80,16},{96,32},{112,48},{1... | collective-permute-start | bytes 3145736 | tf_op jit(solution)/shard_map/ppermute | solution.py:236
  41.5 44.7 %collective-permute-start.6 = (f32[32,32,256]{2,1,0:T(8,128)S(1)}, f32[32,32,256]{2,1,0:T(8,128)S(1)}, u32[]{:S(2)}, u32[]{:S(2)}) collective-permute-start(f32[32,32,256]{2,1,0:T(8,128)S(1)} %add.26), channel_id=1, source_target_pairs={{0,96},{16,112},{32,0},{48,16},{64,32},{80,48},{96,64},{112,80},{1... | collective-permute-start | bytes 3145736 | tf_op jit(solution)/shard_map/ppermute | solution.py:236
  138.6 12.5 %all-to-all-start.2 = ((f32[16,32,256]{2,1,0:T(8,128)}), f32[16,32,256]{2,1,0:T(8,128)S(1)}, u32[]{:S(2)}, u32[]{:S(2)}) async-start(f32[16,32,256]{2,1,0:T(8,128)} %get-tuple-element.35), calls=%async_computation.2 | async-start | bytes 1048576 | tf_op jit(solution)/shard_map/all_to_all | solution.py:281
  142.2 92.6 %all-gather.6.cloned.1.call-start = ((), (), s32[]{:S(2)}) async-start(), calls=%async_computation.3 | async-start | bytes 8454144 | tf_op jit(solution)/shard_map/all_gather | solution.py:292
  151.1 0.8 copy-start
Sparse Core Ops, SparseCore 0:
  11.2 54.6 all-gather.7
  67.9 59.0 all-gather.9
  159.3 75.4 all-gather.5

commit v2 on v0

v2 whole, which is shorter than its diff:
```python
import jax
import jax.numpy as jnp
from jax import lax
from jax.experimental import pallas as pl
from jax.experimental.pallas import tpu as pltpu
from jax.sharding import PartitionSpec as P

LAYERS = 8
GRID = 16
TILE = 256
COLS = TILE // LAYERS
TOPS = 32
MIB = 1024 * 1024
HALF = TILE // 2

NN = (((1,), (0,)), ((), ()))
NT = (((1,), (1,)), ((), ()))

whole = pl.BlockSpec(memory_space=pltpu.VMEM)
in_hbm = pl.BlockSpec(memory_space=pl.ANY)


def split(value):
    high = value.astype(jnp.bfloat16)
    low = (value - high.astype(jnp.float32)).astype(jnp.bfloat16)
    return high, low


def product(left, right, dims):
    ((near,), (far,)), _ = dims
    wide = jnp.concatenate([left[0], left[0], left[1]], axis=near)
    tall = jnp.concatenate([right[0], right[1], right[0]], axis=far)
    return lax.dot_general(wide, tall, dims, preferred_element_type=jnp.float32)


def params(mib):
    return pltpu.CompilerParams(vmem_limit_bytes=mib * MIB)


def prepare_kernel(linv, lower, uinv, upper, rhs, fmat, bmat, share, rhs_t):
    core = lax.rem(lax.axis_index("layer"), 2)
    rows = pl.ds(pl.multiple_of(core * HALF, HALF), HALF)

    def maps(inverse, coupling, out):
        for i in range(2):
            out[i] = -product(split(inverse[i]), split(coupling[i]), NN)

    maps(linv, lower, fmat)
    share[0] = product(split(fmat[1, rows]), split(fmat[0]), NN)
    maps(uinv, upper, bmat)
    share[1] = product(split(bmat[0, rows]), split(bmat[1]), NN)
    for i in range(2):
        rhs_t[i] = rhs[i].T


def leaf_forward_kernel(targets, linv, rhs, low, fwd, *rest):
    outs, (acc, sems) = rest[:10], rest[10:]
    k = pl.program_id(0)
    layer = lax.axis_index("layer")
    core, z = lax.rem(layer, 2), lax.div(layer, 2)

    @pl.when(k == 0)
    def _():
        def clear(i, carry):
            acc[i] = jnp.zeros(acc.shape[1:], jnp.float32)
            return carry

        lax.fori_loop(0, acc.shape[0], clear, 0, unroll=8)

    leaves = linv.shape[0]
    turned = []
    for leaf in range(leaves):
        value = product(split(linv[leaf]), split(rhs[leaf]), NN)
        fwd[leaf] = value
        turned.append(split(value.T))
    for leaf in range(leaves):
        for c in range(2):
            t = targets[k * leaves + leaf, c]
            owner, odd = lax.div(t, 2), lax.rem(t, 2)
            coupled = product(turned[leaf], split(low[leaf, c]), NT)
            for goal in range(LAYERS):
                side = lax.rem(goal % 2 + core, 2)
                away = lax.rem(goal // 2 - z + 4, 4)
                even_place = (side * 4 + away) * GRID + owner
                odd_place = 8 * GRID + (side * GRID + owner) * 4 + away
                acc[jnp.where(odd == 0, even_place, odd_place)] += coupled[
                    goal * COLS : (goal + 1) * COLS
                ]

    @pl.when(k == pl.num_programs(0) - 1)
    def _():
        copies, start = [], 0
        for i, out in enumerate(outs):
            size = out.shape[0]
            copies.append(pltpu.make_async_copy(acc.at[pl.ds(start, size)], out, sems.at[i]))
            start += size
        for copy in copies:
            copy.start()
        for copy in copies:
            copy.wait()


def leaf_forward(targets, linv, rhs, low, step=2):
    leaves = linv.shape[0]
    tile = pl.BlockSpec((step, TILE, TILE), lambda k, *_: (k, 0, 0))
    pair = pl.BlockSpec((step, 2, TILE, TILE), lambda k, *_: (k, 0, 0, 0))
    even = jax.ShapeDtypeStruct((GRID, COLS, TILE), jnp.float32)
    odd = jax.ShapeDtypeStruct((GRID * 4, COLS, TILE), jnp.float32)
    return pl.pallas_call(
        leaf_forward_kernel,
        out_shape=[jax.ShapeDtypeStruct(linv.shape, jnp.float32)] + [even] * 8 + [odd] * 2,
        grid_spec=pltpu.PrefetchScalarGridSpec(
            num_scalar_prefetch=1,
            grid=(leaves // step,),
            in_specs=[tile, tile, pair],
            out_specs=[tile] + [pl.BlockSpec(memory_space=pltpu.HBM)] * 10,
            scratch_shapes=[
                pltpu.VMEM((16 * GRID, COLS, TILE), jnp.float32),
                pltpu.SemaphoreType.DMA((10,)),
            ],
        ),
        compiler_params=params(56),
        name="leaf_forward",
    )(targets, linv, rhs, low)


def fold_kernel(parts, *outs):
    for i, out in enumerate(outs):
        total = parts[0, i]
        for g in range(1, GRID):
            total = total + parts[g, i]
        out[...] = total


def enter_kernel(even, odd, odd_1, odd_2, odd_3, rhs_t, linv, fmat, vec, spread):
    rows = pl.ds(pl.multiple_of(lax.axis_index("layer") * COLS, COLS), COLS)
    total = even[0]
    for g in range(1, GRID):
        total = total + even[g]
    first = product(split(rhs_t[0, rows] - total), split(linv[0]), NT)
    total = (odd[...] + odd_1[...]) + (odd_2[...] + odd_3[...])
    second = product(split(rhs_t[1, rows] - total), split(linv[1]), NT)
    vec[0] = first
    vec[1] = second
    last = second + product(split(first), split(fmat[1]), NT)
    for g in range(GRID):
        spread[g] = last


def chain_kernel(own, other, forward, backward):
    core = lax.rem(lax.axis_index("layer"), 2)
    for i, source in enumerate((own, other)):
        side = core if i == 0 else 1 - core
        rows = pl.ds(pl.multiple_of(side * HALF, HALF), HALF)
        for h in range(1, GRID - 1):
            for which, out in enumerate((forward, backward)):
                high, low = split(source[2 * h + which])
                out[0, h, rows] = high
                out[1, h, rows] = low


def chain_pairs(own, other):
    pairs = jax.ShapeDtypeStruct((2, GRID, TILE, TILE), jnp.bfloat16)
    return pl.pallas_call(
        chain_kernel,
        out_shape=[pairs, pairs],
        in_specs=[whole] * 2,
        out_specs=[whole] * 2,
        compiler_params=params(20),
        name="chain_pairs",
    )(own, other)


def turn_kernel(values, chain, vec, fmat, uinv, bmat, out, spread, states):
    states[0] = jnp.zeros(states.shape[1:], jnp.float32)
    states[1] = values[0]
    carried = values[0]
    for h in range(1, GRID - 1):
        carried = values[h] + product(split(carried), (chain[0, h], chain[1, h]), NT)
        states[h + 1] = carried
    incoming = states[lax.axis_index("grid")]
    first = vec[0] + product(split(incoming), split(fmat[0]), NT)
    second = vec[1] + product(split(first), split(fmat[1]), NT)
    upper_second = product(split(second), split(uinv[1]), NT)
    upper_first = product(split(first), split(uinv[0]), NT)
    out[0] = upper_first
    out[1] = upper_second
    last = upper_first + product(split(upper_second), split(bmat[0]), NT)
    for g in range(GRID):
        spread[g] = last


def leave_kernel(values, chain, vec, bmat, even, spread, states):
    states[GRID - 1] = jnp.zeros(states.shape[1:], jnp.float32)
    states[GRID - 2] = values[GRID - 1]
    carried = values[GRID - 1]
    for h in range(GRID - 2, 0, -1):
        carried = values[h] + product(split(carried), (chain[0, h], chain[1, h]), NT)
        states[h - 1] = carried
    incoming = states[lax.axis_index("grid")]
    second = vec[1] + product(split(incoming), split(bmat[1]), NT)
    even[...] = vec[0] + product(split(second), split(bmat[0]), NT)
    for g in range(GRID):
        spread[g] = second


def copies_kernel(first, second, third, fourth, spread):
    for g in range(GRID):
        for d, value in enumerate((first, second, third, fourth)):
            spread[g, d] = value[...]


def leaf_ready_kernel(uinv, up, fwd, base, factor):
    for leaf in range(uinv.shape[0]):
        inverse = split(uinv[leaf])
        base[leaf] = product(inverse, split(fwd[leaf]), NN)
        for c in range(2):
            factor[leaf, c] = product(inverse, split(up[leaf, c]), NN)


def leaf_ready(uinv, up, fwd, step=2):
    tile = pl.BlockSpec((step, TILE, TILE), lambda k: (k, 0, 0))
    pair = pl.BlockSpec((step, 2, TILE, TILE), lambda k: (k, 0, 0, 0))
    return pl.pallas_call(
        leaf_ready_kernel,
        out_shape=[jax.ShapeDtypeStruct(x.shape, jnp.float32) for x in (uinv, up)],
        grid=(uinv.shape[0] // step,),
        in_specs=[tile, pair, tile],
        out_specs=[tile, pair],
        compiler_params=params(20),
        name="leaf_ready",
    )(uinv, up, fwd)


def leaf_back_kernel(targets, base, factor, *rest):
    even, odd, (out, own, solved, sems) = rest[:2], rest[2], rest[3:]
    k = pl.program_id(0)
    leaves = base.shape[0]
    layer = lax.axis_index("layer")
    core, z = lax.rem(layer, 2), lax.div(layer, 2)

    @pl.when(k == 0)
    def _():
        copies = []
        for side in range(2):
            for d in range(4):
                place = 2 * lax.rem(z - d + 4, 4) + (core if side == 0 else 1 - core)
                for i, source in enumerate((even[side].at[:, d], odd.at[place])):
                    copies.append(
                        pltpu.make_async_copy(
                            source, solved.at[i, :, place], sems.at[i, side * 4 + d]
                        )
                    )
        for copy in copies:
            copy.start()
        for copy in copies:
            copy.wait()
        for i in range(2):
            own[i] = solved[i, lax.axis_index("grid")].reshape(TILE, TILE).T

    for leaf in range(leaves):
        value = base[leaf]
        for c in range(2):
            t = targets[k * leaves + leaf, c]
            picked = solved[lax.rem(t, 2), lax.div(t, 2)].reshape(TILE, TILE)
            value = value - product(split(factor[leaf, c]), split(picked), NT)
        out[leaf] = value


def leaf_back(targets, base, factor, even, odd, step=2):
    leaves = base.shape[0]
    tile = pl.BlockSpec((step, TILE, TILE), lambda k, *_: (k, 0, 0))
    pair = pl.BlockSpec((step, 2, TILE, TILE), lambda k, *_: (k, 0, 0, 0))
    return pl.pallas_call(
        leaf_back_kernel,
        out_shape=[
            jax.ShapeDtypeStruct(base.shape, jnp.float32),
            jax.ShapeDtypeStruct((2, TILE, TILE), jnp.float32),
        ],
        grid_spec=pltpu.PrefetchScalarGridSpec(
            num_scalar_prefetch=1,
            grid=(leaves // step,),
            in_specs=[tile, pair] + [in_hbm] * 3,
            out_specs=[tile, pl.BlockSpec((2, TILE, TILE), lambda k, *_: (0, 0, 0))],
            scratch_shapes=[
                pltpu.VMEM((2, GRID, LAYERS, COLS, TILE), jnp.float32),
                pltpu.SemaphoreType.DMA((2, 8)),
            ],
        ),
        compiler_params=params(56),
        name="leaf_back",
    )(targets, base, factor, *even, odd)


def call(kernel, outs, name, *args, scratch=(), mib=10):
    return pl.pallas_call(
        kernel,
        out_shape=[jax.ShapeDtypeStruct(shape, jnp.float32) for shape in outs],
        in_specs=[whole] * len(args),
        out_specs=[whole] * len(outs),
        scratch_shapes=list(scratch),
        compiler_params=params(mib),
        name=name,
    )(*args)


def after(values):
    return lax.optimization_barrier(values)


def other_core(value):
    return lax.ppermute(value, "layer", [(i, i + 1 - 2 * (i % 2)) for i in range(LAYERS)])


def along_z(value, steps):
    return lax.ppermute(value, "layer", [(i, (i + 2 * steps) % LAYERS) for i in range(LAYERS)])


def exchange(value):
    return lax.all_to_all(value, "grid", split_axis=0, concat_axis=0, tiled=True)


def local(
    leaf_rhs,
    leaf_linv,
    leaf_uinv,
    low_couple,
    up_couple,
    targets,
    top_rhs,
    top_linv,
    top_uinv,
    top_lower,
    top_upper,
):
    two = (2, TILE, TILE)
    slim = (2, COLS, TILE)
    piece = (COLS, TILE)
    spread = (GRID, COLS, TILE)

    tops = (top_linv, top_lower, top_uinv, top_upper, top_rhs)
    fmat, bmat, share, rhs_t = call(
        prepare_kernel, [two, two, (2, HALF, TILE), two], "prepare", *tops, mib=56
    )
    share, leaf_rhs = after((share, leaf_rhs))
    chain = lax.all_gather(share, "grid", axis=0, tiled=True)
    fwd, *parts = leaf_forward(targets, leaf_linv, leaf_rhs, low_couple)
    even_keep, even_send, odd_keep, odd_send = parts[:4], parts[4:8], parts[8], parts[9]
    even = [even_keep[d] + other_core(even_send[d]) for d in (1, 2, 3, 0)]
    odd = odd_keep + other_core(odd_send)
    even = even[3] + along_z(even[0], 1) + along_z(even[1], 2) + along_z(even[2], 3)
    odd = exchange(odd).reshape(GRID, 4, COLS, TILE)
    even, odd = after((even, odd))
    odd = call(fold_kernel, [piece] * 4, "fold", odd)
    odd = [odd[0]] + [along_z(odd[d], d) for d in range(1, 4)]
    even = exchange(even)

    vec, sent = call(
        enter_kernel, [slim, spread], "enter", even, *odd, rhs_t, tops[0], fmat
    )
    vec, sent, chain = after((vec, sent, chain))
    forward, backward = chain_pairs(chain, other_core(chain))
    values = exchange(sent)
    values, forward, backward = after((values, forward, backward))
    states = [pltpu.VMEM(spread, jnp.float32)]
    vec, sent = call(
        turn_kernel,
        [slim, spread],
        "turn",
        *(values, forward, vec, fmat, tops[2], bmat),
        scratch=states,
        mib=56,
    )
    sent, leaf_uinv = after((sent, leaf_uinv))
    values = exchange(sent)
    base, factor = leaf_ready(leaf_uinv, up_couple, fwd)
    values, base, factor = after((values, base, factor))
    even, sent = call(
        leave_kernel,
        [piece, spread],
        "leave",
        *(values, backward, vec, bmat),
        scratch=states,
        mib=56,
    )
    even = [even] + [along_z(even, d) for d in range(1, 4)]
    [even] = call(copies_kernel, [(GRID, 4, COLS, TILE)], "copies", *even)
    odd = exchange(sent)
    even, odd = after((even, odd))
    odd = lax.all_gather(odd, "layer", axis=0, tiled=False)
    even = exchange(even.reshape(GRID * 4, COLS, TILE)).reshape(GRID, 4, COLS, TILE)
    even = [even, other_core(even)]
    return tuple(leaf_back(targets, base, factor, even, odd))


def solution(mesh):
    leaf = P(("layer", "grid"), None, None)
    leaf_pair = P(("layer", "grid"), None, None, None)
    top = P("grid", None, None)
    return jax.shard_map(
        local,
        mesh=mesh,
        in_specs=(leaf, leaf, leaf, leaf_pair, leaf_pair, P(("layer", "grid"), None))
        + (top,) * 5,
        out_specs=(leaf, top),
        check_vma=False,
    )
```

time: 659 us -> 229 us (0.35)
  waiting for transfers between devices: 463 us -> 46.6 us
  matrix products: 54.1 us -> 0 us
  Pallas kernels: 0 us -> 50.5 us
  starting transfers between devices: 97.9 us -> 62.5 us
  blocking collectives: 0 us -> 28.1 us
    psum x1 -> x0, waiting for transfers between devices: 161 us -> none  [local(): summed = lax.psum(partial_value, ('layer', 'grid'))]
    ppermute x30 -> x16, waiting for transfers between devices: 190 us -> 37.9 us  [the longest x9 28.7 us: along_z(): lax.ppermute(value, 'layer', [(i, (i + 2 * steps) % LAYERS) for i in rang...]
    all_gather x1 -> x2, waiting for transfers between devices: 112 us -> 0.01 us  [the longest x1 0.01 us: local(): chain = lax.all_gather(share, 'grid', axis=0, tiled=True)]
    ppermute x30 -> x16, starting transfers between devices: 97.6 us -> 26.4 us  [the longest x9 14.6 us: along_z(): lax.ppermute(value, 'layer', [(i, (i + 2 * steps) % LAYERS) for i in rang...]
    dot_general x47 -> x0, matrix products: 54.1 us -> none  [the longest x30 11.4 us: one_turn(): result = jnp.dot(matrix, carried, precision=highest) + vector]
    pallas_call x0 -> x10, Pallas kernels: none -> 50.5 us  [the longest x6 21.9 us: call(): pl.pallas_call(kernel, out_shape=[jax.ShapeDtypeStruct(shape, jnp.float32...]
    all_to_all x0 -> x5, starting transfers between devices: none -> 36 us  [exchange(): lax.all_to_all(value, 'grid', split_axis=0, concat_axis=0, tiled=True)]
    all_to_all x0 -> x1, blocking collectives: none -> 28.1 us  [exchange(): lax.all_to_all(value, 'grid', split_axis=0, concat_axis=0, tiled=True)]
  transfers between devices with their start and end apart: 32 -> 23, of which waited for: 32 -> 15; matrix products, arithmetic and copies ran while one was open for 0% -> 2% of each run, Pallas kernels for 0% -> 9%
where the time goes in v2:
time: 229 us; the launch traced here: 228 us
  starting transfers between devices  62.5 us (27%)
  Pallas kernels  50.5 us (22%)
  waiting for transfers between devices  46.6 us (20%)
  blocking collectives  28.1 us (12%)
  local copies, waits for them, and re-layouts  21.5 us (9%)
  between operations  14.2 us (6%)
  other arithmetic  4.64 us (2%)
    all_to_all x5, starting transfers between devices, exchange(): lax.all_to_all(value, 'grid', split_axis=0, concat_axis=0, tiled=True)  36 us
    ppermute x9, waiting for transfers between devices, along_z(): lax.ppermute(value, 'layer', [(i, (i + 2 * steps) % LAYERS) for i in rang...  28.7 us
    all_to_all x1, blocking collectives, exchange(): lax.all_to_all(value, 'grid', split_axis=0, concat_axis=0, tiled=True)  28.1 us
    pallas_call x6, Pallas kernels, call(): pl.pallas_call(kernel, out_shape=[jax.ShapeDtypeStruct(shape, jnp.float32...  21.9 us
    unnamed x47, local copies, waits for them, and re-layouts  21.5 us
    ppermute x9, starting transfers between devices, along_z(): lax.ppermute(value, 'layer', [(i, (i + 2 * steps) % LAYERS) for i in rang...  14.6 us
    pallas_call x1, Pallas kernels, leaf_forward(): pl.pallas_call(leaf_forward_kernel, out_shape=[jax.ShapeDtypeStruct(linv....  12 us
    ppermute x7, starting transfers between devices, other_core(): lax.ppermute(value, 'layer', [(i, i + 1 - 2 * (i % 2)) for i in range(LAY...  11.8 us
  transfers between devices with their start and end apart: 23, of which 15 were waited for; matrix products, arithmetic and copies ran while one was open for 2% of the time, Pallas kernels for 9%

profile of v2, /device:TPU:1, one launch (start us, length us, event | category | flops | bytes accessed | tf_op | source)
XLA Modules:
  0.0 228.1 jit_solution(3943583708634139805)
XLA Ops:
  7.2 3.7 %prepare.1 = (f32[2,256,256]{2,1,0:T(8,128)}, f32[2,256,256]{2,1,0:T(8,128)}, f32[2,128,256]{2,1,0:T(8,128)}, f32[2,256,256]{2,1,0:T(8,128)}) custom-call(f32[2,256,256]{2,1,0:T(8,128)} %linv.5, f32[2,256,256]{2,1,0:T(8,128)} %lower.1, f32[2,256,256]{2,1,0:T(8,128)} %uinv.3, f32[2,256,256]{2,1,0:T(8,128)} %upper.1, f32[2,256,256]{2,1,0:T(8,128)} %rhs.1), custom_call_target="tpu_custom_call" | custom-call | tf_op jit(solution)/shard_map/prepare/pallas_call | solution.py:296
  11.6 12.0 %leaf_forward.1 = (f32[8,256,256]{2,1,0:T(8,128)}, f32[16,32,256]{2,1,0:T(8,128)}, f32[16,32,256]{2,1,0:T(8,128)}, f32[16,32,256]{2,1,0:T(8,128)}, f32[16,32,256...) custom-call(s32[8,2]{1,0:T(8,128)} %copy.16.targets, ...), custom_call_target="tpu_custom_call" | custom-call | tf_op jit(solution)/shard_map/leaf_forward/pallas_call | solution.py:109
  25.2 4.0 %collective-permute-done.7 = f32[64,32,256]{2,1,0:T(8,128)S(1)} collective-permute-done((f32[64,32,256]{2,1,0:T(8,128)}, f32[64,32,256]{2,1,0:T(8,128)S(1)}, u32[]{:S(2)}, u32[]{:S(2)}) %collective-permute-start.7) | collective-permute-done | bytes 2097184 | tf_op jit(solution)/shard_map/ppermute | solution.py:312
  29.1 3.4 %add.31 = f32[64,32,256]{2,1,0:T(8,128)} add(f32[64,32,256]{2,1,0:T(8,128)} %get-tuple-element.58, f32[64,32,256]{2,1,0:T(8,128)S(1)} %collective-permute-done.7) | non-fusion elementwise | flops 524288 | bytes 6291456 | tf_op jit(solution)/shard_map/add | solution.py:350
  32.6 7.0 %all-to-all-start = ((f32[64,32,256]{2,1,0:T(8,128)}), f32[64,32,256]{2,1,0:T(8,128)S(1)}, u32[]{:S(2)}, u32[]{:S(2)}) async-start(f32[64,32,256]{2,1,0:T(8,128)} %add.31), calls=%async_computation | async-start | bytes 4194304 | tf_op jit(solution)/shard_map/all_to_all | solution.py:320
  43.9 3.4 %collective-permute-start.4 = (f32[16,32,256]{2,1,0:T(8,128)S(1)}, f32[16,32,256]{2,1,0:T(8,128)S(1)}, u32[]{:S(2)}, u32[]{:S(2)}) collective-permute-start(f32[16,32,256]{2,1,0:T(8,128)S(1)} %add.27), channel_id=1, source_target_pairs={{0,64},{16,80},{32,96},{48,112},{64,0},{80,16},{96,32},{112,48},{1... | collective-permute-start | bytes 1572872 | tf_op jit(solution)/shard_map/ppermute | solution.py:316
  48.2 9.9 %collective-permute-done.2 = f32[16,32,256]{2,1,0:T(8,128)S(1)} collective-permute-done((f32[16,32,256]{2,1,0:T(8,128)S(1)}, f32[16,32,256]{2,1,0:T(8,128)S(1)}, u32[]{:S(2)}, u32[]{:S(2)}) %collective-permute-start.2) | collective-permute-done | bytes 524320 | tf_op jit(solution)/shard_map/ppermute | solution.py:316
  58.0 12.0 %collective-permute-done.4 = f32[16,32,256]{2,1,0:T(8,128)S(1)} collective-permute-done((f32[16,32,256]{2,1,0:T(8,128)S(1)}, f32[16,32,256]{2,1,0:T(8,128)S(1)}, u32[]{:S(2)}, u32[]{:S(2)}) %collective-permute-start.4) | collective-permute-done | bytes 524320 | tf_op jit(solution)/shard_map/ppermute | solution.py:316
  71.3 5.1 %all-to-all-done = f32[64,32,256]{2,1,0:T(8,128)S(1)} async-done(((f32[64,32,256]{2,1,0:T(8,128)}), f32[64,32,256]{2,1,0:T(8,128)S(1)}, u32[]{:S(2)}, u32[]{:S(2)}) %all-to-all-start) | async-done | bytes 2097184 | tf_op jit(solution)/shard_map/all_to_all | solution.py:320
  76.4 9.3 %all-to-all-start.1 = ((f32[16,32,256]{2,1,0:T(8,128)}), f32[16,32,256]{2,1,0:T(8,128)}, u32[]{:S(2)}, u32[]{:S(2)}) async-start(f32[16,32,256]{2,1,0:T(8,128)} %add_add_fusion), calls=%async_computation.1 | async-start | bytes 1048576 | tf_op jit(solution)/shard_map/all_to_all | solution.py:320
  87.8 3.5 %collective-permute-start.9 = (f32[32,256]{1,0:T(8,128)S(1)}, f32[32,256]{1,0:T(8,128)S(1)}, u32[]{:S(2)}, u32[]{:S(2)}) collective-permute-start(f32[32,256]{1,0:T(8,128)S(1)} %get-tuple-element.64), channel_id=1, source_target_pairs={{0,64},{16,80},{32,96},{48,112},{64,0},{80,16},{96,32},{112,48},{1... | collective-permute-start | bytes 98312 | tf_op jit(solution)/shard_map/ppermute | solution.py:316
  99.1 3.9 %collective-permute-start.11 = (f32[32,128,256]{2,1,0:T(8,128)}, f32[32,128,256]{2,1,0:T(8,128)}, u32[]{:S(2)}, u32[]{:S(2)}) collective-permute-start(f32[32,128,256]{2,1,0:T(8,128)} %all-gather.4.cloned.1.call-done.own), channel_id=1, source_target_pairs={{0,16},{16,0},{32,48},{48,32},{64,80},{80,64},{96,112},{112,96},{1... | collective-permute-start | bytes 12582920 | tf_op jit(solution)/shard_map/ppermute | solution.py:312
  103.0 6.9 %all-to-all-start.2 = ((f32[16,32,256]{2,1,0:T(8,128)}), f32[16,32,256]{2,1,0:T(8,128)S(1)}, u32[]{:S(2)}, u32[]{:S(2)}) async-start(f32[16,32,256]{2,1,0:T(8,128)} %get-tuple-element.71), calls=%async_computation.2 | async-start | bytes 1048576 | tf_op jit(solution)/shard_map/all_to_all | solution.py:320
  112.3 3.0 %chain_pairs.1 = (bf16[2,16,256,256]{3,2,1,0:T(8,128)(2,1)S(1)}, bf16[2,16,256,256]{3,2,1,0:T(8,128)(2,1)S(1)}) custom-call(f32[32,128,256]{2,1,0:T(8,128)S(1)} %copy-done.2, f32[32,128,256]{2,1,0:T(8,128)} %collective-permute-done.11.other), custom_call_target="tpu_custom_call" | custom-call | tf_op jit(solution)/shard_map/chain_pairs/pallas_call | solution.py:164
  120.8 8.3 %turn.1 = (f32[2,32,256]{2,1,0:T(8,128)}, f32[16,32,256]{2,1,0:T(8,128)}) custom-call(f32[16,32,256]{2,1,0:T(8,128)} %copy-done.14, bf16[2,16,256,256]{3,2,1,0:T(8,128)(2,1)} %copy-done, f32[2,32,256]{2,1,0:T(8,128)} %copy-done.11, f32[2,256,256]{2,1,0:T(8,128)} %get-tuple-element.67.fmat, f32[2,256,256]{2,1,0:T(8,128)} %uinv.3, ...), custom_call_target="tpu_custom_call" | custom-call | tf_op jit(solution)/shard_map/turn/pallas_call | solution.py:296
  129.1 6.2 %all-to-all-start.3 = ((f32[16,32,256]{2,1,0:T(8,128)}), f32[16,32,256]{2,1,0:T(8,128)S(1)}, u32[]{:S(2)}, u32[]{:S(2)}) async-start(f32[16,32,256]{2,1,0:T(8,128)} %get-tuple-element.80), calls=%async_computation.3 | async-start | bytes 1048576 | tf_op jit(solution)/shard_map/all_to_all | solution.py:320
  139.2 3.3 %leaf_ready.1 = (f32[8,256,256]{2,1,0:T(8,128)S(1)}, f32[8,2,256,256]{3,2,1,0:T(8,128)S(1)}) custom-call(f32[8,256,256]{2,1,0:T(8,128)S(1)} %copy-done.7, f32[8,2,256,256]{3,2,1,0:T(8,128)S(1)} %copy-done.1, f32[8,256,256]{2,1,0:T(8,128)S(1)} %copy-done.8), custom_call_target="tpu_custom_call" | custom-call | tf_op jit(solution)/shard_map/leaf_ready/pallas_call | solution.py:224
  146.6 7.2 %leave.1 = (f32[32,256]{1,0:T(8,128)}, f32[16,32,256]{2,1,0:T(8,128)}) custom-call(f32[16,32,256]{2,1,0:T(8,128)} %copy-done.17, bf16[2,16,256,256]{3,2,1,0:T(8,128)(2,1)} %copy-done.3, f32[2,32,256]{2,1,0:T(8,128)} %get-tuple-element.89.vec, f32[2,256,256]{2,1,0:T(8,128)} %get-tuple-element.78.bmat), custom_call_target="tpu_custom_call" | custom-call | tf_op jit(solution)/shard_map/leave/pallas_call | solution.py:296
  153.8 6.6 %all-to-all-start.4 = ((f32[16,32,256]{2,1,0:T(8,128)}), f32[16,32,256]{2,1,0:T(8,128)S(1)}, u32[]{:S(2)}, u32[]{:S(2)}) async-start(f32[16,32,256]{2,1,0:T(8,128)} %get-tuple-element.91), calls=%async_computation.4 | async-start | bytes 1048576 | tf_op jit(solution)/shard_map/all_to_all | solution.py:320
  163.6 3.4 %collective-permute-done.13.third = f32[32,256]{1,0:T(8,128)S(1)} collective-permute-done((f32[32,256]{1,0:T(8,128)}, f32[32,256]{1,0:T(8,128)S(1)}, u32[]{:S(2)}, u32[]{:S(2)}) %collective-permute-start.13) | collective-permute-done | bytes 32800 | tf_op jit(solution)/shard_map/ppermute | solution.py:316
  171.2 28.1 %all_to_all.30 = f32[64,32,256]{2,1,0:T(8,128)S(1)} all-to-all(f32[64,32,256]{2,1,0:T(8,128)S(1)} %bitcast.5), channel_id=1, replica_groups=mesh['layer'=8,'grid'=16] {'grid'}, dimensions={0} | all-to-all | bytes 4194304 | tf_op jit(solution)/shard_map/all_to_all | solution.py:320
  200.8 5.1 %collective-permute-start.15 = (f32[16,4,32,256]{3,2,1,0:T(8,128)S(1)}, f32[16,4,32,256]{3,2,1,0:T(8,128)S(1)}, u32[]{:S(2)}, u32[]{:S(2)}) collective-permute-start(f32[16,4,32,256]{3,2,1,0:T(8,128)S(1)} %bitcast.6), channel_id=1, source_target_pairs={{0,16},{16,0},{32,48},{48,32},{64,80},{80,64},{96,112},{112,96},{1... | collective-permute-start | bytes 6291464 | tf_op jit(solution)/shard_map/ppermute | solution.py:312
  205.8 3.8 %collective-permute-done.15.rest_1_ = f32[16,4,32,256]{3,2,1,0:T(8,128)S(1)} collective-permute-done((f32[16,4,32,256]{3,2,1,0:T(8,128)S(1)}, f32[16,4,32,256]{3,2,1,0:T(8,128)S(1)}, u32[]{:S(2)}, u32[]{:S(2)}) %collective-permute-start.15) | collective-permute-done | bytes 2097184 | tf_op jit(solution)/shard_map/ppermute | solution.py:312
  210.9 10.3 %leaf_back.1 = (f32[8,256,256]{2,1,0:T(8,128)}, f32[2,256,256]{2,1,0:T(8,128)}) custom-call(s32[8,2]{1,0:T(8,128)} %copy.16.targets, f32[8,256,256]{2,1,0:T(8,128)} %copy-done.9, f32[8,2,256,256]{3,2,1,0:T(8,128)} %copy-done.4, f32[16,4,32,256]{3,2,1,0:T(8,128)} %bitcast.7, f32[16,4,32,256]{3,2,1,0:T(8,128)} %copy-done.16, f32[8,16,32,256]{3,2,1,0:T(8,128)} %bitcast.8), custom_call_target="tpu_custom_call" | custom-call | tf_op jit(solution)/shard_map/leaf_back/pallas_call | solution.py:274
  (87 shorter events, 44.4 us)
Async XLA Ops:
  7.2 91.9 %all-gather.4.cloned.1.call-start = ((), (), s32[]{:S(2)}) async-start(), calls=%async_computation.6 | async-start | bytes 4456448 | tf_op jit(solution)/shard_map/all_gather | solution.py:346
  23.6 5.5 %collective-permute-start.7 = (f32[64,32,256]{2,1,0:T(8,128)}, f32[64,32,256]{2,1,0:T(8,128)S(1)}, u32[]{:S(2)}, u32[]{:S(2)}) collective-permute-start(f32[64,32,256]{2,1,0:T(8,128)} %get-tuple-element.59), channel_id=1, source_target_pairs={{0,16},{16,0},{32,48},{48,32},{64,80},{80,64},{96,112},{112,96},{1... | collective-permute-start | bytes 6291464 | tf_op jit(solution)/shard_map/ppermute | solution.py:312
  32.6 43.8 %all-to-all-start = ((f32[64,32,256]{2,1,0:T(8,128)}), f32[64,32,256]{2,1,0:T(8,128)S(1)}, u32[]{:S(2)}, u32[]{:S(2)}) async-start(f32[64,32,256]{2,1,0:T(8,128)} %add.31), calls=%async_computation | async-start | bytes 4194304 | tf_op jit(solution)/shard_map/all_to_all | solution.py:320
  39.6 2.5 %collective-permute-start.1 = (f32[16,32,256]{2,1,0:T(8,128)}, f32[16,32,256]{2,1,0:T(8,128)S(1)}, u32[]{:S(2)}, u32[]{:S(2)}) collective-permute-start(f32[16,32,256]{2,1,0:T(8,128)} %get-tuple-element.53), channel_id=1, source_target_pairs={{0,16},{16,0},{32,48},{48,32},{64,80},{80,64},{96,112},{112,96},{1... | collective-permute-start | bytes 1572872 | tf_op jit(solution)/shard_map/ppermute | solution.py:312
  40.3 3.5 %collective-permute-start.3 = (f32[16,32,256]{2,1,0:T(8,128)}, f32[16,32,256]{2,1,0:T(8,128)S(1)}, u32[]{:S(2)}, u32[]{:S(2)}) collective-permute-start(f32[16,32,256]{2,1,0:T(8,128)} %get-tuple-element.55), channel_id=1, source_target_pairs={{0,16},{16,0},{32,48},{48,32},{64,80},{80,64},{96,112},{112,96},{1... | collective-permute-start | bytes 1572872 | tf_op jit(solution)/shard_map/ppermute | solution.py:312
  40.4 6.9 %collective-permute-start.5 = (f32[16,32,256]{2,1,0:T(8,128)}, f32[16,32,256]{2,1,0:T(8,128)S(1)}, u32[]{:S(2)}, u32[]{:S(2)}) collective-permute-start(f32[16,32,256]{2,1,0:T(8,128)} %get-tuple-element.57), channel_id=1, source_target_pairs={{0,16},{16,0},{32,48},{48,32},{64,80},{80,64},{96,112},{112,96},{1... | collective-permute-start | bytes 1572872 | tf_op jit(solution)/shard_map/ppermute | solution.py:312
  40.8 7.4 %collective-permute-start = (f32[16,32,256]{2,1,0:T(8,128)}, f32[16,32,256]{2,1,0:T(8,128)S(1)}, u32[]{:S(2)}, u32[]{:S(2)}) collective-permute-start(f32[16,32,256]{2,1,0:T(8,128)} %get-tuple-element.51), channel_id=1, source_target_pairs={{0,16},{16,0},{32,48},{48,32},{64,80},{80,64},{96,112},{112,96},{1... | collective-permute-start | bytes 1572872 | tf_op jit(solution)/shard_map/ppermute | solution.py:312
  42.0 28.3 %copy-start.21 = (f32[16,32,256]{2,1,0:T(8,128)S(1)}, f32[16,32,256]{2,1,0:T(8,128)}, u32[]{:S(2)}) copy-start(f32[16,32,256]{2,1,0:T(8,128)} %get-tuple-element.50) | copy-start | bytes 1572868
  42.1 15.9 %collective-permute-start.2 = (f32[16,32,256]{2,1,0:T(8,128)S(1)}, f32[16,32,256]{2,1,0:T(8,128)S(1)}, u32[]{:S(2)}, u32[]{:S(2)}) collective-permute-start(f32[16,32,256]{2,1,0:T(8,128)S(1)} %add.25), channel_id=1, source_target_pairs={{0,32},{16,48},{32,64},{48,80},{64,96},{80,112},{96,0},{112,16},{1... | collective-permute-start | bytes 1572872 | tf_op jit(solution)/shard_map/ppermute | solution.py:316
  43.9 26.1 %collective-permute-start.4 = (f32[16,32,256]{2,1,0:T(8,128)S(1)}, f32[16,32,256]{2,1,0:T(8,128)S(1)}, u32[]{:S(2)}, u32[]{:S(2)}) collective-permute-start(f32[16,32,256]{2,1,0:T(8,128)S(1)} %add.27), channel_id=1, source_target_pairs={{0,64},{16,80},{32,96},{48,112},{64,0},{80,16},{96,32},{112,48},{1... | collective-permute-start | bytes 1572872 | tf_op jit(solution)/shard_map/ppermute | solution.py:316
  47.4 23.0 %collective-permute-start.6 = (f32[16,32,256]{2,1,0:T(8,128)S(1)}, f32[16,32,256]{2,1,0:T(8,128)S(1)}, u32[]{:S(2)}, u32[]{:S(2)}) collective-permute-start(f32[16,32,256]{2,1,0:T(8,128)S(1)} %add.29), channel_id=1, source_target_pairs={{0,96},{16,112},{32,0},{48,16},{64,32},{80,48},{96,64},{112,80},{1... | collective-permute-start | bytes 1572872 | tf_op jit(solution)/shard_map/ppermute | solution.py:316
  76.4 18.6 %all-to-all-start.1 = ((f32[16,32,256]{2,1,0:T(8,128)}), f32[16,32,256]{2,1,0:T(8,128)}, u32[]{:S(2)}, u32[]{:S(2)}) async-start(f32[16,32,256]{2,1,0:T(8,128)} %add_add_fusion), calls=%async_computation.1 | async-start | bytes 1048576 | tf_op jit(solution)/shard_map/all_to_all | solution.py:320
  85.8 6.3 %collective-permute-start.8 = (f32[32,256]{1,0:T(8,128)S(1)}, f32[32,256]{1,0:T(8,128)S(1)}, u32[]{:S(2)}, u32[]{:S(2)}) collective-permute-start(f32[32,256]{1,0:T(8,128)S(1)} %get-tuple-element.63), channel_id=1, source_target_pairs={{0,32},{16,48},{32,64},{48,80},{64,96},{80,112},{96,0},{112,16},{1... | collective-permute-start | bytes 98312 | tf_op jit(solution)/shard_map/ppermute | solution.py:316
  87.8 5.6 %collective-permute-start.9 = (f32[32,256]{1,0:T(8,128)S(1)}, f32[32,256]{1,0:T(8,128)S(1)}, u32[]{:S(2)}, u32[]{:S(2)}) collective-permute-start(f32[32,256]{1,0:T(8,128)S(1)} %get-tuple-element.64), channel_id=1, source_target_pairs={{0,64},{16,80},{32,96},{48,112},{64,0},{80,16},{96,32},{112,48},{1... | collective-permute-start | bytes 98312 | tf_op jit(solution)/shard_map/ppermute | solution.py:316
  91.4 3.2 %collective-permute-start.10 = (f32[32,256]{1,0:T(8,128)S(1)}, f32[32,256]{1,0:T(8,128)S(1)}, u32[]{:S(2)}, u32[]{:S(2)}) collective-permute-start(f32[32,256]{1,0:T(8,128)S(1)} %get-tuple-element.65), channel_id=1, source_target_pairs={{0,96},{16,112},{32,0},{48,16},{64,32},{80,48},{96,64},{112,80},{1... | collective-permute-start | bytes 98312 | tf_op jit(solution)/shard_map/ppermute | solution.py:316
  99.1 11.0 %collective-permute-start.11 = (f32[32,128,256]{2,1,0:T(8,128)}, f32[32,128,256]{2,1,0:T(8,128)}, u32[]{:S(2)}, u32[]{:S(2)}) collective-permute-start(f32[32,128,256]{2,1,0:T(8,128)} %all-gather.4.cloned.1.call-done.own), channel_id=1, source_target_pairs={{0,16},{16,0},{32,48},{48,32},{64,80},{80,64},{96,112},{112,96},{1... | collective-permute-start | bytes 12582920 | tf_op jit(solution)/shard_map/ppermute | solution.py:312
  103.0 17.0 %all-to-all-start.2 = ((f32[16,32,256]{2,1,0:T(8,128)}), f32[16,32,256]{2,1,0:T(8,128)S(1)}, u32[]{:S(2)}, u32[]{:S(2)}) async-start(f32[16,32,256]{2,1,0:T(8,128)} %get-tuple-element.71), calls=%async_computation.2 | async-start | bytes 1048576 | tf_op jit(solution)/shard_map/all_to_all | solution.py:320
  129.1 16.6 %all-to-all-start.3 = ((f32[16,32,256]{2,1,0:T(8,128)}), f32[16,32,256]{2,1,0:T(8,128)S(1)}, u32[]{:S(2)}, u32[]{:S(2)}) async-start(f32[16,32,256]{2,1,0:T(8,128)} %get-tuple-element.80), calls=%async_computation.3 | async-start | bytes 1048576 | tf_op jit(solution)/shard_map/all_to_all | solution.py:320
  153.8 16.6 %all-to-all-start.4 = ((f32[16,32,256]{2,1,0:T(8,128)}), f32[16,32,256]{2,1,0:T(8,128)S(1)}, u32[]{:S(2)}, u32[]{:S(2)}) async-start(f32[16,32,256]{2,1,0:T(8,128)} %get-tuple-element.91), calls=%async_computation.4 | async-start | bytes 1048576 | tf_op jit(solution)/shard_map/all_to_all | solution.py:320
  160.5 49.2 %all-gather.6.cloned.1.call-start = ((), (), s32[]{:S(2)}) async-start(), calls=%async_computation.7 | async-start | bytes 4718592 | tf_op jit(solution)/shard_map/all_gather | solution.py:390
  160.5 3.1 %collective-permute-start.14 = (f32[32,256]{1,0:T(8,128)}, f32[32,256]{1,0:T(8,128)S(1)}, u32[]{:S(2)}, u32[]{:S(2)}) collective-permute-start(f32[32,256]{1,0:T(8,128)} %get-tuple-element.90.first), channel_id=1, source_target_pairs={{0,96},{16,112},{32,0},{48,16},{64,32},{80,48},{96,64},{112,80},{1... | collective-permute-start | bytes 98312 | tf_op jit(solution)/shard_map/ppermute | solution.py:316
  162.3 4.8 %collective-permute-start.13 = (f32[32,256]{1,0:T(8,128)}, f32[32,256]{1,0:T(8,128)S(1)}, u32[]{:S(2)}, u32[]{:S(2)}) collective-permute-start(f32[32,256]{1,0:T(8,128)} %get-tuple-element.90.first), channel_id=1, source_target_pairs={{0,64},{16,80},{32,96},{48,112},{64,0},{80,16},{96,32},{112,48},{1... | collective-permute-start | bytes 98312 | tf_op jit(solution)/shard_map/ppermute | solution.py:316
  162.3 4.8 %collective-permute-start.12 = (f32[32,256]{1,0:T(8,128)}, f32[32,256]{1,0:T(8,128)S(1)}, u32[]{:S(2)}, u32[]{:S(2)}) collective-permute-start(f32[32,256]{1,0:T(8,128)} %get-tuple-element.90.first), channel_id=1, source_target_pairs={{0,32},{16,48},{32,64},{48,80},{64,96},{80,112},{96,0},{112,16},{1... | collective-permute-start | bytes 98312 | tf_op jit(solution)/shard_map/ppermute | solution.py:316
  200.8 8.9 %collective-permute-start.15 = (f32[16,4,32,256]{3,2,1,0:T(8,128)S(1)}, f32[16,4,32,256]{3,2,1,0:T(8,128)S(1)}, u32[]{:S(2)}, u32[]{:S(2)}) collective-permute-start(f32[16,4,32,256]{3,2,1,0:T(8,128)S(1)} %bitcast.6), channel_id=1, source_target_pairs={{0,16},{16,0},{32,48},{48,32},{64,80},{80,64},{96,112},{112,96},{1... | collective-permute-start | bytes 6291464 | tf_op jit(solution)/shard_map/ppermute | solution.py:312
  (22 other events, 115.1 us)
Sparse Core Ops, SparseCore 0:
  11.0 74.6 all-gather.3
  171.3 32.5 all-gather.5

commit v3 on v2

--- a/solution.py
+++ b/solution.py
@@ -33,8 +33,15 @@
     return lax.dot_general(wide, tall, dims, preferred_element_type=jnp.float32)
 
 
+far = pl.BlockSpec(memory_space=pltpu.HBM)
+
+
 def params(mib):
     return pltpu.CompilerParams(vmem_limit_bytes=mib * MIB)
+
+
+def cost(flops):
+    return pl.CostEstimate(flops=flops, bytes_accessed=0, transcendentals=0)
 
 
 def prepare_kernel(linv, lower, uinv, upper, rhs, fmat, bmat, share, rhs_t):
@@ -54,74 +61,89 @@
 
 
 def leaf_forward_kernel(targets, linv, rhs, low, fwd, *rest):
-    outs, (acc, sems) = rest[:10], rest[10:]
-    k = pl.program_id(0)
+    outs, (acc, linv_in, rhs_in, low_in, fwd_out, in_sems, fwd_sems, sems) = rest[:10], rest[10:]
+    leaves = linv.shape[0]
     layer = lax.axis_index("layer")
     core, z = lax.rem(layer, 2), lax.div(layer, 2)
-
-    @pl.when(k == 0)
-    def _():
-        def clear(i, carry):
-            acc[i] = jnp.zeros(acc.shape[1:], jnp.float32)
-            return carry
-
-        lax.fori_loop(0, acc.shape[0], clear, 0, unroll=8)
-
+    reads = [
+        [
+            pltpu.make_async_copy(source.at[k], held.at[k], in_sems.at[i, k])
+            for i, (source, held) in enumerate(((linv, linv_in), (rhs, rhs_in), (low, low_in)))
+        ]
+        for k in range(leaves)
+    ]
+    for group in reads:
+        for copy in group:
+            copy.start()
+
+    def clear(i, carry):
+        acc[i] = jnp.zeros(acc.shape[1:], jnp.float32)
+        return carry
+
+    lax.fori_loop(0, acc.shape[0], clear, 0, unroll=8)
+    writes = []
+    for start in range(0, leaves, 2):
+        pair = range(start, start + 2)
+        for k in pair:
+            for copy in reads[k]:
+                copy.wait()
+        turned = []
+        for k in pair:
+            value = product(split(linv_in[k]), split(rhs_in[k]), NN)
+            fwd_out[k] = value
+            turned.append(split(value.T))
+        for k in pair:
+            for c in range(2):
+                t = targets[k, c]
+                owner, odd = lax.div(t, 2), lax.rem(t, 2)
+                coupled = product(turned[k - start], split(low_in[k, c]), NT)
+                for goal in range(LAYERS):
+                    side = lax.rem(goal % 2 + core, 2)
+                    away = lax.rem(goal // 2 - z + 4, 4)
+                    even_place = (side * 4 + away) * GRID + owner
+                    odd_place = 8 * GRID + (side * GRID + owner) * 4 + away
+                    acc[jnp.where(odd == 0, even_place, odd_place)] += coupled[
+                        goal * COLS : (goal + 1) * COLS
+                    ]
+        for k in pair:
+            writes.append(pltpu.make_async_copy(fwd_out.at[k], fwd.at[k], fwd_sems.at[k]))
+            writes[-1].start()
+    place = 0
+    for i, out in enumerate(outs):
+        size = out.shape[0]
+        writes.append(pltpu.make_async_copy(acc.at[pl.ds(place, size)], out, sems.at[i]))
+        writes[-1].start()
+        place += size
+    for copy in writes:
+        copy.wait()
+
+
+def leaf_forward(targets, linv, rhs, low):
     leaves = linv.shape[0]
-    turned = []
-    for leaf in range(leaves):
-        value = product(split(linv[leaf]), split(rhs[leaf]), NN)
-        fwd[leaf] = value
-        turned.append(split(value.T))
-    for leaf in range(leaves):
-        for c in range(2):
-            t = targets[k * leaves + leaf, c]
-            owner, odd = lax.div(t, 2), lax.rem(t, 2)
-            coupled = product(turned[leaf], split(low[leaf, c]), NT)
-            for goal in range(LAYERS):
-                side = lax.rem(goal % 2 + core, 2)
-                away = lax.rem(goal // 2 - z + 4, 4)
-                even_place = (side * 4 + away) * GRID + owner
-                odd_place = 8 * GRID + (side * GRID + owner) * 4 + away
-                acc[jnp.where(odd == 0, even_place, odd_place)] += coupled[
-                    goal * COLS : (goal + 1) * COLS
-                ]
-
-    @pl.when(k == pl.num_programs(0) - 1)
-    def _():
-        copies, start = [], 0
-        for i, out in enumerate(outs):
-            size = out.shape[0]
-            copies.append(pltpu.make_async_copy(acc.at[pl.ds(start, size)], out, sems.at[i]))
-            start += size
-        for copy in copies:
-            copy.start()
-        for copy in copies:
-            copy.wait()
-
-
-def leaf_forward(targets, linv, rhs, low, step=2):
-    leaves = linv.shape[0]
-    tile = pl.BlockSpec((step, TILE, TILE), lambda k, *_: (k, 0, 0))
-    pair = pl.BlockSpec((step, 2, TILE, TILE), lambda k, *_: (k, 0, 0, 0))
     even = jax.ShapeDtypeStruct((GRID, COLS, TILE), jnp.float32)
     odd = jax.ShapeDtypeStruct((GRID * 4, COLS, TILE), jnp.float32)
     return pl.pallas_call(
         leaf_forward_kernel,
         out_shape=[jax.ShapeDtypeStruct(linv.shape, jnp.float32)] + [even] * 8 + [odd] * 2,
-        grid_spec=pltpu.PrefetchScalarGridSpec(
-            num_scalar_prefetch=1,
-            grid=(leaves // step,),
-            in_specs=[tile, tile, pair],
-            out_specs=[tile] + [pl.BlockSpec(memory_space=pltpu.HBM)] * 10,
-            scratch_shapes=[
-                pltpu.VMEM((16 * GRID, COLS, TILE), jnp.float32),
-                pltpu.SemaphoreType.DMA((10,)),
-            ],
-        ),
-        compiler_params=params(56),
+        in_specs=[pl.BlockSpec(memory_space=pltpu.SMEM)] + [far] * 3,
+        out_specs=[far] * 11,
+        scratch_shapes=[
+            pltpu.VMEM((16 * GRID, COLS, TILE), jnp.float32),
+            pltpu.VMEM(linv.shape, jnp.float32),
+            pltpu.VMEM(rhs.shape, jnp.float32),
+            pltpu.VMEM(low.shape, jnp.float32),
+            pltpu.VMEM(linv.shape, jnp.float32),
+            pltpu.SemaphoreType.DMA((3, leaves)),
+            pltpu.SemaphoreType.DMA((leaves,)),
+            pltpu.SemaphoreType.DMA((10,)),
+        ],
+        compiler_params=params(58),
         name="leaf_forward",
     )(targets, linv, rhs, low)
+
+
+def gathered_kernel(first, second, third, fourth, out):
+    out[...] = (first[...] + second[...]) + (third[...] + fourth[...])
 
 
 def fold_kernel(parts, *outs):
@@ -205,9 +227,10 @@
 
 
 def copies_kernel(first, second, third, fourth, spread):
-    for g in range(GRID):
-        for d, value in enumerate((first, second, third, fourth)):
-            spread[g, d] = value[...]
+    z = lax.div(lax.axis_index("layer"), 2)
+    for d, value in enumerate((first, second, third, fourth)):
+        for g in range(GRID):
+            spread[g, lax.rem(z - d + 4, 4)] = value[...]
 
 
 def leaf_ready_kernel(uinv, up, fwd, base, factor):
@@ -232,67 +255,98 @@
     )(uinv, up, fwd)
 
 
-def leaf_back_kernel(targets, base, factor, *rest):
-    even, odd, (out, own, solved, sems) = rest[:2], rest[2], rest[3:]
-    k = pl.program_id(0)
+def leaf_back_kernel(
+    targets, base, factor, even, even_other, odd, out, own,
+    solved, base_in, factor_in, out_held, own_held, sems, in_sems, out_sems,
+):
     leaves = base.shape[0]
-    layer = lax.axis_index("layer")
-    core, z = lax.rem(layer, 2), lax.div(layer, 2)
-
-    @pl.when(k == 0)
-    def _():
-        copies = []
-        for side in range(2):
-            for d in range(4):
-                place = 2 * lax.rem(z - d + 4, 4) + (core if side == 0 else 1 - core)
-                for i, source in enumerate((even[side].at[:, d], odd.at[place])):
-                    copies.append(
-                        pltpu.make_async_copy(
-                            source, solved.at[i, :, place], sems.at[i, side * 4 + d]
-                        )
-                    )
-        for copy in copies:
+    core = lax.rem(lax.axis_index("layer"), 2)
+
+    def read(slot, t):
+        owner = lax.div(t, 2)
+
+        @pl.when(lax.rem(t, 2) == 1)
+        def _():
+            pltpu.make_async_copy(odd.at[:, :, owner], solved.at[slot], sems.at[slot]).start()
+
+        @pl.when(lax.rem(t, 2) == 0)
+        def _():
+            for source, side in ((even, core), (even_other, 1 - core)):
+                pltpu.make_async_copy(
+                    source.at[owner], solved.at[slot, :, side], sems.at[slot]
+                ).start()
+
+    def ready(slot):
+        pltpu.make_async_copy(odd.at[:, :, 0], solved.at[slot], sems.at[slot]).wait()
+
+    reads = []
+    for k in range(leaves):
+        for c in range(2):
+            read(2 * k + c, targets[k, c])
+        reads.append(
+            [
+                pltpu.make_async_copy(base.at[k], base_in.at[k], in_sems.at[0, k]),
+                pltpu.make_async_copy(factor.at[k], factor_in.at[k], in_sems.at[1, k]),
+            ]
+        )
+        for copy in reads[k]:
             copy.start()
-        for copy in copies:
-            copy.wait()
-        for i in range(2):
-            own[i] = solved[i, lax.axis_index("grid")].reshape(TILE, TILE).T
-
-    for leaf in range(leaves):
-        value = base[leaf]
-        for c in range(2):
-            t = targets[k * leaves + leaf, c]
-            picked = solved[lax.rem(t, 2), lax.div(t, 2)].reshape(TILE, TILE)
-            value = value - product(split(factor[leaf, c]), split(picked), NT)
-        out[leaf] = value
-
-
-def leaf_back(targets, base, factor, even, odd, step=2):
+    for i in range(2):
+        read(2 * leaves + i, 2 * lax.axis_index("grid") + i)
+
+    writes = []
+    for start in range(0, leaves, 2):
+        pair = range(start, start + 2)
+        for k in pair:
+            for copy in reads[k]:
+                copy.wait()
+            for c in range(2):
+                ready(2 * k + c)
+        for k in pair:
+            value = base_in[k]
+            for c in range(2):
+                picked = solved[2 * k + c].reshape(TILE, TILE)
+                value = value - product(split(factor_in[k, c]), split(picked), NT)
+            out_held[k] = value
+        for k in pair:
+            writes.append(pltpu.make_async_copy(out_held.at[k], out.at[k], out_sems.at[k]))
+            writes[-1].start()
+    for i in range(2):
+        ready(2 * leaves + i)
+        own_held[i] = solved[2 * leaves + i].reshape(TILE, TILE).T
+    writes.append(pltpu.make_async_copy(own_held, own, out_sems.at[leaves]))
+    writes[-1].start()
+    for copy in writes:
+        copy.wait()
+
+
+def leaf_back(targets, base, factor, even, odd):
     leaves = base.shape[0]
-    tile = pl.BlockSpec((step, TILE, TILE), lambda k, *_: (k, 0, 0))
-    pair = pl.BlockSpec((step, 2, TILE, TILE), lambda k, *_: (k, 0, 0, 0))
+    two = (2, TILE, TILE)
     return pl.pallas_call(
         leaf_back_kernel,
         out_shape=[
             jax.ShapeDtypeStruct(base.shape, jnp.float32),
-            jax.ShapeDtypeStruct((2, TILE, TILE), jnp.float32),
+            jax.ShapeDtypeStruct(two, jnp.float32),
         ],
-        grid_spec=pltpu.PrefetchScalarGridSpec(
-            num_scalar_prefetch=1,
-            grid=(leaves // step,),
-            in_specs=[tile, pair] + [in_hbm] * 3,
-            out_specs=[tile, pl.BlockSpec((2, TILE, TILE), lambda k, *_: (0, 0, 0))],
-            scratch_shapes=[
-                pltpu.VMEM((2, GRID, LAYERS, COLS, TILE), jnp.float32),
-                pltpu.SemaphoreType.DMA((2, 8)),
-            ],
-        ),
-        compiler_params=params(56),
+        in_specs=[pl.BlockSpec(memory_space=pltpu.SMEM)] + [far] * 2 + [in_hbm] * 2 + [far],
+        out_specs=[far] * 2,
+        scratch_shapes=[
+            pltpu.VMEM((2 * leaves + 2, 4, 2, COLS, TILE), jnp.float32),
+            pltpu.VMEM(base.shape, jnp.float32),
+            pltpu.VMEM(factor.shape, jnp.float32),
+            pltpu.VMEM(base.shape, jnp.float32),
+            pltpu.VMEM(two, jnp.float32),
+            pltpu.SemaphoreType.DMA((2 * leaves + 2,)),
+            pltpu.SemaphoreType.DMA((2, leaves)),
+            pltpu.SemaphoreType.DMA((leaves + 1,)),
+        ],
+        compiler_params=params(58),
         name="leaf_back",
     )(targets, base, factor, *even, odd)
 
 
-def call(kernel, outs, name, *args, scratch=(), mib=10):
+def call(kernel, outs, name, *args, scratch=(), mib=10, hint=1_000_000):
     return pl.pallas_call(
         kernel,
         out_shape=[jax.ShapeDtypeStruct(shape, jnp.float32) for shape in outs],
@@ -300,6 +354,7 @@
         out_specs=[whole] * len(outs),
         scratch_shapes=list(scratch),
         compiler_params=params(mib),
+        cost_estimate=cost(hint),
         name=name,
     )(*args)
 
@@ -348,8 +403,12 @@
     even_keep, even_send, odd_keep, odd_send = parts[:4], parts[4:8], parts[8], parts[9]
     even = [even_keep[d] + other_core(even_send[d]) for d in (1, 2, 3, 0)]
     odd = odd_keep + other_core(odd_send)
-    even = even[3] + along_z(even[0], 1) + along_z(even[1], 2) + along_z(even[2], 3)
+    odd, leaf_uinv = after((odd, leaf_uinv))
     odd = exchange(odd).reshape(GRID, 4, COLS, TILE)
+    base, factor = leaf_ready(leaf_uinv, up_couple, fwd)
+    even = [even[3]] + [along_z(even[d - 1], d) for d in range(1, 4)]
+    [even] = call(gathered_kernel, [spread], "gathered", *even)
+    even, base, factor = after((even, base, factor))
     even, odd = after((even, odd))
     odd = call(fold_kernel, [piece] * 4, "fold", odd)
     odd = [odd[0]] + [along_z(odd[d], d) for d in range(1, 4)]
@@ -369,25 +428,22 @@
         "turn",
         *(values, forward, vec, fmat, tops[2], bmat),
         scratch=states,
-        mib=56,
+        mib=10,
     )
-    sent, leaf_uinv = after((sent, leaf_uinv))
     values = exchange(sent)
-    base, factor = leaf_ready(leaf_uinv, up_couple, fwd)
-    values, base, factor = after((values, base, factor))
     even, sent = call(
         leave_kernel,
         [piece, spread],
         "leave",
         *(values, backward, vec, bmat),
         scratch=states,
-        mib=56,
+        mib=10,
     )
     even = [even] + [along_z(even, d) for d in range(1, 4)]
     [even] = call(copies_kernel, [(GRID, 4, COLS, TILE)], "copies", *even)
     odd = exchange(sent)
     even, odd = after((even, odd))
-    odd = lax.all_gather(odd, "layer", axis=0, tiled=False)
+    odd = lax.all_gather(odd, "layer", axis=0, tiled=False).reshape(4, 2, *spread)
     even = exchange(even.reshape(GRID * 4, COLS, TILE)).reshape(GRID, 4, COLS, TILE)
     even = [even, other_core(even)]
     return tuple(leaf_back(targets, base, factor, even, odd))

time: 229 us -> 213 us (0.930)
  blocking collectives: 28.1 us -> 44.5 us
  starting transfers between devices: 62.5 us -> 49.5 us
  Pallas kernels: 50.5 us -> 39.3 us
  waiting for transfers between devices: 46.6 us -> 42 us
  local copies, waits for them, and re-layouts: 21.5 us -> 17.8 us
    all_to_all x1 -> x2, blocking collectives: 28.1 us -> 44.5 us  [exchange(): lax.all_to_all(value, 'grid', split_axis=0, concat_axis=0, tiled=True)]
    all_to_all x5 -> x4, starting transfers between devices: 36 us -> 24.4 us  [exchange(): lax.all_to_all(value, 'grid', split_axis=0, concat_axis=0, tiled=True)]
    pallas_call x6 -> x7, Pallas kernels: 21.9 us -> 15.7 us  [call(): pl.pallas_call(kernel, out_shape=[jax.ShapeDtypeStruct(shape, jnp.float32...]
    all_to_all x5 -> x4, waiting for transfers between devices: 8.68 us -> 4.61 us  [exchange(): lax.all_to_all(value, 'grid', split_axis=0, concat_axis=0, tiled=True)]
    unnamed x47, local copies, waits for them, and re-layouts: 21.5 us -> 17.8 us
    pallas_call x1, Pallas kernels: 10.3 us -> 7.2 us  [leaf_back(): pl.pallas_call(leaf_back_kernel, out_shape=[jax.ShapeDtypeStruct(base.sha...]
  transfers between devices with their start and end apart: 23 -> 22, of which waited for: 15 -> 13; matrix products, arithmetic and copies ran while one was open for 2% -> 3% of each run, Pallas kernels for 9% -> 9%
where the time goes in v3:
time: 213 us; the launch traced here: 212 us
  starting transfers between devices  49.5 us (23%)
  blocking collectives  44.5 us (21%)
  waiting for transfers between devices  42 us (20%)
  Pallas kernels  39.3 us (18%)
  local copies, waits for them, and re-layouts  17.8 us (8%)
  between operations  14.2 us (7%)
  other arithmetic  4.82 us (2%)
    all_to_all x2, blocking collectives, exchange(): lax.all_to_all(value, 'grid', split_axis=0, concat_axis=0, tiled=True)  44.5 us
    ppermute x9, waiting for transfers between devices, along_z(): lax.ppermute(value, 'layer', [(i, (i + 2 * steps) % LAYERS) for i in rang...  27.9 us
    all_to_all x4, starting transfers between devices, exchange(): lax.all_to_all(value, 'grid', split_axis=0, concat_axis=0, tiled=True)  24.4 us
    unnamed x47, local copies, waits for them, and re-layouts  17.8 us
    pallas_call x7, Pallas kernels, call(): pl.pallas_call(kernel, out_shape=[jax.ShapeDtypeStruct(shape, jnp.float32...  15.7 us
    ppermute x9, starting transfers between devices, along_z(): lax.ppermute(value, 'layer', [(i, (i + 2 * steps) % LAYERS) for i in rang...  13.4 us
    ppermute x7, starting transfers between devices, other_core(): lax.ppermute(value, 'layer', [(i, i + 1 - 2 * (i % 2)) for i in range(LAY...  11.7 us
    pallas_call x1, Pallas kernels, leaf_forward(): pl.pallas_call(leaf_forward_kernel, out_shape=[jax.ShapeDtypeStruct(linv....  10 us
  transfers between devices with their start and end apart: 22, of which 13 were waited for; matrix products, arithmetic and copies ran while one was open for 3% of the time, Pallas kernels for 9%

profile of v3, /device:TPU:1, one launch (start us, length us, event | category | flops | bytes accessed | tf_op | source)
XLA Modules:
  0.0 212.2 jit_solution(11591977216200174281)
XLA Ops:
  7.2 3.7 %prepare.1 = (f32[2,256,256]{2,1,0:T(8,128)}, f32[2,256,256]{2,1,0:T(8,128)}, f32[2,128,256]{2,1,0:T(8,128)}, f32[2,256,256]{2,1,0:T(8,128)}) custom-call(f32[2,256,256]{2,1,0:T(8,128)} %linv.5, f32[2,256,256]{2,1,0:T(8,128)} %lower.1, f32[2,256,256]{2,1,0:T(8,128)} %uinv.4, f32[2,256,256]{2,1,0:T(8,128)} %upper.1, f32[2,256,256]{2,1,0:T(8,128)} %rhs.1), custom_call_target="tpu_custom_call" | custom-call | flops 1000000 | tf_op jit(solution)/shard_map/prepare/pallas_call | solution.py:350
  11.6 10.0 %leaf_forward.1 = (f32[8,256,256]{2,1,0:T(8,128)}, f32[16,32,256]{2,1,0:T(8,128)}, f32[16,32,256]{2,1,0:T(8,128)}, f32[16,32,256]{2,1,0:T(8,128)}, f32[16,32,256...) custom-call(s32[8,2]{1,0:T(8,128)} %copy.16.targets, ...), custom_call_target="tpu_custom_call" | custom-call | tf_op jit(solution)/shard_map/leaf_forward/pallas_call | solution.py:125
  23.2 4.0 %collective-permute-done.7 = f32[64,32,256]{2,1,0:T(8,128)S(1)} collective-permute-done((f32[64,32,256]{2,1,0:T(8,128)}, f32[64,32,256]{2,1,0:T(8,128)S(1)}, u32[]{:S(2)}, u32[]{:S(2)}) %collective-permute-start.7) | collective-permute-done | bytes 2097184 | tf_op jit(solution)/shard_map/ppermute | solution.py:367
  27.2 3.3 %add.19 = f32[64,32,256]{2,1,0:T(8,128)} add(f32[64,32,256]{2,1,0:T(8,128)} %get-tuple-element.58, f32[64,32,256]{2,1,0:T(8,128)S(1)} %collective-permute-done.7) | non-fusion elementwise | flops 524288 | bytes 6291456 | tf_op jit(solution)/shard_map/add | solution.py:405
  30.5 7.0 %all-to-all-start = ((f32[64,32,256]{2,1,0:T(8,128)}), f32[64,32,256]{2,1,0:T(8,128)S(1)}, u32[]{:S(2)}, u32[]{:S(2)}) async-start(f32[64,32,256]{2,1,0:T(8,128)} %add.19), calls=%async_computation | async-start | bytes 4194304 | tf_op jit(solution)/shard_map/all_to_all | solution.py:375
  43.0 3.4 %collective-permute-start.4 = (f32[16,32,256]{2,1,0:T(8,128)S(1)}, f32[16,32,256]{2,1,0:T(8,128)S(1)}, u32[]{:S(2)}, u32[]{:S(2)}) collective-permute-start(f32[16,32,256]{2,1,0:T(8,128)S(1)} %add.17), channel_id=1, source_target_pairs={{0,64},{16,80},{32,96},{48,112},{64,0},{80,16},{96,32},{112,48},{1... | collective-permute-start | bytes 1572872 | tf_op jit(solution)/shard_map/ppermute | solution.py:371
  47.4 9.8 %collective-permute-done.2.second = f32[16,32,256]{2,1,0:T(8,128)S(1)} collective-permute-done((f32[16,32,256]{2,1,0:T(8,128)S(1)}, f32[16,32,256]{2,1,0:T(8,128)S(1)}, u32[]{:S(2)}, u32[]{:S(2)}) %collective-permute-start.2) | collective-permute-done | bytes 524320 | tf_op jit(solution)/shard_map/ppermute | solution.py:371
  57.2 12.0 %collective-permute-done.4.third = f32[16,32,256]{2,1,0:T(8,128)S(1)} collective-permute-done((f32[16,32,256]{2,1,0:T(8,128)S(1)}, f32[16,32,256]{2,1,0:T(8,128)S(1)}, u32[]{:S(2)}, u32[]{:S(2)}) %collective-permute-start.4) | collective-permute-done | bytes 524320 | tf_op jit(solution)/shard_map/ppermute | solution.py:371
  70.1 3.3 %leaf_ready.1 = (f32[8,256,256]{2,1,0:T(8,128)S(1)}, f32[8,2,256,256]{3,2,1,0:T(8,128)S(1)}) custom-call(f32[8,256,256]{2,1,0:T(8,128)S(1)} %copy-done.11, f32[8,2,256,256]{3,2,1,0:T(8,128)S(1)} %copy-done.2, f32[8,256,256]{2,1,0:T(8,128)S(1)} %copy-done.13), custom_call_target="tpu_custom_call" | custom-call | tf_op jit(solution)/shard_map/leaf_ready/pallas_call | solution.py:247
  76.7 7.0 %all-to-all-start.1 = ((f32[16,32,256]{2,1,0:T(8,128)}), f32[16,32,256]{2,1,0:T(8,128)}, u32[]{:S(2)}, u32[]{:S(2)}) async-start(f32[16,32,256]{2,1,0:T(8,128)} %copy-done.10), calls=%async_computation.1 | async-start | bytes 1048576 | tf_op jit(solution)/shard_map/all_to_all | solution.py:375
  85.6 2.4 %collective-permute-start.9 = (f32[32,256]{1,0:T(8,128)S(1)}, f32[32,256]{1,0:T(8,128)S(1)}, u32[]{:S(2)}, u32[]{:S(2)}) collective-permute-start(f32[32,256]{1,0:T(8,128)S(1)} %get-tuple-element.72), channel_id=1, source_target_pairs={{0,64},{16,80},{32,96},{48,112},{64,0},{80,16},{96,32},{112,48},{1... | collective-permute-start | bytes 98312 | tf_op jit(solution)/shard_map/ppermute | solution.py:371
  96.1 4.0 %collective-permute-start.11 = (f32[32,128,256]{2,1,0:T(8,128)}, f32[32,128,256]{2,1,0:T(8,128)}, u32[]{:S(2)}, u32[]{:S(2)}) collective-permute-start(f32[32,128,256]{2,1,0:T(8,128)} %all-gather.4.cloned.1.call-done.own), channel_id=1, source_target_pairs={{0,16},{16,0},{32,48},{48,32},{64,80},{80,64},{96,112},{112,96},{1... | collective-permute-start | bytes 12582920 | tf_op jit(solution)/shard_map/ppermute | solution.py:367
  100.2 6.6 %all-to-all-start.2 = ((f32[16,32,256]{2,1,0:T(8,128)}), f32[16,32,256]{2,1,0:T(8,128)S(1)}, u32[]{:S(2)}, u32[]{:S(2)}) async-start(f32[16,32,256]{2,1,0:T(8,128)} %get-tuple-element.79), calls=%async_computation.2 | async-start | bytes 1048576 | tf_op jit(solution)/shard_map/all_to_all | solution.py:375
  109.5 3.1 %chain_pairs.1 = (bf16[2,16,256,256]{3,2,1,0:T(8,128)(2,1)S(1)}, bf16[2,16,256,256]{3,2,1,0:T(8,128)(2,1)S(1)}) custom-call(f32[32,128,256]{2,1,0:T(8,128)S(1)} %copy-done.3, f32[32,128,256]{2,1,0:T(8,128)} %collective-permute-done.11.other), custom_call_target="tpu_custom_call" | custom-call | tf_op jit(solution)/shard_map/chain_pairs/pallas_call | solution.py:186
  119.2 4.6 %turn.1 = (f32[2,32,256]{2,1,0:T(8,128)S(1)}, f32[16,32,256]{2,1,0:T(8,128)S(1)}) custom-call(f32[16,32,256]{2,1,0:T(8,128)S(1)} %all-to-all-done.2.values, bf16[2,16,256,256]{3,2,1,0:T(8,128)(2,1)S(1)} %copy-done.1, f32[2,32,256]{2,1,0:T(8,128)S(1)} %get-tuple-element.85.vec, f32[2,256,256]{2,1,0:T(8,128)S(1)} %copy-done.9, f32[2,256,256]{2,1,0:T(8,128)S(1)} %copy-done.8, ...), custom_call_target="tpu_custom_call" | custom-call | flops 1000000 | tf_op jit(solution)/shard_map/turn/pallas_call | solution.py:350
  123.7 16.5 %all_to_all.30.values = f32[16,32,256]{2,1,0:T(8,128)S(1)} all-to-all(f32[16,32,256]{2,1,0:T(8,128)S(1)} %get-tuple-element.87), channel_id=1, replica_groups=mesh['layer'=8,'grid'=16] {'grid'}, dimensions={0} | all-to-all | bytes 1048576 | tf_op jit(solution)/shard_map/all_to_all | solution.py:375
  140.3 4.7 %leave.1 = (f32[32,256]{1,0:T(8,128)S(1)}, f32[16,32,256]{2,1,0:T(8,128)}) custom-call(f32[16,32,256]{2,1,0:T(8,128)S(1)} %all_to_all.30.values, bf16[2,16,256,256]{3,2,1,0:T(8,128)(2,1)S(1)} %copy-done.5, f32[2,32,256]{2,1,0:T(8,128)S(1)} %get-tuple-element.89.vec, f32[2,256,256]{2,1,0:T(8,128)S(1)} %copy-done.14), custom_call_target="tpu_custom_call" | custom-call | flops 1000000 | tf_op jit(solution)/shard_map/leave/pallas_call | solution.py:350
  145.0 3.7 %all-to-all-start.4 = ((f32[16,32,256]{2,1,0:T(8,128)}), f32[16,32,256]{2,1,0:T(8,128)S(1)}, u32[]{:S(2)}, u32[]{:S(2)}) async-start(f32[16,32,256]{2,1,0:T(8,128)} %get-tuple-element.91), calls=%async_computation.4 | async-start | bytes 1048576 | tf_op jit(solution)/shard_map/all_to_all | solution.py:375
  151.7 3.3 %collective-permute-done.13.third = f32[32,256]{1,0:T(8,128)S(1)} collective-permute-done((f32[32,256]{1,0:T(8,128)S(1)}, f32[32,256]{1,0:T(8,128)S(1)}, u32[]{:S(2)}, u32[]{:S(2)}) %collective-permute-start.13) | collective-permute-done | bytes 32800 | tf_op jit(solution)/shard_map/ppermute | solution.py:371
  155.1 2.8 %all-to-all-done.4 = f32[16,32,256]{2,1,0:T(8,128)S(1)} async-done(((f32[16,32,256]{2,1,0:T(8,128)}), f32[16,32,256]{2,1,0:T(8,128)S(1)}, u32[]{:S(2)}, u32[]{:S(2)}) %all-to-all-start.4) | async-done | bytes 524320 | tf_op jit(solution)/shard_map/all_to_all | solution.py:375
  158.8 28.0 %all_to_all.31 = f32[64,32,256]{2,1,0:T(8,128)S(1)} all-to-all(f32[64,32,256]{2,1,0:T(8,128)S(1)} %bitcast.5), channel_id=1, replica_groups=mesh['layer'=8,'grid'=16] {'grid'}, dimensions={0} | all-to-all | bytes 4194304 | tf_op jit(solution)/shard_map/all_to_all | solution.py:375
  188.1 4.8 %collective-permute-start.15 = (f32[16,4,32,256]{3,2,1,0:T(8,128)S(1)}, f32[16,4,32,256]{3,2,1,0:T(8,128)S(1)}, u32[]{:S(2)}, u32[]{:S(2)}) collective-permute-start(f32[16,4,32,256]{3,2,1,0:T(8,128)S(1)} %bitcast.6), channel_id=1, source_target_pairs={{0,16},{16,0},{32,48},{48,32},{64,80},{80,64},{96,112},{112,96},{1... | collective-permute-start | bytes 6291464 | tf_op jit(solution)/shard_map/ppermute | solution.py:367
  192.9 3.8 %collective-permute-done.15.even_other = f32[16,4,32,256]{3,2,1,0:T(8,128)S(1)} collective-permute-done((f32[16,4,32,256]{3,2,1,0:T(8,128)S(1)}, f32[16,4,32,256]{3,2,1,0:T(8,128)S(1)}, u32[]{:S(2)}, u32[]{:S(2)}) %collective-permute-start.15) | collective-permute-done | bytes 2097184 | tf_op jit(solution)/shard_map/ppermute | solution.py:367
  198.1 7.2 %leaf_back.1 = (f32[8,256,256]{2,1,0:T(8,128)}, f32[2,256,256]{2,1,0:T(8,128)}) custom-call(s32[8,2]{1,0:T(8,128)} %copy.16.targets, f32[8,256,256]{2,1,0:T(8,128)} %copy-done.12, f32[8,2,256,256]{3,2,1,0:T(8,128)} %copy-done.6, f32[16,4,32,256]{3,2,1,0:T(8,128)} %bitcast.7, f32[16,4,32,256]{3,2,1,0:T(8,128)} %copy-done.18, f32[4,2,16,32,256]{4,3,2,1,0:T(8,128)} %bitcast.8), custom_call_target="tpu_custom_call" | custom-call | tf_op jit(solution)/shard_map/leaf_back/pallas_call | solution.py:326
  (87 shorter events, 38.8 us)
Async XLA Ops:
  7.2 89.0 %all-gather.4.cloned.1.call-start = ((), (), s32[]{:S(2)}) async-start(), calls=%async_computation.6 | async-start | bytes 4456448 | tf_op jit(solution)/shard_map/all_gather | solution.py:401
  21.7 5.5 %collective-permute-start.7 = (f32[64,32,256]{2,1,0:T(8,128)}, f32[64,32,256]{2,1,0:T(8,128)S(1)}, u32[]{:S(2)}, u32[]{:S(2)}) collective-permute-start(f32[64,32,256]{2,1,0:T(8,128)} %get-tuple-element.59), channel_id=1, source_target_pairs={{0,16},{16,0},{32,48},{48,32},{64,80},{80,64},{96,112},{112,96},{1... | collective-permute-start | bytes 6291464 | tf_op jit(solution)/shard_map/ppermute | solution.py:367
  30.5 46.2 %all-to-all-start = ((f32[64,32,256]{2,1,0:T(8,128)}), f32[64,32,256]{2,1,0:T(8,128)S(1)}, u32[]{:S(2)}, u32[]{:S(2)}) async-start(f32[64,32,256]{2,1,0:T(8,128)} %add.19), calls=%async_computation | async-start | bytes 4194304 | tf_op jit(solution)/shard_map/all_to_all | solution.py:375
  37.5 2.4 %collective-permute-start.1 = (f32[16,32,256]{2,1,0:T(8,128)}, f32[16,32,256]{2,1,0:T(8,128)S(1)}, u32[]{:S(2)}, u32[]{:S(2)}) collective-permute-start(f32[16,32,256]{2,1,0:T(8,128)} %get-tuple-element.53), channel_id=1, source_target_pairs={{0,16},{16,0},{32,48},{48,32},{64,80},{80,64},{96,112},{112,96},{1... | collective-permute-start | bytes 1572872 | tf_op jit(solution)/shard_map/ppermute | solution.py:367
  38.2 4.8 %collective-permute-start.3 = (f32[16,32,256]{2,1,0:T(8,128)}, f32[16,32,256]{2,1,0:T(8,128)S(1)}, u32[]{:S(2)}, u32[]{:S(2)}) collective-permute-start(f32[16,32,256]{2,1,0:T(8,128)} %get-tuple-element.55), channel_id=1, source_target_pairs={{0,16},{16,0},{32,48},{48,32},{64,80},{80,64},{96,112},{112,96},{1... | collective-permute-start | bytes 1572872 | tf_op jit(solution)/shard_map/ppermute | solution.py:367
  38.3 8.1 %collective-permute-start.5 = (f32[16,32,256]{2,1,0:T(8,128)}, f32[16,32,256]{2,1,0:T(8,128)S(1)}, u32[]{:S(2)}, u32[]{:S(2)}) collective-permute-start(f32[16,32,256]{2,1,0:T(8,128)} %get-tuple-element.57), channel_id=1, source_target_pairs={{0,16},{16,0},{32,48},{48,32},{64,80},{80,64},{96,112},{112,96},{1... | collective-permute-start | bytes 1572872 | tf_op jit(solution)/shard_map/ppermute | solution.py:367
  38.7 8.6 %collective-permute-start = (f32[16,32,256]{2,1,0:T(8,128)}, f32[16,32,256]{2,1,0:T(8,128)S(1)}, u32[]{:S(2)}, u32[]{:S(2)}) collective-permute-start(f32[16,32,256]{2,1,0:T(8,128)} %get-tuple-element.51), channel_id=1, source_target_pairs={{0,16},{16,0},{32,48},{48,32},{64,80},{80,64},{96,112},{112,96},{1... | collective-permute-start | bytes 1572872 | tf_op jit(solution)/shard_map/ppermute | solution.py:367
  40.0 30.1 %copy-start.13 = (f32[8,256,256]{2,1,0:T(8,128)S(1)}, f32[8,256,256]{2,1,0:T(8,128)}, u32[]{:S(2)}) copy-start(f32[8,256,256]{2,1,0:T(8,128)} %get-tuple-element.61.fwd) | copy-start | bytes 6291460
  41.2 16.0 %collective-permute-start.2 = (f32[16,32,256]{2,1,0:T(8,128)S(1)}, f32[16,32,256]{2,1,0:T(8,128)S(1)}, u32[]{:S(2)}, u32[]{:S(2)}) collective-permute-start(f32[16,32,256]{2,1,0:T(8,128)S(1)} %add.16), channel_id=1, source_target_pairs={{0,32},{16,48},{32,64},{48,80},{64,96},{80,112},{96,0},{112,16},{1... | collective-permute-start | bytes 1572872 | tf_op jit(solution)/shard_map/ppermute | solution.py:371
  43.0 27.1 %copy-start.11 = (f32[8,256,256]{2,1,0:T(8,128)S(1)}, f32[8,256,256]{2,1,0:T(8,128)}, u32[]{:S(2)}) copy-start(f32[8,256,256]{2,1,0:T(8,128)} %uinv.3) | copy-start | bytes 6291460
  43.0 26.1 %collective-permute-start.4 = (f32[16,32,256]{2,1,0:T(8,128)S(1)}, f32[16,32,256]{2,1,0:T(8,128)S(1)}, u32[]{:S(2)}, u32[]{:S(2)}) collective-permute-start(f32[16,32,256]{2,1,0:T(8,128)S(1)} %add.17), channel_id=1, source_target_pairs={{0,64},{16,80},{32,96},{48,112},{64,0},{80,16},{96,32},{112,48},{1... | collective-permute-start | bytes 1572872 | tf_op jit(solution)/shard_map/ppermute | solution.py:371
  46.5 22.7 %collective-permute-start.6 = (f32[16,32,256]{2,1,0:T(8,128)S(1)}, f32[16,32,256]{2,1,0:T(8,128)S(1)}, u32[]{:S(2)}, u32[]{:S(2)}) collective-permute-start(f32[16,32,256]{2,1,0:T(8,128)S(1)} %add.18), channel_id=1, source_target_pairs={{0,96},{16,112},{32,0},{48,16},{64,32},{80,48},{96,64},{112,80},{1... | collective-permute-start | bytes 1572872 | tf_op jit(solution)/shard_map/ppermute | solution.py:371
  76.7 16.1 %all-to-all-start.1 = ((f32[16,32,256]{2,1,0:T(8,128)}), f32[16,32,256]{2,1,0:T(8,128)}, u32[]{:S(2)}, u32[]{:S(2)}) async-start(f32[16,32,256]{2,1,0:T(8,128)} %copy-done.10), calls=%async_computation.1 | async-start | bytes 1048576 | tf_op jit(solution)/shard_map/all_to_all | solution.py:375
  83.8 4.9 %collective-permute-start.8 = (f32[32,256]{1,0:T(8,128)S(1)}, f32[32,256]{1,0:T(8,128)S(1)}, u32[]{:S(2)}, u32[]{:S(2)}) collective-permute-start(f32[32,256]{1,0:T(8,128)S(1)} %get-tuple-element.71), channel_id=1, source_target_pairs={{0,32},{16,48},{32,64},{48,80},{64,96},{80,112},{96,0},{112,16},{1... | collective-permute-start | bytes 98312 | tf_op jit(solution)/shard_map/ppermute | solution.py:371
  85.6 4.3 %collective-permute-start.9 = (f32[32,256]{1,0:T(8,128)S(1)}, f32[32,256]{1,0:T(8,128)S(1)}, u32[]{:S(2)}, u32[]{:S(2)}) collective-permute-start(f32[32,256]{1,0:T(8,128)S(1)} %get-tuple-element.72), channel_id=1, source_target_pairs={{0,64},{16,80},{32,96},{48,112},{64,0},{80,16},{96,32},{112,48},{1... | collective-permute-start | bytes 98312 | tf_op jit(solution)/shard_map/ppermute | solution.py:371
  88.0 3.2 %collective-permute-start.10 = (f32[32,256]{1,0:T(8,128)S(1)}, f32[32,256]{1,0:T(8,128)S(1)}, u32[]{:S(2)}, u32[]{:S(2)}) collective-permute-start(f32[32,256]{1,0:T(8,128)S(1)} %get-tuple-element.73), channel_id=1, source_target_pairs={{0,96},{16,112},{32,0},{48,16},{64,32},{80,48},{96,64},{112,80},{1... | collective-permute-start | bytes 98312 | tf_op jit(solution)/shard_map/ppermute | solution.py:371
  96.1 11.2 %collective-permute-start.11 = (f32[32,128,256]{2,1,0:T(8,128)}, f32[32,128,256]{2,1,0:T(8,128)}, u32[]{:S(2)}, u32[]{:S(2)}) collective-permute-start(f32[32,128,256]{2,1,0:T(8,128)} %all-gather.4.cloned.1.call-done.own), channel_id=1, source_target_pairs={{0,16},{16,0},{32,48},{48,32},{64,80},{80,64},{96,112},{112,96},{1... | collective-permute-start | bytes 12582920 | tf_op jit(solution)/shard_map/ppermute | solution.py:367
  100.2 16.8 %all-to-all-start.2 = ((f32[16,32,256]{2,1,0:T(8,128)}), f32[16,32,256]{2,1,0:T(8,128)S(1)}, u32[]{:S(2)}, u32[]{:S(2)}) async-start(f32[16,32,256]{2,1,0:T(8,128)} %get-tuple-element.79), calls=%async_computation.2 | async-start | bytes 1048576 | tf_op jit(solution)/shard_map/all_to_all | solution.py:375
  145.0 13.0 %all-to-all-start.4 = ((f32[16,32,256]{2,1,0:T(8,128)}), f32[16,32,256]{2,1,0:T(8,128)S(1)}, u32[]{:S(2)}, u32[]{:S(2)}) async-start(f32[16,32,256]{2,1,0:T(8,128)} %get-tuple-element.91), calls=%async_computation.4 | async-start | bytes 1048576 | tf_op jit(solution)/shard_map/all_to_all | solution.py:375
  148.7 48.0 %all-gather.6.cloned.1.call-start = ((), (), s32[]{:S(2)}) async-start(), calls=%async_computation.7 | async-start | bytes 4718592 | tf_op jit(solution)/shard_map/all_gather | solution.py:446
  148.8 2.9 %collective-permute-start.14 = (f32[32,256]{1,0:T(8,128)S(1)}, f32[32,256]{1,0:T(8,128)S(1)}, u32[]{:S(2)}, u32[]{:S(2)}) collective-permute-start(f32[32,256]{1,0:T(8,128)S(1)} %get-tuple-element.90.first), channel_id=1, source_target_pairs={{0,96},{16,112},{32,0},{48,16},{64,32},{80,48},{96,64},{112,80},{1... | collective-permute-start | bytes 98312 | tf_op jit(solution)/shard_map/ppermute | solution.py:371
  150.6 4.3 %collective-permute-start.13 = (f32[32,256]{1,0:T(8,128)S(1)}, f32[32,256]{1,0:T(8,128)S(1)}, u32[]{:S(2)}, u32[]{:S(2)}) collective-permute-start(f32[32,256]{1,0:T(8,128)S(1)} %get-tuple-element.90.first), channel_id=1, source_target_pairs={{0,64},{16,80},{32,96},{48,112},{64,0},{80,16},{96,32},{112,48},{1... | collective-permute-start | bytes 98312 | tf_op jit(solution)/shard_map/ppermute | solution.py:371
  150.6 4.3 %collective-permute-start.12 = (f32[32,256]{1,0:T(8,128)S(1)}, f32[32,256]{1,0:T(8,128)S(1)}, u32[]{:S(2)}, u32[]{:S(2)}) collective-permute-start(f32[32,256]{1,0:T(8,128)S(1)} %get-tuple-element.90.first), channel_id=1, source_target_pairs={{0,32},{16,48},{32,64},{48,80},{64,96},{80,112},{96,0},{112,16},{1... | collective-permute-start | bytes 98312 | tf_op jit(solution)/shard_map/ppermute | solution.py:371
  188.1 8.6 %collective-permute-start.15 = (f32[16,4,32,256]{3,2,1,0:T(8,128)S(1)}, f32[16,4,32,256]{3,2,1,0:T(8,128)S(1)}, u32[]{:S(2)}, u32[]{:S(2)}) collective-permute-start(f32[16,4,32,256]{3,2,1,0:T(8,128)S(1)} %bitcast.6), channel_id=1, source_target_pairs={{0,16},{16,0},{32,48},{48,32},{64,80},{80,64},{96,112},{112,96},{1... | collective-permute-start | bytes 6291464 | tf_op jit(solution)/shard_map/ppermute | solution.py:367
  (21 other events, 147.6 us)
Sparse Core Ops, SparseCore 0:
  11.1 72.0 all-gather.3
  158.9 33.0 all-gather.5

commit v4 on v3

--- a/solution.py
+++ b/solution.py
@@ -1,3 +1,5 @@
+import functools
+
 import jax
 import jax.numpy as jnp
 from jax import lax
@@ -10,6 +12,9 @@
 TILE = 256
 COLS = TILE // LAYERS
 TOPS = 32
+SIDE = 4
+ROW_GROUPS = [[SIDE * x + y for y in range(SIDE)] for x in range(SIDE)]
+COLUMN_GROUPS = [[SIDE * x + y for x in range(SIDE)] for y in range(SIDE)]
 MIB = 1024 * 1024
 HALF = TILE // 2
 
@@ -165,42 +170,62 @@
     vec[0] = first
     vec[1] = second
     last = second + product(split(first), split(fmat[1]), NT)
-    for g in range(GRID):
-        spread[g] = last
-
-
-def chain_kernel(own, other, forward, backward):
+    for i in range(SIDE):
+        spread[i] = last
+
+
+def halves():
     core = lax.rem(lax.axis_index("layer"), 2)
-    for i, source in enumerate((own, other)):
-        side = core if i == 0 else 1 - core
-        rows = pl.ds(pl.multiple_of(side * HALF, HALF), HALF)
-        for h in range(1, GRID - 1):
-            for which, out in enumerate((forward, backward)):
-                high, low = split(source[2 * h + which])
-                out[0, h, rows] = high
-                out[1, h, rows] = low
-
-
-def chain_pairs(own, other):
-    pairs = jax.ShapeDtypeStruct((2, GRID, TILE, TILE), jnp.bfloat16)
-    return pl.pallas_call(
-        chain_kernel,
-        out_shape=[pairs, pairs],
-        in_specs=[whole] * 2,
-        out_specs=[whole] * 2,
-        compiler_params=params(20),
-        name="chain_pairs",
-    )(own, other)
-
-
-def turn_kernel(values, chain, vec, fmat, uinv, bmat, out, spread, states):
-    states[0] = jnp.zeros(states.shape[1:], jnp.float32)
-    states[1] = values[0]
-    carried = values[0]
-    for h in range(1, GRID - 1):
-        carried = values[h] + product(split(carried), (chain[0, h], chain[1, h]), NT)
-        states[h + 1] = carried
-    incoming = states[lax.axis_index("grid")]
+    return [pl.ds(pl.multiple_of(side * HALF, HALF), HALF) for side in (core, 1 - core)]
+
+
+def group_kernel(*refs):
+    pieces, (forward, backward, share) = refs[: 2 * SIDE], refs[2 * SIDE :]
+    y = lax.rem(lax.axis_index("grid"), SIDE)
+    mine, theirs = halves()
+    for which, out in enumerate((forward, backward)):
+        for step in range(SIDE):
+            place = lax.rem(y - step + SIDE, SIDE)
+            out[place, mine] = pieces[step][which]
+            out[place, theirs] = pieces[SIDE + step][which]
+    for which, out, order in ((0, forward, (3, 2, 1, 0)), (1, backward, (0, 1, 2, 3))):
+        made = out[order[0], mine]
+        for i in order[1:]:
+            made = product(split(made), split(out[i]), NN)
+        share[which] = made
+
+
+def total_kernel(order, values, steps, spread):
+    carried = values[order[0]]
+    for i in order[1:]:
+        carried = values[i] + product(split(carried), split(steps[i]), NT)
+    for i in range(SIDE):
+        spread[i] = carried
+
+
+def arriving(which, across, values, steps, own, other, states, held):
+    mine, theirs = halves()
+    for i in (1, 2):
+        held[i, mine] = own[i, which]
+        held[i, theirs] = other[i, which]
+    x = lax.div(lax.axis_index("grid"), SIDE)
+    y = lax.rem(lax.axis_index("grid"), SIDE)
+    order, step = (list(range(SIDE)), 1) if which == 0 else (list(range(SIDE))[::-1], -1)
+    carried = jnp.zeros(states.shape[1:], jnp.float32)
+    states[order[0]] = carried
+    for i in order[:-1]:
+        carried = across[i] if i == order[0] else across[i] + product(split(carried), split(held[i]), NT)
+        states[i + step] = carried
+    carried = states[x]
+    states[SIDE + order[0]] = carried
+    for i in order[:-1]:
+        carried = values[i] + product(split(carried), split(steps[i]), NT)
+        states[SIDE + i + step] = carried
+    return states[SIDE + y]
+
+
+def turn_kernel(across, values, steps, own, other, vec, fmat, uinv, bmat, out, spread, states, held):
+    incoming = arriving(0, across, values, steps, own, other, states, held)
     first = vec[0] + product(split(incoming), split(fmat[0]), NT)
     second = vec[1] + product(split(first), split(fmat[1]), NT)
     upper_second = product(split(second), split(uinv[1]), NT)
@@ -208,18 +233,12 @@
     out[0] = upper_first
     out[1] = upper_second
     last = upper_first + product(split(upper_second), split(bmat[0]), NT)
-    for g in range(GRID):
-        spread[g] = last
-
-
-def leave_kernel(values, chain, vec, bmat, even, spread, states):
-    states[GRID - 1] = jnp.zeros(states.shape[1:], jnp.float32)
-    states[GRID - 2] = values[GRID - 1]
-    carried = values[GRID - 1]
-    for h in range(GRID - 2, 0, -1):
-        carried = values[h] + product(split(carried), (chain[0, h], chain[1, h]), NT)
-        states[h - 1] = carried
-    incoming = states[lax.axis_index("grid")]
+    for i in range(SIDE):
+        spread[i] = last
+
+
+def leave_kernel(across, values, steps, own, other, vec, bmat, even, spread, states, held):
+    incoming = arriving(1, across, values, steps, own, other, states, held)
     second = vec[1] + product(split(incoming), split(bmat[1]), NT)
     even[...] = vec[0] + product(split(second), split(bmat[0]), NT)
     for g in range(GRID):
@@ -371,6 +390,19 @@
     return lax.ppermute(value, "layer", [(i, (i + 2 * steps) % LAYERS) for i in range(LAYERS)])
 
 
+def along_y(value, steps):
+    pairs = [
+        (SIDE * x + y, SIDE * x + (y + steps) % SIDE) for x in range(SIDE) for y in range(SIDE)
+    ]
+    return lax.ppermute(value, "grid", pairs)
+
+
+def within(value, groups):
+    return lax.all_to_all(
+        value, "grid", split_axis=0, concat_axis=0, axis_index_groups=groups, tiled=True
+    )
+
+
 def exchange(value):
     return lax.all_to_all(value, "grid", split_axis=0, concat_axis=0, tiled=True)
 
@@ -390,7 +422,7 @@
 ):
     two = (2, TILE, TILE)
     slim = (2, COLS, TILE)
-    piece = (COLS, TILE)
+    slip = (COLS, TILE)
     spread = (GRID, COLS, TILE)
 
     tops = (top_linv, top_lower, top_uinv, top_upper, top_rhs)
@@ -398,53 +430,62 @@
         prepare_kernel, [two, two, (2, HALF, TILE), two], "prepare", *tops, mib=56
     )
     share, leaf_rhs = after((share, leaf_rhs))
-    chain = lax.all_gather(share, "grid", axis=0, tiled=True)
+    rows = [share] + [along_y(share, step) for step in range(1, SIDE)]
     fwd, *parts = leaf_forward(targets, leaf_linv, leaf_rhs, low_couple)
     even_keep, even_send, odd_keep, odd_send = parts[:4], parts[4:8], parts[8], parts[9]
+    odd = exchange(odd_keep + other_core(odd_send)).reshape(GRID, 4, COLS, TILE)
     even = [even_keep[d] + other_core(even_send[d]) for d in (1, 2, 3, 0)]
-    odd = odd_keep + other_core(odd_send)
-    odd, leaf_uinv = after((odd, leaf_uinv))
-    odd = exchange(odd).reshape(GRID, 4, COLS, TILE)
-    base, factor = leaf_ready(leaf_uinv, up_couple, fwd)
+    rows = rows + [other_core(piece) for piece in rows]
     even = [even[3]] + [along_z(even[d - 1], d) for d in range(1, 4)]
     [even] = call(gathered_kernel, [spread], "gathered", *even)
-    even, base, factor = after((even, base, factor))
     even, odd = after((even, odd))
-    odd = call(fold_kernel, [piece] * 4, "fold", odd)
+    odd = call(fold_kernel, [slip] * 4, "fold", odd)
+    odd, rows = after((odd, rows))
+    four = (SIDE, TILE, TILE)
+    forward, backward, share = call(
+        group_kernel, [four, four, (2, HALF, TILE)], "group", *rows
+    )
+    columns = lax.all_gather(share, "grid", axis=0, axis_index_groups=COLUMN_GROUPS)
     odd = [odd[0]] + [along_z(odd[d], d) for d in range(1, 4)]
     even = exchange(even)
 
-    vec, sent = call(
-        enter_kernel, [slim, spread], "enter", even, *odd, rhs_t, tops[0], fmat
-    )
-    vec, sent, chain = after((vec, sent, chain))
-    forward, backward = chain_pairs(chain, other_core(chain))
-    values = exchange(sent)
-    values, forward, backward = after((values, forward, backward))
-    states = [pltpu.VMEM(spread, jnp.float32)]
+    small = (SIDE, COLS, TILE)
+    vec, sent = call(enter_kernel, [slim, small], "enter", even, *odd, rhs_t, tops[0], fmat)
+    values = within(sent, ROW_GROUPS)
+    states = [
+        pltpu.VMEM((2 * SIDE, COLS, TILE), jnp.float32),
+        pltpu.VMEM(four, jnp.float32),
+    ]
+    up_order, down_order = list(range(SIDE)), list(range(SIDE))[::-1]
+    [sent] = call(functools.partial(total_kernel, up_order), [small], "total", values, forward)
+    sent, columns = after((sent, columns))
+    columns = (columns, other_core(columns))
+    across = within(sent, COLUMN_GROUPS)
     vec, sent = call(
         turn_kernel,
-        [slim, spread],
+        [slim, small],
         "turn",
-        *(values, forward, vec, fmat, tops[2], bmat),
+        *(across, values, forward, *columns, vec, fmat, tops[2], bmat),
         scratch=states,
-        mib=10,
     )
-    values = exchange(sent)
+    values = within(sent, ROW_GROUPS)
+    [sent] = call(functools.partial(total_kernel, down_order), [small], "total", values, backward)
+    across = within(sent, COLUMN_GROUPS)
     even, sent = call(
         leave_kernel,
-        [piece, spread],
+        [slip, spread],
         "leave",
-        *(values, backward, vec, bmat),
+        *(across, values, backward, *columns, vec, bmat),
         scratch=states,
-        mib=10,
     )
     even = [even] + [along_z(even, d) for d in range(1, 4)]
     [even] = call(copies_kernel, [(GRID, 4, COLS, TILE)], "copies", *even)
     odd = exchange(sent)
-    even, odd = after((even, odd))
+    even, odd, leaf_uinv = after((even, odd, leaf_uinv))
+    base, factor = leaf_ready(leaf_uinv, up_couple, fwd)
     odd = lax.all_gather(odd, "layer", axis=0, tiled=False).reshape(4, 2, *spread)
     even = exchange(even.reshape(GRID * 4, COLS, TILE)).reshape(GRID, 4, COLS, TILE)
+    even, base, factor = after((even, base, factor))
     even = [even, other_core(even)]
     return tuple(leaf_back(targets, base, factor, even, odd))
 

time: 213 us -> 223 us (1.047)
  starting transfers between devices: 49.5 us -> 66.8 us
  blocking collectives: 44.5 us -> 29.8 us
  waiting for transfers between devices: 42 us -> 52.7 us
  local copies, waits for them, and re-layouts: 17.8 us -> 15 us
    ppermute x0 -> x3, waiting for transfers between devices: none -> 22.5 us  [along_y(): return lax.ppermute(value, 'grid', pairs)]
    ppermute x9, waiting for transfers between devices: 27.9 us -> 6.31 us  [along_z(): lax.ppermute(value, 'layer', [(i, (i + 2 * steps) % LAYERS) for i in rang...]
    all_to_all x2 -> x4, blocking collectives: 44.5 us -> 29.8 us  [within(): lax.all_to_all(value, 'grid', split_axis=0, concat_axis=0, axis_index_gro...]
    all_to_all x4, waiting for transfers between devices: 4.61 us -> 15 us  [exchange(): lax.all_to_all(value, 'grid', split_axis=0, concat_axis=0, tiled=True)]
    ppermute x0 -> x3, starting transfers between devices: none -> 7.17 us  [along_y(): return lax.ppermute(value, 'grid', pairs)]
    ppermute x9, starting transfers between devices: 13.4 us -> 20.2 us  [along_z(): lax.ppermute(value, 'layer', [(i, (i + 2 * steps) % LAYERS) for i in rang...]
    ppermute x7 -> x11, starting transfers between devices: 11.7 us -> 16.5 us  [other_core(): lax.ppermute(value, 'layer', [(i, i + 1 - 2 * (i % 2)) for i in range(LAY...]
    pallas_call x1 -> x0, Pallas kernels: 3.11 us -> none  [chain_pairs(): pl.pallas_call(chain_kernel, out_shape=[pairs, pairs], in_specs=[whole] *...]
  transfers between devices with their start and end apart: 22 -> 29, of which waited for: 13 -> 12; matrix products, arithmetic and copies ran while one was open for 3% -> 1% of each run, Pallas kernels for 9% -> 4%
where the time goes in v4:
time: 223 us; the launch traced here: 222 us
  starting transfers between devices  66.8 us (30%)
  waiting for transfers between devices  52.7 us (24%)
  Pallas kernels  37.5 us (17%)
  blocking collectives  29.8 us (13%)
  local copies, waits for them, and re-layouts  15 us (7%)
  between operations  14.3 us (6%)
  other arithmetic  5.8 us (3%)
    all_to_all x4, blocking collectives, within(): lax.all_to_all(value, 'grid', split_axis=0, concat_axis=0, axis_index_gro...  29.8 us
    all_to_all x4, starting transfers between devices, exchange(): lax.all_to_all(value, 'grid', split_axis=0, concat_axis=0, tiled=True)  22.9 us
    ppermute x3, waiting for transfers between devices, along_y(): return lax.ppermute(value, 'grid', pairs)  22.5 us
    ppermute x9, starting transfers between devices, along_z(): lax.ppermute(value, 'layer', [(i, (i + 2 * steps) % LAYERS) for i in rang...  20.2 us
    pallas_call x10, Pallas kernels, call(): pl.pallas_call(kernel, out_shape=[jax.ShapeDtypeStruct(shape, jnp.float32...  17 us
    ppermute x11, starting transfers between devices, other_core(): lax.ppermute(value, 'layer', [(i, i + 1 - 2 * (i % 2)) for i in range(LAY...  16.5 us
    unnamed x39, local copies, waits for them, and re-layouts  15 us
    all_to_all x4, waiting for transfers between devices, exchange(): lax.all_to_all(value, 'grid', split_axis=0, concat_axis=0, tiled=True)  15 us
  transfers between devices with their start and end apart: 29, of which 12 were waited for; matrix products, arithmetic and copies ran while one was open for 1% of the time, Pallas kernels for 4%

profile of v4, /device:TPU:1, one launch (start us, length us, event | category | flops | bytes accessed | tf_op | source)
XLA Modules:
  0.0 222.0 jit_solution(17597916465182469624)
XLA Ops:
  8.5 3.7 %prepare.1 = (f32[2,256,256]{2,1,0:T(8,128)}, f32[2,256,256]{2,1,0:T(8,128)}, f32[2,128,256]{2,1,0:T(8,128)}, f32[2,256,256]{2,1,0:T(8,128)}) custom-call(f32[2,256,256]{2,1,0:T(8,128)} %linv.5, f32[2,256,256]{2,1,0:T(8,128)} %lower.1, f32[2,256,256]{2,1,0:T(8,128)} %uinv.3, f32[2,256,256]{2,1,0:T(8,128)} %upper.1, f32[2,256,256]{2,1,0:T(8,128)} %rhs.1), custom_call_target="tpu_custom_call" | custom-call | flops 1000000 | tf_op jit(solution)/shard_map/prepare/pallas_call | solution.py:369
  12.2 10.0 %leaf_forward.1 = (f32[8,256,256]{2,1,0:T(8,128)}, f32[16,32,256]{2,1,0:T(8,128)}, f32[16,32,256]{2,1,0:T(8,128)}, f32[16,32,256]{2,1,0:T(8,128)}, f32[16,32,256...) custom-call(s32[8,2]{1,0:T(8,128)} %copy.16.targets, ...), custom_call_target="tpu_custom_call" | custom-call | tf_op jit(solution)/shard_map/leaf_forward/pallas_call | solution.py:130
  23.8 4.0 %collective-permute-done.7 = f32[64,32,256]{2,1,0:T(8,128)S(1)} collective-permute-done((f32[64,32,256]{2,1,0:T(8,128)}, f32[64,32,256]{2,1,0:T(8,128)S(1)}, u32[]{:S(2)}, u32[]{:S(2)}) %collective-permute-start.7) | collective-permute-done | bytes 2097184 | tf_op jit(solution)/shard_map/ppermute | solution.py:386
  27.8 3.4 %add.19 = f32[64,32,256]{2,1,0:T(8,128)} add(f32[64,32,256]{2,1,0:T(8,128)} %get-tuple-element.66, f32[64,32,256]{2,1,0:T(8,128)S(1)} %collective-permute-done.7) | non-fusion elementwise | flops 524288 | bytes 6291456 | tf_op jit(solution)/shard_map/add | solution.py:436
  31.1 7.0 %all-to-all-start = ((f32[64,32,256]{2,1,0:T(8,128)}), f32[64,32,256]{2,1,0:T(8,128)S(1)}, u32[]{:S(2)}, u32[]{:S(2)}) async-start(f32[64,32,256]{2,1,0:T(8,128)} %add.19), calls=%async_computation | async-start | bytes 4194304 | tf_op jit(solution)/shard_map/all_to_all | solution.py:407
  47.5 3.4 %collective-permute-start.4 = (f32[16,32,256]{2,1,0:T(8,128)S(1)}, f32[16,32,256]{2,1,0:T(8,128)S(1)}, u32[]{:S(2)}, u32[]{:S(2)}) collective-permute-start(f32[16,32,256]{2,1,0:T(8,128)S(1)} %add.17), channel_id=1, source_target_pairs={{0,64},{16,80},{32,96},{48,112},{64,0},{80,16},{96,32},{112,48},{1... | collective-permute-start | bytes 1572872 | tf_op jit(solution)/shard_map/ppermute | solution.py:390
  51.0 16.9 %collective-permute-done.10.refs_3_ = f32[2,128,256]{2,1,0:T(8,128)S(1)} collective-permute-done((f32[2,128,256]{2,1,0:T(8,128)S(1)}, f32[2,128,256]{2,1,0:T(8,128)S(1)}, u32[]{:S(2)}, u32[]{:S(2)}) %collective-permute-start.10) | collective-permute-done | bytes 262176 | tf_op jit(solution)/shard_map/ppermute | solution.py:397
  67.9 3.8 %collective-permute-start.6 = (f32[16,32,256]{2,1,0:T(8,128)S(1)}, f32[16,32,256]{2,1,0:T(8,128)S(1)}, u32[]{:S(2)}, u32[]{:S(2)}) collective-permute-start(f32[16,32,256]{2,1,0:T(8,128)S(1)} %add.18), channel_id=1, source_target_pairs={{0,96},{16,112},{32,0},{48,16},{64,32},{80,48},{96,64},{112,80},{1... | collective-permute-start | bytes 1572872 | tf_op jit(solution)/shard_map/ppermute | solution.py:390
  71.7 3.7 %collective-permute-start.8 = (f32[2,128,256]{2,1,0:T(8,128)S(1)}, f32[2,128,256]{2,1,0:T(8,128)}, u32[]{:S(2)}, u32[]{:S(2)}) collective-permute-start(f32[2,128,256]{2,1,0:T(8,128)S(1)} %copy-done.13), channel_id=1, source_target_pairs={{0,1},{1,2},{2,3},{3,0},{4,5},{5,6},{6,7},{7,4},{8,9},{9,10},{10,1... | collective-permute-start | bytes 786440 | tf_op jit(solution)/shard_map/ppermute | solution.py:397
  75.4 5.6 %collective-permute-done.8.refs_1_ = f32[2,128,256]{2,1,0:T(8,128)} collective-permute-done((f32[2,128,256]{2,1,0:T(8,128)S(1)}, f32[2,128,256]{2,1,0:T(8,128)}, u32[]{:S(2)}, u32[]{:S(2)}) %collective-permute-start.8) | collective-permute-done | bytes 262176 | tf_op jit(solution)/shard_map/ppermute | solution.py:397
  88.9 5.8 %all-to-all-start.1 = ((f32[16,32,256]{2,1,0:T(8,128)}), f32[16,32,256]{2,1,0:T(8,128)}, u32[]{:S(2)}, u32[]{:S(2)}) async-start(f32[16,32,256]{2,1,0:T(8,128)} %gathered.1), calls=%async_computation.1 | async-start | bytes 1048576 | tf_op jit(solution)/shard_map/all_to_all | solution.py:407
  108.7 7.4 %all_to_all.40.values = f32[4,32,256]{2,1,0:T(8,128)S(1)} all-to-all(f32[4,32,256]{2,1,0:T(8,128)S(1)} %get-tuple-element.81), channel_id=1, replica_groups={{0,1,2,3},{4,5,6,7},{8,9,10,11},{12,13,14,15},{16,17,18,19},{20,21,22,2..., dimensions={0} | all-to-all | bytes 262144 | tf_op jit(solution)/shard_map/all_to_all | solution.py:401
  116.8 3.8 %collective-permute-start.18 = (f32[4,2,128,256]{3,2,1,0:T(8,128)}, f32[4,2,128,256]{3,2,1,0:T(8,128)S(1)}, u32[]{:S(2)}, u32[]{:S(2)}) collective-permute-start(f32[4,2,128,256]{3,2,1,0:T(8,128)} %bitcast.6), channel_id=1, source_target_pairs={{0,16},{16,0},{32,48},{48,32},{64,80},{80,64},{96,112},{112,96},{1... | collective-permute-start | bytes 3145736 | tf_op jit(solution)/shard_map/ppermute | solution.py:386
  120.7 7.8 %all_to_all.41.across = f32[4,32,256]{2,1,0:T(8,128)S(1)} all-to-all(f32[4,32,256]{2,1,0:T(8,128)S(1)} %total.2), channel_id=1, replica_groups={{0,4,8,12},{1,5,9,13},{2,6,10,14},{3,7,11,15},{16,20,24,28},{17,21,25,2..., dimensions={0} | all-to-all | bytes 262144 | tf_op jit(solution)/shard_map/all_to_all | solution.py:401
  133.2 7.3 %all_to_all.42.values = f32[4,32,256]{2,1,0:T(8,128)S(1)} all-to-all(f32[4,32,256]{2,1,0:T(8,128)S(1)} %get-tuple-element.96), channel_id=1, replica_groups={{0,1,2,3},{4,5,6,7},{8,9,10,11},{12,13,14,15},{16,17,18,19},{20,21,22,2..., dimensions={0} | all-to-all | bytes 262144 | tf_op jit(solution)/shard_map/all_to_all | solution.py:401
  141.3 7.2 %all_to_all.43.across = f32[4,32,256]{2,1,0:T(8,128)S(1)} all-to-all(f32[4,32,256]{2,1,0:T(8,128)S(1)} %total.3), channel_id=1, replica_groups={{0,4,8,12},{1,5,9,13},{2,6,10,14},{3,7,11,15},{16,20,24,28},{17,21,25,2..., dimensions={0} | all-to-all | bytes 262144 | tf_op jit(solution)/shard_map/all_to_all | solution.py:401
  151.0 3.6 %all-to-all-start.6 = ((f32[16,32,256]{2,1,0:T(8,128)}), f32[16,32,256]{2,1,0:T(8,128)S(1)}, u32[]{:S(2)}, u32[]{:S(2)}) async-start(f32[16,32,256]{2,1,0:T(8,128)} %get-tuple-element.100), calls=%async_computation.6 | async-start | bytes 1048576 | tf_op jit(solution)/shard_map/all_to_all | solution.py:407
  154.6 4.9 %collective-permute-start.21 = (f32[32,256]{1,0:T(8,128)S(1)}, f32[32,256]{1,0:T(8,128)S(1)}, u32[]{:S(2)}, u32[]{:S(2)}) collective-permute-start(f32[32,256]{1,0:T(8,128)S(1)} %get-tuple-element.99.first), channel_id=1, source_target_pairs={{0,96},{16,112},{32,0},{48,16},{64,32},{80,48},{96,64},{112,80},{1... | collective-permute-start | bytes 98312 | tf_op jit(solution)/shard_map/ppermute | solution.py:390
  160.5 3.5 %collective-permute-done.20.third = f32[32,256]{1,0:T(8,128)S(1)} collective-permute-done((f32[32,256]{1,0:T(8,128)S(1)}, f32[32,256]{1,0:T(8,128)S(1)}, u32[]{:S(2)}, u32[]{:S(2)}) %collective-permute-start.20) | collective-permute-done | bytes 32800 | tf_op jit(solution)/shard_map/ppermute | solution.py:390
  166.3 6.6 %all-to-all-start.7 = ((f32[64,32,256]{2,1,0:T(8,128)}), f32[64,32,256]{2,1,0:T(8,128)}, u32[]{:S(2)}, u32[]{:S(2)}) async-start(f32[64,32,256]{2,1,0:T(8,128)} %bitcast.2), calls=%async_computation.7 | async-start | bytes 4194304 | tf_op jit(solution)/shard_map/all_to_all | solution.py:407
  183.4 12.8 %all-to-all-done.7 = f32[64,32,256]{2,1,0:T(8,128)} async-done(((f32[64,32,256]{2,1,0:T(8,128)}), f32[64,32,256]{2,1,0:T(8,128)}, u32[]{:S(2)}, u32[]{:S(2)}) %all-to-all-start.7) | async-done | bytes 2097184 | tf_op jit(solution)/shard_map/all_to_all | solution.py:407
  196.2 6.4 %collective-permute-start.22 = (f32[16,4,32,256]{3,2,1,0:T(8,128)}, f32[16,4,32,256]{3,2,1,0:T(8,128)S(1)}, u32[]{:S(2)}, u32[]{:S(2)}) collective-permute-start(f32[16,4,32,256]{3,2,1,0:T(8,128)} %bitcast.3.even), channel_id=1, source_target_pairs={{0,16},{16,0},{32,48},{48,32},{64,80},{80,64},{96,112},{112,96},{1... | collective-permute-start | bytes 6291464 | tf_op jit(solution)/shard_map/ppermute | solution.py:386
  202.6 4.0 %collective-permute-done.22.even_other = f32[16,4,32,256]{3,2,1,0:T(8,128)S(1)} collective-permute-done((f32[16,4,32,256]{3,2,1,0:T(8,128)}, f32[16,4,32,256]{3,2,1,0:T(8,128)S(1)}, u32[]{:S(2)}, u32[]{:S(2)}) %collective-permute-start.22) | collective-permute-done | bytes 2097184 | tf_op jit(solution)/shard_map/ppermute | solution.py:386
  207.9 7.2 %leaf_back.1 = (f32[8,256,256]{2,1,0:T(8,128)}, f32[2,256,256]{2,1,0:T(8,128)}) custom-call(s32[8,2]{1,0:T(8,128)} %copy.16.targets, f32[8,256,256]{2,1,0:T(8,128)} %copy-done.11, f32[8,2,256,256]{3,2,1,0:T(8,128)} %copy-done.3, f32[16,4,32,256]{3,2,1,0:T(8,128)} %bitcast.3.even, f32[16,4,32,256]{3,2,1,0:T(8,128)} %copy-done.15, f32[4,2,16,32,256]{4,3,2,1,0:T(8,128)} %bitcast.9), custom_call_target="tpu_custom_call" | custom-call | tf_op jit(solution)/shard_map/leaf_back/pallas_call | solution.py:345
  (97 shorter events, 57.8 us)
Async XLA Ops:
  22.3 5.5 %collective-permute-start.7 = (f32[64,32,256]{2,1,0:T(8,128)}, f32[64,32,256]{2,1,0:T(8,128)S(1)}, u32[]{:S(2)}, u32[]{:S(2)}) collective-permute-start(f32[64,32,256]{2,1,0:T(8,128)} %get-tuple-element.67), channel_id=1, source_target_pairs={{0,16},{16,0},{32,48},{48,32},{64,80},{80,64},{96,112},{112,96},{1... | collective-permute-start | bytes 6291464 | tf_op jit(solution)/shard_map/ppermute | solution.py:386
  31.1 53.7 %all-to-all-start = ((f32[64,32,256]{2,1,0:T(8,128)}), f32[64,32,256]{2,1,0:T(8,128)S(1)}, u32[]{:S(2)}, u32[]{:S(2)}) async-start(f32[64,32,256]{2,1,0:T(8,128)} %add.19), calls=%async_computation | async-start | bytes 4194304 | tf_op jit(solution)/shard_map/all_to_all | solution.py:407
  38.1 78.7 %all-gather.5.cloned.1.call-start = ((), (), s32[]{:S(2)}) async-start(), calls=%async_computation.8 | async-start | bytes 1310720 | tf_op jit(solution)/shard_map/all_gather | solution.py:448
  38.2 4.7 %collective-permute-start.1 = (f32[16,32,256]{2,1,0:T(8,128)S(1)}, f32[16,32,256]{2,1,0:T(8,128)S(1)}, u32[]{:S(2)}, u32[]{:S(2)}) collective-permute-start(f32[16,32,256]{2,1,0:T(8,128)S(1)} %copy-done.18), channel_id=1, source_target_pairs={{0,16},{16,0},{32,48},{48,32},{64,80},{80,64},{96,112},{112,96},{1... | collective-permute-start | bytes 1572872 | tf_op jit(solution)/shard_map/ppermute | solution.py:386
  38.9 5.8 %collective-permute-start.3 = (f32[16,32,256]{2,1,0:T(8,128)}, f32[16,32,256]{2,1,0:T(8,128)S(1)}, u32[]{:S(2)}, u32[]{:S(2)}) collective-permute-start(f32[16,32,256]{2,1,0:T(8,128)} %get-tuple-element.63), channel_id=1, source_target_pairs={{0,16},{16,0},{32,48},{48,32},{64,80},{80,64},{96,112},{112,96},{1... | collective-permute-start | bytes 1572872 | tf_op jit(solution)/shard_map/ppermute | solution.py:386
  39.0 8.5 %collective-permute-start.5 = (f32[16,32,256]{2,1,0:T(8,128)}, f32[16,32,256]{2,1,0:T(8,128)S(1)}, u32[]{:S(2)}, u32[]{:S(2)}) collective-permute-start(f32[16,32,256]{2,1,0:T(8,128)} %get-tuple-element.65), channel_id=1, source_target_pairs={{0,16},{16,0},{32,48},{48,32},{64,80},{80,64},{96,112},{112,96},{1... | collective-permute-start | bytes 1572872 | tf_op jit(solution)/shard_map/ppermute | solution.py:386
  39.4 28.5 %collective-permute-start.10 = (f32[2,128,256]{2,1,0:T(8,128)S(1)}, f32[2,128,256]{2,1,0:T(8,128)S(1)}, u32[]{:S(2)}, u32[]{:S(2)}) collective-permute-start(f32[2,128,256]{2,1,0:T(8,128)S(1)} %copy-done.13), channel_id=1, source_target_pairs={{0,3},{1,0},{2,1},{3,2},{4,7},{5,4},{6,5},{7,6},{8,11},{9,8},{10,9... | collective-permute-start | bytes 786440 | tf_op jit(solution)/shard_map/ppermute | solution.py:397
  42.3 29.4 %collective-permute-start.9 = (f32[2,128,256]{2,1,0:T(8,128)S(1)}, f32[2,128,256]{2,1,0:T(8,128)S(1)}, u32[]{:S(2)}, u32[]{:S(2)}) collective-permute-start(f32[2,128,256]{2,1,0:T(8,128)S(1)} %copy-done.13), channel_id=1, source_target_pairs={{0,2},{1,3},{2,0},{3,1},{4,6},{5,7},{6,4},{7,5},{8,10},{9,11},{10,... | collective-permute-start | bytes 786440 | tf_op jit(solution)/shard_map/ppermute | solution.py:397
  42.9 40.4 %collective-permute-start = (f32[16,32,256]{2,1,0:T(8,128)}, f32[16,32,256]{2,1,0:T(8,128)S(1)}, u32[]{:S(2)}, u32[]{:S(2)}) collective-permute-start(f32[16,32,256]{2,1,0:T(8,128)} %get-tuple-element.59), channel_id=1, source_target_pairs={{0,16},{16,0},{32,48},{48,32},{64,80},{80,64},{96,112},{112,96},{1... | collective-permute-start | bytes 1572872 | tf_op jit(solution)/shard_map/ppermute | solution.py:386
  44.7 38.6 %collective-permute-start.2 = (f32[16,32,256]{2,1,0:T(8,128)S(1)}, f32[16,32,256]{2,1,0:T(8,128)S(1)}, u32[]{:S(2)}, u32[]{:S(2)}) collective-permute-start(f32[16,32,256]{2,1,0:T(8,128)S(1)} %add.16), channel_id=1, source_target_pairs={{0,32},{16,48},{32,64},{48,80},{64,96},{80,112},{96,0},{112,16},{1... | collective-permute-start | bytes 1572872 | tf_op jit(solution)/shard_map/ppermute | solution.py:390
  47.5 36.2 %collective-permute-start.4 = (f32[16,32,256]{2,1,0:T(8,128)S(1)}, f32[16,32,256]{2,1,0:T(8,128)S(1)}, u32[]{:S(2)}, u32[]{:S(2)}) collective-permute-start(f32[16,32,256]{2,1,0:T(8,128)S(1)} %add.17), channel_id=1, source_target_pairs={{0,64},{16,80},{32,96},{48,112},{64,0},{80,16},{96,32},{112,48},{1... | collective-permute-start | bytes 1572872 | tf_op jit(solution)/shard_map/ppermute | solution.py:390
  67.9 16.1 %collective-permute-start.6 = (f32[16,32,256]{2,1,0:T(8,128)S(1)}, f32[16,32,256]{2,1,0:T(8,128)S(1)}, u32[]{:S(2)}, u32[]{:S(2)}) collective-permute-start(f32[16,32,256]{2,1,0:T(8,128)S(1)} %add.18), channel_id=1, source_target_pairs={{0,96},{16,112},{32,0},{48,16},{64,32},{80,48},{96,64},{112,80},{1... | collective-permute-start | bytes 1572872 | tf_op jit(solution)/shard_map/ppermute | solution.py:390
  71.7 9.3 %collective-permute-start.8 = (f32[2,128,256]{2,1,0:T(8,128)S(1)}, f32[2,128,256]{2,1,0:T(8,128)}, u32[]{:S(2)}, u32[]{:S(2)}) collective-permute-start(f32[2,128,256]{2,1,0:T(8,128)S(1)} %copy-done.13), channel_id=1, source_target_pairs={{0,1},{1,2},{2,3},{3,0},{4,5},{5,6},{6,7},{7,4},{8,9},{9,10},{10,1... | collective-permute-start | bytes 786440 | tf_op jit(solution)/shard_map/ppermute | solution.py:397
  88.9 16.2 %all-to-all-start.1 = ((f32[16,32,256]{2,1,0:T(8,128)}), f32[16,32,256]{2,1,0:T(8,128)}, u32[]{:S(2)}, u32[]{:S(2)}) async-start(f32[16,32,256]{2,1,0:T(8,128)} %gathered.1), calls=%async_computation.1 | async-start | bytes 1048576 | tf_op jit(solution)/shard_map/all_to_all | solution.py:407
  94.7 5.7 %collective-permute-start.15 = (f32[32,256]{1,0:T(8,128)S(1)}, f32[32,256]{1,0:T(8,128)S(1)}, u32[]{:S(2)}, u32[]{:S(2)}) collective-permute-start(f32[32,256]{1,0:T(8,128)S(1)} %get-tuple-element.76), channel_id=1, source_target_pairs={{0,32},{16,48},{32,64},{48,80},{64,96},{80,112},{96,0},{112,16},{1... | collective-permute-start | bytes 98312 | tf_op jit(solution)/shard_map/ppermute | solution.py:390
  96.4 5.4 %collective-permute-start.16 = (f32[32,256]{1,0:T(8,128)S(1)}, f32[32,256]{1,0:T(8,128)S(1)}, u32[]{:S(2)}, u32[]{:S(2)}) collective-permute-start(f32[32,256]{1,0:T(8,128)S(1)} %get-tuple-element.77), channel_id=1, source_target_pairs={{0,64},{16,80},{32,96},{48,112},{64,0},{80,16},{96,32},{112,48},{1... | collective-permute-start | bytes 98312 | tf_op jit(solution)/shard_map/ppermute | solution.py:390
  116.8 11.7 %collective-permute-start.18 = (f32[4,2,128,256]{3,2,1,0:T(8,128)}, f32[4,2,128,256]{3,2,1,0:T(8,128)S(1)}, u32[]{:S(2)}, u32[]{:S(2)}) collective-permute-start(f32[4,2,128,256]{3,2,1,0:T(8,128)} %bitcast.6), channel_id=1, source_target_pairs={{0,16},{16,0},{32,48},{48,32},{64,80},{80,64},{96,112},{112,96},{1... | collective-permute-start | bytes 3145736 | tf_op jit(solution)/shard_map/ppermute | solution.py:386
  151.0 14.5 %all-to-all-start.6 = ((f32[16,32,256]{2,1,0:T(8,128)}), f32[16,32,256]{2,1,0:T(8,128)S(1)}, u32[]{:S(2)}, u32[]{:S(2)}) async-start(f32[16,32,256]{2,1,0:T(8,128)} %get-tuple-element.100), calls=%async_computation.6 | async-start | bytes 1048576 | tf_op jit(solution)/shard_map/all_to_all | solution.py:407
  154.6 52.0 %all-gather.7.cloned.1.call-start = ((), (), s32[]{:S(2)}) async-start(), calls=%async_computation.9 | async-start | bytes 4718592 | tf_op jit(solution)/shard_map/all_gather | solution.py:486
  154.6 5.9 %collective-permute-start.21 = (f32[32,256]{1,0:T(8,128)S(1)}, f32[32,256]{1,0:T(8,128)S(1)}, u32[]{:S(2)}, u32[]{:S(2)}) collective-permute-start(f32[32,256]{1,0:T(8,128)S(1)} %get-tuple-element.99.first), channel_id=1, source_target_pairs={{0,96},{16,112},{32,0},{48,16},{64,32},{80,48},{96,64},{112,80},{1... | collective-permute-start | bytes 98312 | tf_op jit(solution)/shard_map/ppermute | solution.py:390
  159.5 4.5 %collective-permute-start.20 = (f32[32,256]{1,0:T(8,128)S(1)}, f32[32,256]{1,0:T(8,128)S(1)}, u32[]{:S(2)}, u32[]{:S(2)}) collective-permute-start(f32[32,256]{1,0:T(8,128)S(1)} %get-tuple-element.99.first), channel_id=1, source_target_pairs={{0,64},{16,80},{32,96},{48,112},{64,0},{80,16},{96,32},{112,48},{1... | collective-permute-start | bytes 98312 | tf_op jit(solution)/shard_map/ppermute | solution.py:390
  159.5 4.5 %collective-permute-start.19 = (f32[32,256]{1,0:T(8,128)S(1)}, f32[32,256]{1,0:T(8,128)S(1)}, u32[]{:S(2)}, u32[]{:S(2)}) collective-permute-start(f32[32,256]{1,0:T(8,128)S(1)} %get-tuple-element.99.first), channel_id=1, source_target_pairs={{0,32},{16,48},{32,64},{48,80},{64,96},{80,112},{96,0},{112,16},{1... | collective-permute-start | bytes 98312 | tf_op jit(solution)/shard_map/ppermute | solution.py:390
  166.3 29.9 %all-to-all-start.7 = ((f32[64,32,256]{2,1,0:T(8,128)}), f32[64,32,256]{2,1,0:T(8,128)}, u32[]{:S(2)}, u32[]{:S(2)}) async-start(f32[64,32,256]{2,1,0:T(8,128)} %bitcast.2), calls=%async_computation.7 | async-start | bytes 4194304 | tf_op jit(solution)/shard_map/all_to_all | solution.py:407
  196.2 10.4 %collective-permute-start.22 = (f32[16,4,32,256]{3,2,1,0:T(8,128)}, f32[16,4,32,256]{3,2,1,0:T(8,128)S(1)}, u32[]{:S(2)}, u32[]{:S(2)}) collective-permute-start(f32[16,4,32,256]{3,2,1,0:T(8,128)} %bitcast.3.even), channel_id=1, source_target_pairs={{0,16},{16,0},{32,48},{48,32},{64,80},{80,64},{96,112},{112,96},{1... | collective-permute-start | bytes 6291464 | tf_op jit(solution)/shard_map/ppermute | solution.py:386
  (24 other events, 191.2 us)
Sparse Core Ops, SparseCore 0:
  89.0 24.3 all-gather.4
  166.4 40.1 all-gather.6

commit v5 on v3

--- a/solution.py
+++ b/solution.py
@@ -140,6 +140,23 @@
         compiler_params=params(58),
         name="leaf_forward",
     )(targets, linv, rhs, low)
+
+
+def joined_kernel(first, second, out):
+    out[...] = first[...] + second[...]
+
+
+def joined(first, second, steps=4):
+    block = pl.BlockSpec((first.shape[0] // steps, COLS, TILE), lambda i: (i, 0, 0))
+    return pl.pallas_call(
+        joined_kernel,
+        out_shape=jax.ShapeDtypeStruct(first.shape, jnp.float32),
+        grid=(steps,),
+        in_specs=[block] * 2,
+        out_specs=block,
+        compiler_params=params(20),
+        name="joined",
+    )(first, second)
 
 
 def gathered_kernel(first, second, third, fourth, out):
@@ -402,7 +419,7 @@
     fwd, *parts = leaf_forward(targets, leaf_linv, leaf_rhs, low_couple)
     even_keep, even_send, odd_keep, odd_send = parts[:4], parts[4:8], parts[8], parts[9]
     even = [even_keep[d] + other_core(even_send[d]) for d in (1, 2, 3, 0)]
-    odd = odd_keep + other_core(odd_send)
+    odd = joined(odd_keep, other_core(odd_send))
     odd, leaf_uinv = after((odd, leaf_uinv))
     odd = exchange(odd).reshape(GRID, 4, COLS, TILE)
     base, factor = leaf_ready(leaf_uinv, up_couple, fwd)

time: 213 us -> 213 us (level)
  other arithmetic: 4.82 us -> 1.49 us
    add x1 -> x0, other arithmetic: 3.33 us -> none  [local(): odd = odd_keep + other_core(odd_send)]
    unnamed x47 -> x49, local copies, waits for them, and re-layouts: 17.8 us -> 19.3 us
  transfers between devices with their start and end apart: 22 -> 22, of which waited for: 13 -> 13; matrix products, arithmetic and copies ran while one was open for 3% -> 1% of each run, Pallas kernels for 9% -> 10%
where the time goes in v5:
time: 213 us; the launch traced here: 212 us
  starting transfers between devices  49.6 us (23%)
  blocking collectives  44.5 us (21%)
  waiting for transfers between devices  42.1 us (20%)
  Pallas kernels  41.2 us (19%)
  local copies, waits for them, and re-layouts  19.3 us (9%)
  between operations  14.2 us (7%)
    all_to_all x2, blocking collectives, exchange(): lax.all_to_all(value, 'grid', split_axis=0, concat_axis=0, tiled=True)  44.5 us
    ppermute x9, waiting for transfers between devices, along_z(): lax.ppermute(value, 'layer', [(i, (i + 2 * steps) % LAYERS) for i in rang...  28 us
    all_to_all x4, starting transfers between devices, exchange(): lax.all_to_all(value, 'grid', split_axis=0, concat_axis=0, tiled=True)  24.7 us
    unnamed x49, local copies, waits for them, and re-layouts  19.3 us
    pallas_call x7, Pallas kernels, call(): pl.pallas_call(kernel, out_shape=[jax.ShapeDtypeStruct(shape, jnp.float32...  15.7 us
    ppermute x9, starting transfers between devices, along_z(): lax.ppermute(value, 'layer', [(i, (i + 2 * steps) % LAYERS) for i in rang...  13.4 us
    ppermute x7, starting transfers between devices, other_core(): lax.ppermute(value, 'layer', [(i, i + 1 - 2 * (i % 2)) for i in range(LAY...  11.4 us
    pallas_call x1, Pallas kernels, leaf_forward(): pl.pallas_call(leaf_forward_kernel, out_shape=[jax.ShapeDtypeStruct(linv....  10 us
  transfers between devices with their start and end apart: 22, of which 13 were waited for; matrix products, arithmetic and copies ran while one was open for 1% of the time, Pallas kernels for 10%

profile of v5, /device:TPU:1, one launch (start us, length us, event | category | flops | bytes accessed | tf_op | source)
XLA Modules:
  0.0 212.4 jit_solution(18366017678951847786)
XLA Ops:
  7.2 3.7 %prepare.1 = (f32[2,256,256]{2,1,0:T(8,128)}, f32[2,256,256]{2,1,0:T(8,128)}, f32[2,128,256]{2,1,0:T(8,128)}, f32[2,256,256]{2,1,0:T(8,128)}) custom-call(f32[2,256,256]{2,1,0:T(8,128)} %linv.5, f32[2,256,256]{2,1,0:T(8,128)} %lower.1, f32[2,256,256]{2,1,0:T(8,128)} %uinv.4, f32[2,256,256]{2,1,0:T(8,128)} %upper.1, f32[2,256,256]{2,1,0:T(8,128)} %rhs.1), custom_call_target="tpu_custom_call" | custom-call | flops 1000000 | tf_op jit(solution)/shard_map/prepare/pallas_call | solution.py:367
  11.6 10.0 %leaf_forward.1 = (f32[8,256,256]{2,1,0:T(8,128)}, f32[16,32,256]{2,1,0:T(8,128)}, f32[16,32,256]{2,1,0:T(8,128)}, f32[16,32,256]{2,1,0:T(8,128)}, f32[16,32,256...) custom-call(s32[8,2]{1,0:T(8,128)} %copy.16.targets, ...), custom_call_target="tpu_custom_call" | custom-call | tf_op jit(solution)/shard_map/leaf_forward/pallas_call | solution.py:125
  23.2 4.0 %collective-permute-done.7.second = f32[64,32,256]{2,1,0:T(8,128)S(1)} collective-permute-done((f32[64,32,256]{2,1,0:T(8,128)}, f32[64,32,256]{2,1,0:T(8,128)S(1)}, u32[]{:S(2)}, u32[]{:S(2)}) %collective-permute-start.7) | collective-permute-done | bytes 2097184 | tf_op jit(solution)/shard_map/ppermute | solution.py:384
  30.7 7.0 %all-to-all-start = ((f32[64,32,256]{2,1,0:T(8,128)}), f32[64,32,256]{2,1,0:T(8,128)S(1)}, u32[]{:S(2)}, u32[]{:S(2)}) async-start(f32[64,32,256]{2,1,0:T(8,128)} %joined.1), calls=%async_computation | async-start | bytes 4194304 | tf_op jit(solution)/shard_map/all_to_all | solution.py:392
  43.2 3.4 %collective-permute-start.4 = (f32[16,32,256]{2,1,0:T(8,128)S(1)}, f32[16,32,256]{2,1,0:T(8,128)S(1)}, u32[]{:S(2)}, u32[]{:S(2)}) collective-permute-start(f32[16,32,256]{2,1,0:T(8,128)S(1)} %add.14), channel_id=1, source_target_pairs={{0,64},{16,80},{32,96},{48,112},{64,0},{80,16},{96,32},{112,48},{1... | collective-permute-start | bytes 1572872 | tf_op jit(solution)/shard_map/ppermute | solution.py:388
  47.6 9.8 %collective-permute-done.2.second = f32[16,32,256]{2,1,0:T(8,128)S(1)} collective-permute-done((f32[16,32,256]{2,1,0:T(8,128)S(1)}, f32[16,32,256]{2,1,0:T(8,128)S(1)}, u32[]{:S(2)}, u32[]{:S(2)}) %collective-permute-start.2) | collective-permute-done | bytes 524320 | tf_op jit(solution)/shard_map/ppermute | solution.py:388
  57.4 12.0 %collective-permute-done.4.third = f32[16,32,256]{2,1,0:T(8,128)S(1)} collective-permute-done((f32[16,32,256]{2,1,0:T(8,128)S(1)}, f32[16,32,256]{2,1,0:T(8,128)S(1)}, u32[]{:S(2)}, u32[]{:S(2)}) %collective-permute-start.4) | collective-permute-done | bytes 524320 | tf_op jit(solution)/shard_map/ppermute | solution.py:388
  70.3 3.3 %leaf_ready.1 = (f32[8,256,256]{2,1,0:T(8,128)S(1)}, f32[8,2,256,256]{3,2,1,0:T(8,128)S(1)}) custom-call(f32[8,256,256]{2,1,0:T(8,128)S(1)} %copy-done.12, f32[8,2,256,256]{3,2,1,0:T(8,128)S(1)} %copy-done.2, f32[8,256,256]{2,1,0:T(8,128)S(1)} %copy-done.14), custom_call_target="tpu_custom_call" | custom-call | tf_op jit(solution)/shard_map/leaf_ready/pallas_call | solution.py:264
  76.8 7.0 %all-to-all-start.1 = ((f32[16,32,256]{2,1,0:T(8,128)}), f32[16,32,256]{2,1,0:T(8,128)}, u32[]{:S(2)}, u32[]{:S(2)}) async-start(f32[16,32,256]{2,1,0:T(8,128)} %copy-done.11), calls=%async_computation.1 | async-start | bytes 1048576 | tf_op jit(solution)/shard_map/all_to_all | solution.py:392
  85.8 2.5 %collective-permute-start.9 = (f32[32,256]{1,0:T(8,128)S(1)}, f32[32,256]{1,0:T(8,128)S(1)}, u32[]{:S(2)}, u32[]{:S(2)}) collective-permute-start(f32[32,256]{1,0:T(8,128)S(1)} %get-tuple-element.72), channel_id=1, source_target_pairs={{0,64},{16,80},{32,96},{48,112},{64,0},{80,16},{96,32},{112,48},{1... | collective-permute-start | bytes 98312 | tf_op jit(solution)/shard_map/ppermute | solution.py:388
  94.0 2.4 %enter.1 = (f32[2,32,256]{2,1,0:T(8,128)S(1)}, f32[16,32,256]{2,1,0:T(8,128)}) custom-call(f32[16,32,256]{2,1,0:T(8,128)} %all-to-all-done.1.even, f32[32,256]{1,0:T(8,128)S(1)} %get-tuple-element.70.odd, f32[32,256]{1,0:T(8,128)S(1)} %collective-permute-done.8.odd_1, f32[32,256]{1,0:T(8,128)S(1)} %collective-permute-done.9.odd_2, ...), custom_call_target="tpu_custom_call" | custom-call | flops 1000000 | tf_op jit(solution)/shard_map/enter/pallas_call | solution.py:367
  96.4 3.8 %collective-permute-start.11 = (f32[32,128,256]{2,1,0:T(8,128)}, f32[32,128,256]{2,1,0:T(8,128)}, u32[]{:S(2)}, u32[]{:S(2)}) collective-permute-start(f32[32,128,256]{2,1,0:T(8,128)} %all-gather.4.cloned.1.call-done.own), channel_id=1, source_target_pairs={{0,16},{16,0},{32,48},{48,32},{64,80},{80,64},{96,112},{112,96},{1... | collective-permute-start | bytes 12582920 | tf_op jit(solution)/shard_map/ppermute | solution.py:384
  100.2 6.9 %all-to-all-start.2 = ((f32[16,32,256]{2,1,0:T(8,128)}), f32[16,32,256]{2,1,0:T(8,128)S(1)}, u32[]{:S(2)}, u32[]{:S(2)}) async-start(f32[16,32,256]{2,1,0:T(8,128)} %get-tuple-element.79), calls=%async_computation.2 | async-start | bytes 1048576 | tf_op jit(solution)/shard_map/all_to_all | solution.py:392
  109.6 3.1 %chain_pairs.1 = (bf16[2,16,256,256]{3,2,1,0:T(8,128)(2,1)S(1)}, bf16[2,16,256,256]{3,2,1,0:T(8,128)(2,1)S(1)}) custom-call(f32[32,128,256]{2,1,0:T(8,128)S(1)} %copy-done.3, f32[32,128,256]{2,1,0:T(8,128)} %collective-permute-done.11.other), custom_call_target="tpu_custom_call" | custom-call | tf_op jit(solution)/shard_map/chain_pairs/pallas_call | solution.py:203
  119.5 4.6 %turn.1 = (f32[2,32,256]{2,1,0:T(8,128)S(1)}, f32[16,32,256]{2,1,0:T(8,128)S(1)}) custom-call(f32[16,32,256]{2,1,0:T(8,128)S(1)} %all-to-all-done.2.values, bf16[2,16,256,256]{3,2,1,0:T(8,128)(2,1)S(1)} %copy-done.1, f32[2,32,256]{2,1,0:T(8,128)S(1)} %get-tuple-element.85.vec, f32[2,256,256]{2,1,0:T(8,128)S(1)} %copy-done.10, f32[2,256,256]{2,1,0:T(8,128)S(1)} %copy-done.9, ...), custom_call_target="tpu_custom_call" | custom-call | flops 1000000 | tf_op jit(solution)/shard_map/turn/pallas_call | solution.py:367
  124.0 16.5 %all_to_all.30.values = f32[16,32,256]{2,1,0:T(8,128)S(1)} all-to-all(f32[16,32,256]{2,1,0:T(8,128)S(1)} %get-tuple-element.87), channel_id=1, replica_groups=mesh['layer'=8,'grid'=16] {'grid'}, dimensions={0} | all-to-all | bytes 1048576 | tf_op jit(solution)/shard_map/all_to_all | solution.py:392
  140.5 4.7 %leave.1 = (f32[32,256]{1,0:T(8,128)S(1)}, f32[16,32,256]{2,1,0:T(8,128)}) custom-call(f32[16,32,256]{2,1,0:T(8,128)S(1)} %all_to_all.30.values, bf16[2,16,256,256]{3,2,1,0:T(8,128)(2,1)S(1)} %copy-done.5, f32[2,32,256]{2,1,0:T(8,128)S(1)} %get-tuple-element.89.vec, f32[2,256,256]{2,1,0:T(8,128)S(1)} %copy-done.15), custom_call_target="tpu_custom_call" | custom-call | flops 1000000 | tf_op jit(solution)/shard_map/leave/pallas_call | solution.py:367
  145.2 3.7 %all-to-all-start.4 = ((f32[16,32,256]{2,1,0:T(8,128)}), f32[16,32,256]{2,1,0:T(8,128)S(1)}, u32[]{:S(2)}, u32[]{:S(2)}) async-start(f32[16,32,256]{2,1,0:T(8,128)} %get-tuple-element.91), calls=%async_computation.4 | async-start | bytes 1048576 | tf_op jit(solution)/shard_map/all_to_all | solution.py:392
  151.9 3.3 %collective-permute-done.13.third = f32[32,256]{1,0:T(8,128)S(1)} collective-permute-done((f32[32,256]{1,0:T(8,128)S(1)}, f32[32,256]{1,0:T(8,128)S(1)}, u32[]{:S(2)}, u32[]{:S(2)}) %collective-permute-start.13) | collective-permute-done | bytes 32800 | tf_op jit(solution)/shard_map/ppermute | solution.py:388
  155.4 2.8 %all-to-all-done.4 = f32[16,32,256]{2,1,0:T(8,128)S(1)} async-done(((f32[16,32,256]{2,1,0:T(8,128)}), f32[16,32,256]{2,1,0:T(8,128)S(1)}, u32[]{:S(2)}, u32[]{:S(2)}) %all-to-all-start.4) | async-done | bytes 524320 | tf_op jit(solution)/shard_map/all_to_all | solution.py:392
  159.0 28.0 %all_to_all.31 = f32[64,32,256]{2,1,0:T(8,128)S(1)} all-to-all(f32[64,32,256]{2,1,0:T(8,128)S(1)} %bitcast.5), channel_id=1, replica_groups=mesh['layer'=8,'grid'=16] {'grid'}, dimensions={0} | all-to-all | bytes 4194304 | tf_op jit(solution)/shard_map/all_to_all | solution.py:392
  188.3 4.8 %collective-permute-start.15 = (f32[16,4,32,256]{3,2,1,0:T(8,128)S(1)}, f32[16,4,32,256]{3,2,1,0:T(8,128)S(1)}, u32[]{:S(2)}, u32[]{:S(2)}) collective-permute-start(f32[16,4,32,256]{3,2,1,0:T(8,128)S(1)} %bitcast.6), channel_id=1, source_target_pairs={{0,16},{16,0},{32,48},{48,32},{64,80},{80,64},{96,112},{112,96},{1... | collective-permute-start | bytes 6291464 | tf_op jit(solution)/shard_map/ppermute | solution.py:384
  193.2 3.8 %collective-permute-done.15.even_other = f32[16,4,32,256]{3,2,1,0:T(8,128)S(1)} collective-permute-done((f32[16,4,32,256]{3,2,1,0:T(8,128)S(1)}, f32[16,4,32,256]{3,2,1,0:T(8,128)S(1)}, u32[]{:S(2)}, u32[]{:S(2)}) %collective-permute-start.15) | collective-permute-done | bytes 2097184 | tf_op jit(solution)/shard_map/ppermute | solution.py:384
  198.4 7.2 %leaf_back.1 = (f32[8,256,256]{2,1,0:T(8,128)}, f32[2,256,256]{2,1,0:T(8,128)}) custom-call(s32[8,2]{1,0:T(8,128)} %copy.16.targets, f32[8,256,256]{2,1,0:T(8,128)} %copy-done.13, f32[8,2,256,256]{3,2,1,0:T(8,128)} %copy-done.6, f32[16,4,32,256]{3,2,1,0:T(8,128)} %bitcast.7, f32[16,4,32,256]{3,2,1,0:T(8,128)} %copy-done.19, f32[4,2,16,32,256]{4,3,2,1,0:T(8,128)} %bitcast.8), custom_call_target="tpu_custom_call" | custom-call | tf_op jit(solution)/shard_map/leaf_back/pallas_call | solution.py:343
  (89 shorter events, 39.8 us)
Async XLA Ops:
  7.2 89.2 %all-gather.4.cloned.1.call-start = ((), (), s32[]{:S(2)}) async-start(), calls=%async_computation.6 | async-start | bytes 4456448 | tf_op jit(solution)/shard_map/all_gather | solution.py:418
  21.7 5.5 %collective-permute-start.7 = (f32[64,32,256]{2,1,0:T(8,128)}, f32[64,32,256]{2,1,0:T(8,128)S(1)}, u32[]{:S(2)}, u32[]{:S(2)}) collective-permute-start(f32[64,32,256]{2,1,0:T(8,128)} %get-tuple-element.59), channel_id=1, source_target_pairs={{0,16},{16,0},{32,48},{48,32},{64,80},{80,64},{96,112},{112,96},{1... | collective-permute-start | bytes 6291464 | tf_op jit(solution)/shard_map/ppermute | solution.py:384
  30.7 46.2 %all-to-all-start = ((f32[64,32,256]{2,1,0:T(8,128)}), f32[64,32,256]{2,1,0:T(8,128)S(1)}, u32[]{:S(2)}, u32[]{:S(2)}) async-start(f32[64,32,256]{2,1,0:T(8,128)} %joined.1), calls=%async_computation | async-start | bytes 4194304 | tf_op jit(solution)/shard_map/all_to_all | solution.py:392
  37.7 2.4 %collective-permute-start.1 = (f32[16,32,256]{2,1,0:T(8,128)}, f32[16,32,256]{2,1,0:T(8,128)S(1)}, u32[]{:S(2)}, u32[]{:S(2)}) collective-permute-start(f32[16,32,256]{2,1,0:T(8,128)} %get-tuple-element.53), channel_id=1, source_target_pairs={{0,16},{16,0},{32,48},{48,32},{64,80},{80,64},{96,112},{112,96},{1... | collective-permute-start | bytes 1572872 | tf_op jit(solution)/shard_map/ppermute | solution.py:384
  38.4 4.8 %collective-permute-start.3 = (f32[16,32,256]{2,1,0:T(8,128)}, f32[16,32,256]{2,1,0:T(8,128)S(1)}, u32[]{:S(2)}, u32[]{:S(2)}) collective-permute-start(f32[16,32,256]{2,1,0:T(8,128)} %get-tuple-element.55), channel_id=1, source_target_pairs={{0,16},{16,0},{32,48},{48,32},{64,80},{80,64},{96,112},{112,96},{1... | collective-permute-start | bytes 1572872 | tf_op jit(solution)/shard_map/ppermute | solution.py:384
  38.5 8.1 %collective-permute-start.5 = (f32[16,32,256]{2,1,0:T(8,128)}, f32[16,32,256]{2,1,0:T(8,128)S(1)}, u32[]{:S(2)}, u32[]{:S(2)}) collective-permute-start(f32[16,32,256]{2,1,0:T(8,128)} %get-tuple-element.57), channel_id=1, source_target_pairs={{0,16},{16,0},{32,48},{48,32},{64,80},{80,64},{96,112},{112,96},{1... | collective-permute-start | bytes 1572872 | tf_op jit(solution)/shard_map/ppermute | solution.py:384
  38.9 8.6 %collective-permute-start = (f32[16,32,256]{2,1,0:T(8,128)}, f32[16,32,256]{2,1,0:T(8,128)S(1)}, u32[]{:S(2)}, u32[]{:S(2)}) collective-permute-start(f32[16,32,256]{2,1,0:T(8,128)} %get-tuple-element.51), channel_id=1, source_target_pairs={{0,16},{16,0},{32,48},{48,32},{64,80},{80,64},{96,112},{112,96},{1... | collective-permute-start | bytes 1572872 | tf_op jit(solution)/shard_map/ppermute | solution.py:384
  40.1 30.1 %copy-start.14 = (f32[8,256,256]{2,1,0:T(8,128)S(1)}, f32[8,256,256]{2,1,0:T(8,128)}, u32[]{:S(2)}) copy-start(f32[8,256,256]{2,1,0:T(8,128)} %get-tuple-element.61.fwd) | copy-start | bytes 6291460
  41.4 16.0 %collective-permute-start.2 = (f32[16,32,256]{2,1,0:T(8,128)S(1)}, f32[16,32,256]{2,1,0:T(8,128)S(1)}, u32[]{:S(2)}, u32[]{:S(2)}) collective-permute-start(f32[16,32,256]{2,1,0:T(8,128)S(1)} %add.13), channel_id=1, source_target_pairs={{0,32},{16,48},{32,64},{48,80},{64,96},{80,112},{96,0},{112,16},{1... | collective-permute-start | bytes 1572872 | tf_op jit(solution)/shard_map/ppermute | solution.py:388
  43.1 27.1 %copy-start.12 = (f32[8,256,256]{2,1,0:T(8,128)S(1)}, f32[8,256,256]{2,1,0:T(8,128)}, u32[]{:S(2)}) copy-start(f32[8,256,256]{2,1,0:T(8,128)} %uinv.3) | copy-start | bytes 6291460
  43.2 26.1 %collective-permute-start.4 = (f32[16,32,256]{2,1,0:T(8,128)S(1)}, f32[16,32,256]{2,1,0:T(8,128)S(1)}, u32[]{:S(2)}, u32[]{:S(2)}) collective-permute-start(f32[16,32,256]{2,1,0:T(8,128)S(1)} %add.14), channel_id=1, source_target_pairs={{0,64},{16,80},{32,96},{48,112},{64,0},{80,16},{96,32},{112,48},{1... | collective-permute-start | bytes 1572872 | tf_op jit(solution)/shard_map/ppermute | solution.py:388
  46.7 22.7 %collective-permute-start.6 = (f32[16,32,256]{2,1,0:T(8,128)S(1)}, f32[16,32,256]{2,1,0:T(8,128)S(1)}, u32[]{:S(2)}, u32[]{:S(2)}) collective-permute-start(f32[16,32,256]{2,1,0:T(8,128)S(1)} %add.15), channel_id=1, source_target_pairs={{0,96},{16,112},{32,0},{48,16},{64,32},{80,48},{96,64},{112,80},{1... | collective-permute-start | bytes 1572872 | tf_op jit(solution)/shard_map/ppermute | solution.py:388
  76.8 16.2 %all-to-all-start.1 = ((f32[16,32,256]{2,1,0:T(8,128)}), f32[16,32,256]{2,1,0:T(8,128)}, u32[]{:S(2)}, u32[]{:S(2)}) async-start(f32[16,32,256]{2,1,0:T(8,128)} %copy-done.11), calls=%async_computation.1 | async-start | bytes 1048576 | tf_op jit(solution)/shard_map/all_to_all | solution.py:392
  84.0 4.9 %collective-permute-start.8 = (f32[32,256]{1,0:T(8,128)S(1)}, f32[32,256]{1,0:T(8,128)S(1)}, u32[]{:S(2)}, u32[]{:S(2)}) collective-permute-start(f32[32,256]{1,0:T(8,128)S(1)} %get-tuple-element.71), channel_id=1, source_target_pairs={{0,32},{16,48},{32,64},{48,80},{64,96},{80,112},{96,0},{112,16},{1... | collective-permute-start | bytes 98312 | tf_op jit(solution)/shard_map/ppermute | solution.py:388
  85.8 4.3 %collective-permute-start.9 = (f32[32,256]{1,0:T(8,128)S(1)}, f32[32,256]{1,0:T(8,128)S(1)}, u32[]{:S(2)}, u32[]{:S(2)}) collective-permute-start(f32[32,256]{1,0:T(8,128)S(1)} %get-tuple-element.72), channel_id=1, source_target_pairs={{0,64},{16,80},{32,96},{48,112},{64,0},{80,16},{96,32},{112,48},{1... | collective-permute-start | bytes 98312 | tf_op jit(solution)/shard_map/ppermute | solution.py:388
  88.3 3.2 %collective-permute-start.10 = (f32[32,256]{1,0:T(8,128)S(1)}, f32[32,256]{1,0:T(8,128)S(1)}, u32[]{:S(2)}, u32[]{:S(2)}) collective-permute-start(f32[32,256]{1,0:T(8,128)S(1)} %get-tuple-element.73), channel_id=1, source_target_pairs={{0,96},{16,112},{32,0},{48,16},{64,32},{80,48},{96,64},{112,80},{1... | collective-permute-start | bytes 98312 | tf_op jit(solution)/shard_map/ppermute | solution.py:388
  96.4 10.9 %collective-permute-start.11 = (f32[32,128,256]{2,1,0:T(8,128)}, f32[32,128,256]{2,1,0:T(8,128)}, u32[]{:S(2)}, u32[]{:S(2)}) collective-permute-start(f32[32,128,256]{2,1,0:T(8,128)} %all-gather.4.cloned.1.call-done.own), channel_id=1, source_target_pairs={{0,16},{16,0},{32,48},{48,32},{64,80},{80,64},{96,112},{112,96},{1... | collective-permute-start | bytes 12582920 | tf_op jit(solution)/shard_map/ppermute | solution.py:384
  100.2 17.0 %all-to-all-start.2 = ((f32[16,32,256]{2,1,0:T(8,128)}), f32[16,32,256]{2,1,0:T(8,128)S(1)}, u32[]{:S(2)}, u32[]{:S(2)}) async-start(f32[16,32,256]{2,1,0:T(8,128)} %get-tuple-element.79), calls=%async_computation.2 | async-start | bytes 1048576 | tf_op jit(solution)/shard_map/all_to_all | solution.py:392
  145.2 13.0 %all-to-all-start.4 = ((f32[16,32,256]{2,1,0:T(8,128)}), f32[16,32,256]{2,1,0:T(8,128)S(1)}, u32[]{:S(2)}, u32[]{:S(2)}) async-start(f32[16,32,256]{2,1,0:T(8,128)} %get-tuple-element.91), calls=%async_computation.4 | async-start | bytes 1048576 | tf_op jit(solution)/shard_map/all_to_all | solution.py:392
  149.0 48.0 %all-gather.6.cloned.1.call-start = ((), (), s32[]{:S(2)}) async-start(), calls=%async_computation.7 | async-start | bytes 4718592 | tf_op jit(solution)/shard_map/all_gather | solution.py:463
  149.0 2.9 %collective-permute-start.14 = (f32[32,256]{1,0:T(8,128)S(1)}, f32[32,256]{1,0:T(8,128)S(1)}, u32[]{:S(2)}, u32[]{:S(2)}) collective-permute-start(f32[32,256]{1,0:T(8,128)S(1)} %get-tuple-element.90.first), channel_id=1, source_target_pairs={{0,96},{16,112},{32,0},{48,16},{64,32},{80,48},{96,64},{112,80},{1... | collective-permute-start | bytes 98312 | tf_op jit(solution)/shard_map/ppermute | solution.py:388
  150.9 4.3 %collective-permute-start.13 = (f32[32,256]{1,0:T(8,128)S(1)}, f32[32,256]{1,0:T(8,128)S(1)}, u32[]{:S(2)}, u32[]{:S(2)}) collective-permute-start(f32[32,256]{1,0:T(8,128)S(1)} %get-tuple-element.90.first), channel_id=1, source_target_pairs={{0,64},{16,80},{32,96},{48,112},{64,0},{80,16},{96,32},{112,48},{1... | collective-permute-start | bytes 98312 | tf_op jit(solution)/shard_map/ppermute | solution.py:388
  150.9 4.3 %collective-permute-start.12 = (f32[32,256]{1,0:T(8,128)S(1)}, f32[32,256]{1,0:T(8,128)S(1)}, u32[]{:S(2)}, u32[]{:S(2)}) collective-permute-start(f32[32,256]{1,0:T(8,128)S(1)} %get-tuple-element.90.first), channel_id=1, source_target_pairs={{0,32},{16,48},{32,64},{48,80},{64,96},{80,112},{96,0},{112,16},{1... | collective-permute-start | bytes 98312 | tf_op jit(solution)/shard_map/ppermute | solution.py:388
  188.3 8.6 %collective-permute-start.15 = (f32[16,4,32,256]{3,2,1,0:T(8,128)S(1)}, f32[16,4,32,256]{3,2,1,0:T(8,128)S(1)}, u32[]{:S(2)}, u32[]{:S(2)}) collective-permute-start(f32[16,4,32,256]{3,2,1,0:T(8,128)S(1)} %bitcast.6), channel_id=1, source_target_pairs={{0,16},{16,0},{32,48},{48,32},{64,80},{80,64},{96,112},{112,96},{1... | collective-permute-start | bytes 6291464 | tf_op jit(solution)/shard_map/ppermute | solution.py:384
  (22 other events, 149.8 us)
Sparse Core Ops, SparseCore 0:
  11.1 72.1 all-gather.3
  159.2 33.0 all-gather.5
